TPU v7x, 768 devices: a whole 4x8x12 slice. The times are simulated.
768 devices in a mesh: gx: 8 (over y_lo, x), gy: 12 (over z), gz: 8 (over y_hi, core).
Axes of the slice: x: 4, y: 8 (y_hi: 4, y_lo: 2; y = y_hi * 2 + y_lo), z: 12, core: 2. Of those that a mesh axis runs over, the one named last changes fastest.
Arguments:
- adjoint_start: float32 [6, 64, 256, 1536], P(None, 'gz', 'gx', 'gy'), may hold values from -6 to 6
- eddy_visc: float32 [64, 256, 1536], P('gz', 'gx', 'gy'), may hold values from 0.4 to 1.2
- diag_coef: float32 [64, 256, 1536], P('gz', 'gx', 'gy'), may hold values from 6 to 8
- coupling: float32 [6, 6], replicated, may hold values from -5 to 5
- metric_terms: float32 [3, 6, 64, 256, 1536], P(None, None, 'gz', 'gx', 'gy'), may hold values from -0.3125 to 0.3125
- sample_cells: int32 [2048], replicated, may hold values from 0 to 393215
- sample_weights: float32 [2048], replicated, may hold values from -6 to 6
- face_codes: int32 [6], replicated, may hold values from 0 to 2
Outputs:
- adjoint_field: float32 [6, 64, 256, 1536], P(None, 'gz', 'gx', 'gy')
- height_grad: float32 [256, 1536], P('gx', ('gy', 'gz'))
Inputs may be any that keep to these rules, and one draw needn't show every extreme that they name: `sample_cells`: each entry is x * 1536 + y for a sample column (x, y); a column may be sampled more than once. `face_codes`: faces in the order streamwise low, streamwise high, spanwise low, spanwise high, bottom, top; 0 fixed zero, 1 zero gradient, 2 mirrored with opposite sign.
All inputs are finite; a program needn't handle non-finite values.
Results may differ from a plain program's by a relative error of at most 0.00011.
Values sent between devices are 32-bit elements; how exact they have to be, the bound alone decides.
No kernel may reach another device: no remote copies, remote signals or barrier semaphores. Data moves between devices by JAX's collectives and lax.ppermute only.
A program may use at most 64 MiB of HBM per device.

v0:
```python
import jax
import jax.numpy as jnp
from jax import lax
from jax.sharding import PartitionSpec as P

relax_rate = 0.9


def padded_2(x, sides, width):
    for axis, dim in sides:
        devices, length = (lax.axis_size(axis), x.shape[dim])
        up = [(i, (i + 1) % devices) for i in range(devices - 1)]
        down = [(j, i) for i, j in up]
        last = lax.slice_in_dim(x, length - width, length, axis=dim)
        leading = lax.slice_in_dim(x, 0, width, axis=dim)
        before = lax.ppermute(last, axis, up)
        after = lax.ppermute(leading, axis, down)
        x = jnp.concatenate([before, x, after], axis=dim)
    return x


def face_factors(face_codes):
    return jnp.where(face_codes == 1, 1.0, jnp.where(face_codes == 2, -1.0, 0.0)).astype(
        jnp.float32
    )


def fix_axis(padded, along, width, at_low, at_high, low_factor, high_factor):
    length = padded.shape[along]
    low_edge = lax.slice_in_dim(padded, width, width + 1, axis=along)
    low_ghost = lax.slice_in_dim(padded, width - 1, width, axis=along)
    high_edge = lax.slice_in_dim(padded, length - width - 1, length - width, axis=along)
    high_ghost = lax.slice_in_dim(padded, length - width, length - width + 1, axis=along)
    padded = lax.dynamic_update_slice_in_dim(
        padded, jnp.where(at_low, low_factor * low_edge, low_ghost), width - 1, along
    )
    padded = lax.dynamic_update_slice_in_dim(
        padded, jnp.where(at_high, high_factor * high_edge, high_ghost), length - width, along
    )
    return padded


def fix_faces(padded, width, factors, places):
    (index_x, count_x), (index_y, count_y), (index_z, count_z) = places
    padded = fix_axis(
        padded, 2, width, index_x == 0, index_x == count_x - 1, factors[0], factors[1]
    )
    padded = fix_axis(
        padded, 3, width, index_y == 0, index_y == count_y - 1, factors[2], factors[3]
    )
    padded = fix_axis(
        padded, 1, width, index_z == 0, index_z == count_z - 1, factors[4], factors[5]
    )
    return padded


def neighbor_sum(padded):
    total = padded[:, 2:, 1:-1, 1:-1] + padded[:, :-2, 1:-1, 1:-1]
    total = total + padded[:, 1:-1, 2:, 1:-1] + padded[:, 1:-1, :-2, 1:-1]
    total = total + padded[:, 1:-1, 1:-1, 2:] + padded[:, 1:-1, 1:-1, :-2]
    return total


def relax(adjoint, diag, source, beside, coupling):
    coupled = jnp.einsum("ef,ezxy->fzxy", coupling, adjoint, precision=lax.Precision.HIGHEST)
    remainder = source - (diag[None] * adjoint + coupled - beside)
    return adjoint + relax_rate * remainder / diag[None]


def sample_source(cells, weights, starts, extents, total_y, hub_level, fields):
    start_z, start_x, start_y = starts
    ext_z, ext_x, ext_y = extents
    col_x = cells // total_y - start_x
    col_y = cells % total_y - start_y
    lev_z = hub_level - start_z
    inside = (
        (col_x >= 0)
        & (col_x < ext_x)
        & (col_y >= 0)
        & (col_y < ext_y)
        & (lev_z >= 0)
        & (lev_z < ext_z)
    )
    flat_index = jnp.where(inside, (lev_z * ext_x + col_x) * ext_y + col_y, ext_z * ext_x * ext_y)
    flat_cells = (
        jnp.zeros((ext_z * ext_x * ext_y,), jnp.float32).at[flat_index].add(weights, mode="drop")
    )
    leading = flat_cells.reshape(1, ext_z, ext_x, ext_y)
    return jnp.concatenate([leading, jnp.zeros((fields - 1, ext_z, ext_x, ext_y), jnp.float32)], 0)


def local(
    adjoint_start,
    eddy_visc,
    diag_coef,
    coupling,
    metric_terms,
    sample_cells,
    sample_weights,
    face_codes,
):
    fields, cells_z, cells_x, cells_y = adjoint_start.shape
    index_x = lax.axis_index("gx")
    index_y = lax.axis_index("gy")
    index_z = lax.axis_index("gz")
    count_x = lax.axis_size("gx")
    count_y = lax.axis_size("gy")
    count_z = lax.axis_size("gz")
    places = ((index_x, count_x), (index_y, count_y), (index_z, count_z))
    total_y = cells_y * count_y
    total_z = cells_z * count_z
    hub_level = total_z // 4
    start_x = index_x * cells_x
    start_y = index_y * cells_y
    start_z = index_z * cells_z
    factors = face_factors(face_codes)
    source = sample_source(
        sample_cells,
        sample_weights,
        (start_z, start_x, start_y),
        (cells_z, cells_x, cells_y),
        total_y,
        hub_level,
        fields,
    )
    adjoint = adjoint_start
    for sweep_no in range(2):
        fluxes = eddy_visc[None] * adjoint
        padded = padded_2(fluxes, (("gx", 2), ("gy", 3), ("gz", 1)), 1)
        padded = fix_faces(padded, 1, factors, places)
        adjoint = relax(adjoint, diag_coef, source, neighbor_sum(padded), coupling)
    level_frac = (
        (start_z + jnp.arange(cells_z, dtype=jnp.int32)).astype(jnp.float32) + 0.5
    ) / total_z
    level_weights = 1.0 - 0.5 * level_frac
    sums_list = []
    for term_no in range(3):
        column_terms = jnp.sum(metric_terms[term_no] * adjoint, axis=0)
        sums_list.append(
            jnp.tensordot(level_weights, column_terms, axes=1, precision=lax.Precision.HIGHEST)
        )
    partial_sums = jnp.stack(sums_list, 0)
    share = cells_y // count_z
    totals = lax.psum(partial_sums, "gz")
    span_pad = padded_2(totals[2], (("gy", 1),), 1)
    base_full = totals[0] - 0.5 * (span_pad[:, 2:] - span_pad[:, :-2])
    base_sum = lax.dynamic_slice_in_dim(base_full, index_z * share, share, 1)
    stream_sum = lax.dynamic_slice_in_dim(totals[1], index_z * share, share, 1)
    stream_pad = padded_2(stream_sum, (("gx", 0),), 1)
    height_grad = base_sum - 0.5 * (stream_pad[2:] - stream_pad[:-2])
    return (adjoint, height_grad)


def solution(mesh):
    return jax.shard_map(
        local,
        mesh=mesh,
        in_specs=(
            P(None, "gz", "gx", "gy"),
            P("gz", "gx", "gy"),
            P("gz", "gx", "gy"),
            P(),
            P(None, None, "gz", "gx", "gy"),
            P(),
            P(),
            P(),
        ),
        out_specs=(P(None, "gz", "gx", "gy"), P("gx", ("gy", "gz"))),
        check_vma=False,
    )
```

profile of v0, /device:TPU:230, one launch (start us, length us, event | category | flops | bytes accessed | tf_op | source)
XLA Modules:
  0.0 231.2 jit_solution(2735290502110445571)
XLA Ops:
  4.8 3.3 %collective-permute-start.1 = (f32[6,8,1,128]{3,0,2,1:T(8,128)S(1)}, f32[6,8,1,128]{3,0,2,1:T(8,128)S(1)}, u32[]{:S(2)}, u32[]{:S(2)}) collective-permute-start(f32[6,8,1,128]{3,0,2,1:T(8,128)S(1)} %get-tuple-element.37), channel_id=1, source_target_pairs={{96,0},{192,96},{288,192},{384,288},{480,384},{576,480},{672,576},... | collective-permute-start | bytes 73736 | tf_op jit(solution)/shard_map/ppermute | solution.py:17
  8.9 3.8 %collective-permute-done.1 = f32[6,8,1,128]{3,0,2,1:T(8,128)S(1)} collective-permute-done((f32[6,8,1,128]{3,0,2,1:T(8,128)S(1)}, f32[6,8,1,128]{3,0,2,1:T(8,128)S(1)}, u32[]{:S(2)}, u32[]{:S(2)}) %collective-permute-start.1) | collective-permute-done | bytes 24608 | tf_op jit(solution)/shard_map/ppermute | solution.py:17
  13.7 5.5 %collective-permute-start.2 = (f32[6,8,34,1]{2,1,3,0:T(8,128)S(1)}, f32[6,8,34,1]{2,1,3,0:T(8,128)S(1)}, u32[]{:S(2)}, u32[]{:S(2)}) collective-permute-start(f32[6,8,34,1]{2,1,3,0:T(8,128)S(1)} %copy.107), channel_id=1, source_target_pairs={{0,8},{8,16},{16,24},{24,32},{32,40},{40,48},{48,56},{56,64},{64,7... | collective-permute-start | bytes 19592 | tf_op jit(solution)/shard_map/ppermute | solution.py:16
  21.7 11.5 %scatter_custom_fusion = f32[32768]{0:T(1024)S(1)} fusion(s32[2048]{0:T(1024)S(1)} %compare_select_fusion, f32[2048]{0:T(1024)} %param.14, f32[]{:T(128)} %constant.25.clone.1), kind=kCustom, calls=%fused_computation.95 | custom fusion | flops 2048 | bytes 131584 | tf_op jit(solution)/shard_map/scatter-add | solution.py:86
  36.5 5.9 %collective-permute-start.5 = (f32[6,1,34,130]{3,0,2,1:T(8,128)S(1)}, f32[6,1,34,130]{3,0,2,1:T(8,128)S(1)}, u32[]{:S(2)}, u32[]{:S(2)}) collective-permute-start(f32[6,1,34,130]{3,0,2,1:T(8,128)S(1)} %get-tuple-element.22), channel_id=1, source_target_pairs={{1,0},{2,1},{3,2},{4,3},{5,4},{6,5},{7,6},{9,8},{10,9},{11,10},{12... | collective-permute-start | bytes 318248 | tf_op jit(solution)/shard_map/ppermute | solution.py:17
  44.6 2.7 %collective-permute-done.5 = f32[6,1,34,130]{3,0,2,1:T(8,128)S(1)} collective-permute-done((f32[6,1,34,130]{3,0,2,1:T(8,128)S(1)}, f32[6,1,34,130]{3,0,2,1:T(8,128)S(1)}, u32[]{:S(2)}, u32[]{:S(2)}) %collective-permute-start.5) | collective-permute-done | bytes 106112 | tf_op jit(solution)/shard_map/ppermute | solution.py:17
  49.6 3.5 %slice_select_fusion.2 = (f32[6,10,34,1]{3,0,2,1:T(8,128)}, f32[6,10,34,1]{3,0,2,1:T(8,128)}) fusion(f32[6,10,34,130]{3,0,2,1:T(8,128)S(1)} %fusion.28, f32[]{:T(128)} %bitcast.5, pred[]{:T(512)S(6)} %eq.37, f32[]{:T(128)} %bitcast.4, pred[]{:T(512)S(6)} %eq.36), kind=kLoop, calls=%fused_computation.9 | loop fusion | flops 8160 | bytes 48970 | tf_op jit(solution)/shard_map/jit(_where)/select_n | solution.py:38
  53.1 5.3 %dynamic_update_slice.38 = f32[6,10,34,130]{3,0,2,1:T(8,128)S(1)} dynamic-update-slice(f32[6,10,34,130]{3,0,2,1:T(8,128)S(1)} %fusion.28, f32[6,10,34,1]{3,0,2,1:T(8,128)} %get-tuple-element.26, s32[]{:T(128)} %constant.28.clone.1, s32[]{:T(128)} %constant.28.clone.1, s32[]{:T(128)} %constant.28.clone.1, s32[]{:T(128)} %constant.28.clone.1) | dynamic-update-slice | bytes 16324 | tf_op jit(solution)/shard_map/dynamic_update_slice | solution.py:34
  58.4 28.4 %dynamic_update_slice.39 = f32[6,10,34,130]{3,0,2,1:T(8,128)S(1)} dynamic-update-slice(f32[6,10,34,130]{3,0,2,1:T(8,128)S(1)} %dynamic_update_slice.38, f32[6,10,34,1]{3,0,2,1:T(8,128)} %get-tuple-element.25, s32[]{:T(128)} %constant.28.clone.1, s32[]{:T(128)} %constant.28.clone.1, s32[]{:T(128)} %constant.28.clone.1, s32[]{:T(128)} %constant.23.clone.1) | dynamic-update-slice | bytes 16324 | tf_op jit(solution)/shard_map/dynamic_update_slice | solution.py:37
  88.6 4.1 %broadcast_multiply_fusion = (f32[6,8,32,128]{3,0,2,1:T(8,128)S(1)}, f32[6,8,32,128]{3,0,2,1:T(8,128)}) fusion(f32[8,32,128]{2,1,0:T(8,128)S(1)} %copy-done.6, f32[6,10,34,130]{3,0,2,1:T(8,128)S(1)} %fusion.18, f32[6,8,32,128]{3,2,1,0:T(8,128)S(1)} %copy-done.5, f32[6,6]{1,0:T(8,128)S(1)} %copy-done, f32[8,32,128]{2,1,0:T(8,128)S(1)} %copy-done.7, ...), kind=kOutput, calls=%fused_computation.48 | convolution fusion | flops 16711680 | bytes 9834496 | tf_op jit(solution)/shard_map/ef,ezxy->fzxy/dot_general | solution.py:65
  92.7 3.2 %collective-permute-start.6 = (f32[6,8,1,128]{3,0,2,1:T(8,128)S(1)}, f32[6,8,1,128]{3,0,2,1:T(8,128)S(1)}, u32[]{:S(2)}, u32[]{:S(2)}) collective-permute-start(f32[6,8,1,128]{3,0,2,1:T(8,128)S(1)} %get-tuple-element.34), channel_id=1, source_target_pairs={{0,96},{96,192},{192,288},{288,384},{384,480},{480,576},{576,672},... | collective-permute-start | bytes 73736 | tf_op jit(solution)/shard_map/ppermute | solution.py:16
  95.9 2.7 %collective-permute-start.7 = (f32[6,8,1,128]{3,0,2,1:T(8,128)S(1)}, f32[6,8,1,128]{3,0,2,1:T(8,128)S(1)}, u32[]{:S(2)}, u32[]{:S(2)}) collective-permute-start(f32[6,8,1,128]{3,0,2,1:T(8,128)S(1)} %get-tuple-element.35), channel_id=1, source_target_pairs={{96,0},{192,96},{288,192},{384,288},{480,384},{576,480},{672,576},... | collective-permute-start | bytes 73736 | tf_op jit(solution)/shard_map/ppermute | solution.py:17
  98.6 5.2 %collective-permute-done.7 = f32[6,8,1,128]{3,0,2,1:T(8,128)S(1)} collective-permute-done((f32[6,8,1,128]{3,0,2,1:T(8,128)S(1)}, f32[6,8,1,128]{3,0,2,1:T(8,128)S(1)}, u32[]{:S(2)}, u32[]{:S(2)}) %collective-permute-start.7) | collective-permute-done | bytes 24608 | tf_op jit(solution)/shard_map/ppermute | solution.py:17
  104.8 5.1 %collective-permute-start.8 = (f32[6,8,34,1]{2,1,3,0:T(8,128)S(1)}, f32[6,8,34,1]{2,1,3,0:T(8,128)S(1)}, u32[]{:S(2)}, u32[]{:S(2)}) collective-permute-start(f32[6,8,34,1]{2,1,3,0:T(8,128)S(1)} %copy.113), channel_id=1, source_target_pairs={{0,8},{8,16},{16,24},{24,32},{32,40},{40,48},{48,56},{56,64},{64,7... | collective-permute-start | bytes 19592 | tf_op jit(solution)/shard_map/ppermute | solution.py:16
  112.9 4.4 %collective-permute-done.9 = f32[6,8,34,1]{2,1,3,0:T(8,128)S(1)} collective-permute-done((f32[6,8,34,1]{2,1,3,0:T(8,128)S(1)}, f32[6,8,34,1]{2,1,3,0:T(8,128)S(1)}, u32[]{:S(2)}, u32[]{:S(2)}) %collective-permute-start.9) | collective-permute-done | bytes 6560 | tf_op jit(solution)/shard_map/ppermute | solution.py:17
  120.9 6.0 %collective-permute-start.11 = (f32[6,1,34,130]{3,0,2,1:T(8,128)}, f32[6,1,34,130]{3,0,2,1:T(8,128)}, u32[]{:S(2)}, u32[]{:S(2)}) collective-permute-start(f32[6,1,34,130]{3,0,2,1:T(8,128)} %get-tuple-element.20), channel_id=1, source_target_pairs={{1,0},{2,1},{3,2},{4,3},{5,4},{6,5},{7,6},{9,8},{10,9},{11,10},{12... | collective-permute-start | bytes 318248 | tf_op jit(solution)/shard_map/ppermute | solution.py:17
  129.3 3.4 %collective-permute-done.11 = f32[6,1,34,130]{3,0,2,1:T(8,128)} collective-permute-done((f32[6,1,34,130]{3,0,2,1:T(8,128)}, f32[6,1,34,130]{3,0,2,1:T(8,128)}, u32[]{:S(2)}, u32[]{:S(2)}) %collective-permute-start.11) | collective-permute-done | bytes 106112 | tf_op jit(solution)/shard_map/ppermute | solution.py:17
  136.1 3.5 %slice_select_fusion = (f32[6,10,34,1]{3,0,2,1:T(8,128)}, f32[6,10,34,1]{3,0,2,1:T(8,128)}) fusion(f32[6,10,34,130]{3,0,2,1:T(8,128)S(1)} %fusion.26, f32[]{:T(128)} %bitcast.5, pred[]{:T(512)S(6)} %eq.37, f32[]{:T(128)} %bitcast.4, pred[]{:T(512)S(6)} %eq.36), kind=kLoop, calls=%fused_computation.5 | loop fusion | flops 8160 | bytes 48970 | tf_op jit(solution)/shard_map/jit(_where)/select_n | solution.py:38
  139.6 5.3 %dynamic_update_slice.44 = f32[6,10,34,130]{3,0,2,1:T(8,128)S(1)} dynamic-update-slice(f32[6,10,34,130]{3,0,2,1:T(8,128)S(1)} %fusion.26, f32[6,10,34,1]{3,0,2,1:T(8,128)} %get-tuple-element.24, s32[]{:T(128)} %constant.28.clone.1, s32[]{:T(128)} %constant.28.clone.1, s32[]{:T(128)} %constant.28.clone.1, s32[]{:T(128)} %constant.28.clone.1) | dynamic-update-slice | bytes 16324 | tf_op jit(solution)/shard_map/dynamic_update_slice | solution.py:34
  144.8 28.4 %dynamic_update_slice.45 = f32[6,10,34,130]{3,0,2,1:T(8,128)S(1)} dynamic-update-slice(f32[6,10,34,130]{3,0,2,1:T(8,128)S(1)} %dynamic_update_slice.44, f32[6,10,34,1]{3,0,2,1:T(8,128)} %get-tuple-element.23, s32[]{:T(128)} %constant.28.clone.1, s32[]{:T(128)} %constant.28.clone.1, s32[]{:T(128)} %constant.28.clone.1, s32[]{:T(128)} %constant.23.clone.1) | dynamic-update-slice | bytes 16324 | tf_op jit(solution)/shard_map/dynamic_update_slice | solution.py:37
  175.2 4.3 %fusion.15 = (f32[8,32,128]{2,1,0:T(8,128)S(1)}, f32[8,32,128]{2,1,0:T(8,128)S(1)}, f32[8,32,128]{2,1,0:T(8,128)S(1)}, f32[6,8,32,128]{3,0,2,1:T(8,128)S(1)}) fusion(f32[1,6,8,32,128]{4,3,2,1,0:T(8,128)S(1)} %copy-done.3, f32[1,6,8,32,128]{4,3,2,1,0:T(8,128)S(1)} %copy-done.4, f32[1,6,8,32,128]{4,3,2,1,0:T(8,128)S(1)} %copy-done.2, ...), kind=kOutput, calls=%fused_computation.47 | convolution fusion | flops 17596416 | bytes 12193792 | tf_op jit(solution)/shard_map/ef,ezxy->fzxy/dot_general | solution.py:65
  180.6 33.4 %psum.7 = f32[3,32,128]{1,2,0:T(8,128)S(1)} all-reduce(f32[3,32,128]{1,2,0:T(8,128)S(1)} %copy.120), channel_id=1, replica_groups=mesh['gx'=8,'gy'=12,'gz'=8] {'gz'}, use_global_device_ids=true, to_apply=%region_4.5 | all-reduce | flops 12288 | bytes 98304 | tf_op jit(solution)/shard_map/psum | solution.py:144
  216.2 6.0 %collective-permute-start.15 = (f32[1,16]{1,0:T(1,128)S(1)}, f32[1,16]{1,0:T(1,128)S(1)}, u32[]{:S(2)}, u32[]{:S(2)}) collective-permute-start(f32[1,16]{1,0:T(1,128)S(1)} %bitcast.81), channel_id=1, source_target_pairs={{0,96},{96,192},{192,288},{288,384},{384,480},{480,576},{576,672},... | collective-permute-start | bytes 200 | tf_op jit(solution)/shard_map/ppermute | solution.py:16
  224.1 5.1 %collective-permute-start.13 = (f32[32,1]{0,1:T(1,128)S(1)}, f32[32,1]{0,1:T(1,128)S(1)}, u32[]{:S(2)}, u32[]{:S(2)}) collective-permute-start(f32[32,1]{0,1:T(1,128)S(1)} %get-tuple-element.41), channel_id=1, source_target_pairs={{0,8},{8,16},{16,24},{24,32},{32,40},{40,48},{48,56},{56,64},{64,7... | collective-permute-start | bytes 392 | tf_op jit(solution)/shard_map/ppermute | solution.py:16
  (92 shorter events, 40.1 us)
Async XLA Ops:
  0.6 87.9 %copy-start = (f32[6,6]{1,0:T(8,128)S(1)}, f32[6,6]{1,0:T(8,128)}, u32[]{:S(2)}) copy-start(f32[6,6]{1,0:T(8,128)} %param.11) | copy-start | bytes 436
  2.3 6.6 %collective-permute-start = (f32[6,8,1,128]{3,0,2,1:T(8,128)S(1)}, f32[6,8,1,128]{3,0,2,1:T(8,128)S(1)}, u32[]{:S(2)}, u32[]{:S(2)}) collective-permute-start(f32[6,8,1,128]{3,0,2,1:T(8,128)S(1)} %get-tuple-element.36), channel_id=1, source_target_pairs={{0,96},{96,192},{192,288},{288,384},{384,480},{480,576},{576,672},... | collective-permute-start | bytes 73736 | tf_op jit(solution)/shard_map/ppermute | solution.py:16
  4.8 7.9 %collective-permute-start.1 = (f32[6,8,1,128]{3,0,2,1:T(8,128)S(1)}, f32[6,8,1,128]{3,0,2,1:T(8,128)S(1)}, u32[]{:S(2)}, u32[]{:S(2)}) collective-permute-start(f32[6,8,1,128]{3,0,2,1:T(8,128)S(1)} %get-tuple-element.37), channel_id=1, source_target_pairs={{96,0},{192,96},{288,192},{384,288},{480,384},{576,480},{672,576},... | collective-permute-start | bytes 73736 | tf_op jit(solution)/shard_map/ppermute | solution.py:17
  12.9 8.8 %copy-start.9 = (s32[6]{0:T(128)S(1)}, s32[6]{0:T(128)}, u32[]{:S(2)}) copy-start(s32[6]{0:T(128)} %param.15) | copy-start | bytes 76
  13.7 19.4 %collective-permute-start.2 = (f32[6,8,34,1]{2,1,3,0:T(8,128)S(1)}, f32[6,8,34,1]{2,1,3,0:T(8,128)S(1)}, u32[]{:S(2)}, u32[]{:S(2)}) collective-permute-start(f32[6,8,34,1]{2,1,3,0:T(8,128)S(1)} %copy.107), channel_id=1, source_target_pairs={{0,8},{8,16},{16,24},{24,32},{32,40},{40,48},{48,56},{56,64},{64,7... | collective-permute-start | bytes 19592 | tf_op jit(solution)/shard_map/ppermute | solution.py:16
  19.7 14.0 %collective-permute-start.3 = (f32[6,8,34,1]{2,1,3,0:T(8,128)S(1)}, f32[6,8,34,1]{2,1,3,0:T(8,128)S(1)}, u32[]{:S(2)}, u32[]{:S(2)}) collective-permute-start(f32[6,8,34,1]{2,1,3,0:T(8,128)S(1)} %copy.108), channel_id=1, source_target_pairs={{8,0},{16,8},{24,16},{32,24},{40,32},{48,40},{56,48},{64,56},{72,6... | collective-permute-start | bytes 19592 | tf_op jit(solution)/shard_map/ppermute | solution.py:17
  34.6 10.0 %collective-permute-start.4 = (f32[6,1,34,130]{3,0,2,1:T(8,128)S(1)}, f32[6,1,34,130]{3,0,2,1:T(8,128)S(1)}, u32[]{:S(2)}, u32[]{:S(2)}) collective-permute-start(f32[6,1,34,130]{3,0,2,1:T(8,128)S(1)} %get-tuple-element.21), channel_id=1, source_target_pairs={{0,1},{1,2},{2,3},{3,4},{4,5},{5,6},{6,7},{8,9},{9,10},{10,11},{11... | collective-permute-start | bytes 318248 | tf_op jit(solution)/shard_map/ppermute | solution.py:16
  36.5 10.7 %collective-permute-start.5 = (f32[6,1,34,130]{3,0,2,1:T(8,128)S(1)}, f32[6,1,34,130]{3,0,2,1:T(8,128)S(1)}, u32[]{:S(2)}, u32[]{:S(2)}) collective-permute-start(f32[6,1,34,130]{3,0,2,1:T(8,128)S(1)} %get-tuple-element.22), channel_id=1, source_target_pairs={{1,0},{2,1},{3,2},{4,3},{5,4},{6,5},{7,6},{9,8},{10,9},{11,10},{12... | collective-permute-start | bytes 318248 | tf_op jit(solution)/shard_map/ppermute | solution.py:17
  92.7 5.8 %collective-permute-start.6 = (f32[6,8,1,128]{3,0,2,1:T(8,128)S(1)}, f32[6,8,1,128]{3,0,2,1:T(8,128)S(1)}, u32[]{:S(2)}, u32[]{:S(2)}) collective-permute-start(f32[6,8,1,128]{3,0,2,1:T(8,128)S(1)} %get-tuple-element.34), channel_id=1, source_target_pairs={{0,96},{96,192},{192,288},{288,384},{384,480},{480,576},{576,672},... | collective-permute-start | bytes 73736 | tf_op jit(solution)/shard_map/ppermute | solution.py:16
  95.9 7.9 %collective-permute-start.7 = (f32[6,8,1,128]{3,0,2,1:T(8,128)S(1)}, f32[6,8,1,128]{3,0,2,1:T(8,128)S(1)}, u32[]{:S(2)}, u32[]{:S(2)}) collective-permute-start(f32[6,8,1,128]{3,0,2,1:T(8,128)S(1)} %get-tuple-element.35), channel_id=1, source_target_pairs={{96,0},{192,96},{288,192},{384,288},{480,384},{576,480},{672,576},... | collective-permute-start | bytes 73736 | tf_op jit(solution)/shard_map/ppermute | solution.py:17
  104.8 7.5 %collective-permute-start.8 = (f32[6,8,34,1]{2,1,3,0:T(8,128)S(1)}, f32[6,8,34,1]{2,1,3,0:T(8,128)S(1)}, u32[]{:S(2)}, u32[]{:S(2)}) collective-permute-start(f32[6,8,34,1]{2,1,3,0:T(8,128)S(1)} %copy.113), channel_id=1, source_target_pairs={{0,8},{8,16},{16,24},{24,32},{32,40},{40,48},{48,56},{56,64},{64,7... | collective-permute-start | bytes 19592 | tf_op jit(solution)/shard_map/ppermute | solution.py:16
  110.4 6.9 %collective-permute-start.9 = (f32[6,8,34,1]{2,1,3,0:T(8,128)S(1)}, f32[6,8,34,1]{2,1,3,0:T(8,128)S(1)}, u32[]{:S(2)}, u32[]{:S(2)}) collective-permute-start(f32[6,8,34,1]{2,1,3,0:T(8,128)S(1)} %copy.114), channel_id=1, source_target_pairs={{8,0},{16,8},{24,16},{32,24},{40,32},{48,40},{56,48},{64,56},{72,6... | collective-permute-start | bytes 19592 | tf_op jit(solution)/shard_map/ppermute | solution.py:17
  117.9 9.0 %copy-start.1 = (f32[3,6,8,32,128]{4,3,2,1,0:T(8,128)S(1)}, f32[3,6,8,32,128]{4,3,2,1,0:T(8,128)}, u32[]{:S(2)}) copy-start(f32[3,6,8,32,128]{4,3,2,1,0:T(8,128)} %param.12) | copy-start | bytes 7077892
  119.0 10.3 %collective-permute-start.10 = (f32[6,1,34,130]{3,0,2,1:T(8,128)}, f32[6,1,34,130]{3,0,2,1:T(8,128)}, u32[]{:S(2)}, u32[]{:S(2)}) collective-permute-start(f32[6,1,34,130]{3,0,2,1:T(8,128)} %get-tuple-element.19), channel_id=1, source_target_pairs={{0,1},{1,2},{2,3},{3,4},{4,5},{5,6},{6,7},{8,9},{9,10},{10,11},{11... | collective-permute-start | bytes 318248 | tf_op jit(solution)/shard_map/ppermute | solution.py:16
  120.9 11.7 %collective-permute-start.11 = (f32[6,1,34,130]{3,0,2,1:T(8,128)}, f32[6,1,34,130]{3,0,2,1:T(8,128)}, u32[]{:S(2)}, u32[]{:S(2)}) collective-permute-start(f32[6,1,34,130]{3,0,2,1:T(8,128)} %get-tuple-element.20), channel_id=1, source_target_pairs={{1,0},{2,1},{3,2},{4,3},{5,4},{6,5},{7,6},{9,8},{10,9},{11,10},{12... | collective-permute-start | bytes 318248 | tf_op jit(solution)/shard_map/ppermute | solution.py:17
  173.2 1.9 copy-start.2
  173.2 1.9 copy-start.3
  173.3 1.9 copy-start.4
  173.3 1.9 copy-start.8
  173.3 1.9 copy-start.10
  214.2 16.1 %collective-permute-start.14 = (f32[1,16]{1,0:T(1,128)S(1)}, f32[1,16]{1,0:T(1,128)S(1)}, u32[]{:S(2)}, u32[]{:S(2)}) collective-permute-start(f32[1,16]{1,0:T(1,128)S(1)} %bitcast.82), channel_id=1, source_target_pairs={{96,0},{192,96},{288,192},{384,288},{480,384},{576,480},{672,576},... | collective-permute-start | bytes 200 | tf_op jit(solution)/shard_map/ppermute | solution.py:17
  216.2 14.2 %collective-permute-start.15 = (f32[1,16]{1,0:T(1,128)S(1)}, f32[1,16]{1,0:T(1,128)S(1)}, u32[]{:S(2)}, u32[]{:S(2)}) collective-permute-start(f32[1,16]{1,0:T(1,128)S(1)} %bitcast.81), channel_id=1, source_target_pairs={{0,96},{96,192},{192,288},{288,384},{384,480},{480,576},{576,672},... | collective-permute-start | bytes 200 | tf_op jit(solution)/shard_map/ppermute | solution.py:16
  222.2 8.3 %collective-permute-start.12 = (f32[32,1]{0,1:T(1,128)S(1)}, f32[32,1]{0,1:T(1,128)S(1)}, u32[]{:S(2)}, u32[]{:S(2)}) collective-permute-start(f32[32,1]{0,1:T(1,128)S(1)} %get-tuple-element.42), channel_id=1, source_target_pairs={{8,0},{16,8},{24,16},{32,24},{40,32},{48,40},{56,48},{64,56},{72,6... | collective-permute-start | bytes 392 | tf_op jit(solution)/shard_map/ppermute | solution.py:17
  224.1 6.4 %collective-permute-start.13 = (f32[32,1]{0,1:T(1,128)S(1)}, f32[32,1]{0,1:T(1,128)S(1)}, u32[]{:S(2)}, u32[]{:S(2)}) collective-permute-start(f32[32,1]{0,1:T(1,128)S(1)} %get-tuple-element.41), channel_id=1, source_target_pairs={{0,8},{8,16},{16,24},{24,32},{32,40},{40,48},{48,56},{56,64},{64,7... | collective-permute-start | bytes 392 | tf_op jit(solution)/shard_map/ppermute | solution.py:16
  (3 other events, 5.4 us)
where the time goes:
time: 232 us; the launch traced here: 231 us
  local copies, waits for them, and re-layouts  76.8 us (33%)
  starting transfers between devices  56.8 us (24%)
  blocking collectives  33.4 us (14%)
  other arithmetic  31.6 us (14%)
  waiting for transfers between devices  21.9 us (9%)
  matrix products  9.34 us (4%)
    dynamic_update_slice x2, local copies, waits for them, and re-layouts, fix_axis(): lax.dynamic_update_slice_in_dim(padded, jnp.where(at_high, high_factor *...  56.8 us
    psum x1, blocking collectives, local(): totals = lax.psum(partial_sums, 'gz')  33.4 us
    ppermute x8, starting transfers between devices, padded_2(): before = lax.ppermute(last, axis, up)  31.3 us
    ppermute x8, starting transfers between devices, padded_2(): after = lax.ppermute(leading, axis, down)  25.6 us
    ppermute x8, waiting for transfers between devices, padded_2(): after = lax.ppermute(leading, axis, down)  19.5 us
    scatter-add x1, other arithmetic, sample_source(): jnp.zeros((ext_z * ext_x * ext_y,), jnp.float32).at[flat_index]  11.5 us
    dynamic_update_slice x2, local copies, waits for them, and re-layouts, fix_axis(): lax.dynamic_update_slice_in_dim(padded, jnp.where(at_low, low_factor * lo...  10.5 us
    dot_general x2, matrix products, relax(): jnp.einsum('ef,ezxy->fzxy', coupling, adjoint, precision=lax.Precision.HI...  8.43 us
  transfers between devices with their start and end apart: 16, of which 8 were waited for; matrix products, arithmetic and copies ran while one was open for 8% of the time, Pallas kernels for 0%

commit v1 on v0

v1 whole, which is shorter than its diff:
```python
import functools

import jax
import jax.numpy as jnp
from jax import lax
from jax.experimental import pallas as pl
from jax.experimental.pallas import tpu as pltpu
from jax.sharding import PartitionSpec as P

relax_rate = 0.9
keep_rate = 0.1

FIELDS = 6
LEV = 8
ROWS = 32
COLS = 128
EXT = 40
EDDY, RATE, STRIP = 6, 7, 8
SLOT = 16

VM = pl.BlockSpec(memory_space=pltpu.VMEM)
SM = pl.BlockSpec(memory_space=pltpu.SMEM)
PARAMS = pltpu.CompilerParams(vmem_limit_bytes=32 * 1024 * 1024)


def roll(v, shift, axis):
    return pltpu.roll(v, shift % v.shape[axis], axis)


def iota(shape, axis):
    return lax.broadcasted_iota(jnp.int32, shape, axis)


def f32(*shape):
    return jax.ShapeDtypeStruct(shape, jnp.float32)


def pack_y(adj, eddy, diag, metric, own, to_right, to_left):
    lane = iota((8, COLS), 1)
    slot, j = lane // SLOT, lane % SLOT
    quad, jj = j // 4, j % 4

    def level(z, _):
        zg, zq = z // 4, z % 4
        for t in range(ROWS // 8):
            rows = pl.ds(8 * t, 8)
            c = jnp.zeros((8, COLS), jnp.float32)
            for p in range(8):
                if p < FIELDS:
                    v = adj[p, z, rows, :]
                elif p == EDDY:
                    v = eddy[z, rows, :]
                else:
                    v = relax_rate / diag[z, rows, :]
                c = jnp.where((slot == p) & (j >= 1) & (j <= 6), roll(v, SLOT * p + 4, 1), c)
                if p < FIELDS:
                    m = metric[0, p, z, rows, :]
                    c = jnp.where((slot == p) & (j >= 8) & (j <= 9), roll(m, SLOT * p + 9, 1), c)
            c8 = roll(c, 8, 1)
            own[z, rows, :] = jnp.where(j < 8, c, jnp.where(j >= 9, c8, 0.0))
            at = 4 * zq
            right = jnp.where(jj == 0, pltpu.roll(c, (at + 120) % 128, 1), pltpu.roll(c, at, 1))
            left = jnp.where(jj == 3, pltpu.roll(c, (at + 122) % 128, 1), pltpu.roll(c, (at + 124) % 128, 1))
            here = quad == zq
            to_right[zg, rows, :] = jnp.where(here, right, to_right[zg, rows, :])
            to_left[zg, rows, :] = jnp.where(here, left, to_left[zg, rows, :])
        return 0

    to_right[...] = jnp.zeros_like(to_right)
    to_left[...] = jnp.zeros_like(to_left)
    lax.fori_loop(0, LEV, level, 0)


def make_source(total_y, idx, cells, weights, src, acc):
    start_x, start_y = idx[0] * ROWS, idx[1] * COLS
    r = iota((48, COLS), 0)
    row_x = jnp.where(r < EXT - 5, r, r - EXT) + start_x
    row_x = jnp.where(r < EXT, row_x, -1)
    l = iota((2 * COLS, COLS), 0)
    j = l - COLS
    col_y = jnp.where((j >= 1) & (j <= 6), j - 4, j + (COLS - 12))
    col_y = jnp.where(l < COLS, l, col_y) + start_y
    col_y = jnp.where((l < COLS) | ((j >= 1) & (j <= 6)) | ((j >= 9) & (j <= 14)), col_y, -1)
    acc[...] = jnp.zeros_like(acc)

    def chunk(k, _):
        c = cells[pl.ds(k, 1), :]
        w = weights[pl.ds(k, 1), :]
        x = ((c.astype(jnp.float32) + 0.5) * (1.0 / total_y)).astype(jnp.int32)
        y = c - x * total_y
        high = w.astype(jnp.bfloat16).astype(jnp.float32)
        mid = (w - high).astype(jnp.bfloat16).astype(jnp.float32)
        low = w - high - mid
        hit = row_x == x
        parts = [jnp.where(hit, v, 0.0).astype(jnp.bfloat16) for v in (low, mid, high)]
        one = jnp.where(col_y == y, 1.0, 0.0).astype(jnp.bfloat16)
        acc[...] += lax.dot_general(
            jnp.concatenate(parts, 0), one, (((1,), (1,)), ((), ())), preferred_element_type=jnp.float32
        )
        return 0

    lax.fori_loop(0, 16, chunk, 0)
    total = acc[0:EXT, :] + acc[48 : 48 + EXT, :] + acc[96 : 96 + EXT, :]
    src[0] = total[:, :COLS]
    src[1] = total[:, COLS:]


def pack_x(own, from_left, from_right, adj, eddy, diag, metric, strip, to_low, to_high):
    j = iota((ROWS, COLS), 1) % SLOT

    def level(z, _):
        zg, at = z // 4, 4 * (z % 4)
        low = pltpu.roll(from_left[zg], (128 - at) % 128, 1)
        high = pltpu.roll(from_right[zg], (140 - at) % 128, 1)
        s = jnp.where(j < 4, low, jnp.where(j >= 12, high, own[z]))
        strip[z] = s
        for msg, a, near in ((to_low, 0, 0), (to_high, ROWS - 3, ROWS - 1)):
            for p in range(FIELDS):
                msg[z, pl.ds(3 * p, 3), :] = adj[p, z, a : a + 3, :]
                msg[z, pl.ds(26 + p, 1), :] = metric[0, p, z, near : near + 1, :]
            msg[z, 18:21, :] = eddy[z, a : a + 3, :]
            b = a if a == 0 else a + 1
            msg[z, 21:23, :] = relax_rate / diag[z, b : b + 2, :]
            msg[z, 23:26, :] = s[a : a + 3, :]
        return 0

    lax.fori_loop(0, LEV, level, 0)


def spread(s, plane):
    m = jnp.where(iota(s.shape, 1) // SLOT == plane, s, 0.0)
    m = m + roll(m, SLOT, 1)
    m = m + roll(m, 2 * SLOT, 1)
    return m + roll(m, 4 * SLOT, 1)


def face(codes, i):
    return jnp.where(codes[i] == 1, 1.0, jnp.where(codes[i] == 2, -1.0, 0.0)).astype(jnp.float32)


class Edges:
    def __init__(self, idx, codes):
        self.low_x, self.high_x = idx[0] == 0, idx[0] == idx[3] - 1
        self.low_y, self.high_y = idx[1] == 0, idx[1] == idx[4] - 1
        self.low_z, self.high_z = idx[2] == 0, idx[2] == idx[5] - 1
        self.factors = [face(codes, i) for i in range(6)]
        self.row = iota((8, COLS), 0)
        self.j = iota((EXT, COLS), 1) % SLOT

    def rows(self, v):
        t4 = v[32:40]
        t4 = jnp.where((self.row == 7) & self.low_x, self.factors[0] * roll(v[0:8], 7, 0), t4)
        t4 = jnp.where((self.row == 0) & self.high_x, self.factors[1] * roll(v[24:32], 1, 0), t4)
        return jnp.concatenate([v[0:32], t4], 0)

    def lanes(self, v):
        low = jnp.where((self.j == 3) & self.low_y, self.factors[2] * roll(v, -1, 1), v)
        return jnp.where((self.j == 12) & self.high_y, self.factors[3] * roll(v, 1, 1), low)

    def flux(self, p, v):
        if p == FIELDS:
            v = self.lanes(v)
        return self.rows(v)


def put_coupling(coup, mix):
    slot = iota((1, COLS), 1) // SLOT
    for d in range(8):
        v = jnp.zeros((1, COLS), jnp.float32)
        for f in range(FIELDS):
            e = (f + d) % 8
            if e < FIELDS:
                v = jnp.where(slot == f, coup[e, f], v)
        mix[d : d + 1, :] = v


def sweep(center, below, above, value, rate, strip_rate, coup, mix, src, flag, store):
    lane = iota((EXT, COLS), 1)
    strip_flux = center(FIELDS)
    for f in range(FIELDS):
        v = center(f)
        left = jnp.where(lane == 0, roll(strip_flux, -(SLOT * f + 3), 1), roll(v, 1, 1))
        right = jnp.where(lane == COLS - 1, roll(strip_flux, COLS - 1 - (SLOT * f + 12), 1), roll(v, -1, 1))
        beside = above(f) + below(f) + roll(v, -1, 0) + roll(v, 1, 0) + right + left
        coupled = coup[0, f] * value(0)
        for e in range(1, FIELDS):
            coupled = coupled + coup[e, f] * value(e)
        rest = beside - coupled
        if f == 0:
            rest = rest + flag * src[0]
        store(f, keep_rate * value(f) + rate * rest)
    v = strip_flux
    beside = above(FIELDS) + below(FIELDS) + roll(v, -1, 0) + roll(v, 1, 0) + roll(v, -1, 1) + roll(v, 1, 1)
    a = value(FIELDS)
    coupled = a * mix[0:1, :]
    for d in range(1, 8):
        coupled = coupled + roll(a, -SLOT * d, 1) * mix[d : d + 1, :]
    store(FIELDS, keep_rate * a + strip_rate * (beside - coupled + flag * src[1]))


def level_sums(z, start_z, total_z, field, strip, metric, metric_row, x, sums, out, zo):
    w = 1.0 - 0.5 * (((start_z + z).astype(jnp.float32) + 0.5) / total_z)
    s0 = s2 = s1 = halo = None
    for f in range(FIELDS):
        a = field(f)
        own = a[:ROWS]
        out[f, zo] = own
        terms = [metric[k, f, z] * own for k in range(3)] + [metric_row[f, z] * a[ROWS:]]
        if f == 0:
            s0, s1, s2, halo = terms
        else:
            s0, s1, s2, halo = s0 + terms[0], s1 + terms[1], s2 + terms[2], halo + terms[3]
    s = x[z, STRIP, :ROWS, :]
    j = iota((ROWS, COLS), 1) % SLOT
    m = jnp.where(j == 3, roll(s, 3, 1), jnp.where(j == 12, roll(s, -3, 1), 0.0))
    sums[0, :ROWS] += w * s0
    sums[1, :ROWS] += w * s1
    sums[1, ROWS:] += w * halo
    sums[2, :ROWS] += w * s2
    sums[3, :ROWS] += w * (m * strip[:ROWS])


def pack_z(idx, codes, strip, from_low, from_high, adj, eddy, diag, x, metric_row, msg_a, msg_b):
    def level(z, _):
        lo, hi = from_low.at[z], from_high.at[z]
        for p in range(9):
            at = 3 * p
            if p < FIELDS:
                v = adj[p, z]
            elif p == EDDY:
                v = eddy[z]
            elif p == RATE:
                v = relax_rate / diag[z]
            else:
                v = strip[z]
                at = 23
            x[z, p, :ROWS, :] = v
            x[z, p, ROWS:, :] = jnp.zeros((8, COLS), jnp.float32)
            if p == RATE:
                x[z, p, 32:34, :] = hi[21:23, :]
                x[z, p, 38:40, :] = lo[21:23, :]
            else:
                x[z, p, 32:35, :] = hi[at : at + 3, :]
                x[z, p, 37:40, :] = lo[at : at + 3, :]
        for f in range(FIELDS):
            metric_row[f, z] = jnp.zeros((8, COLS), jnp.float32)
            metric_row[f, z, 0:1, :] = hi[26 + f : 27 + f, :]
            metric_row[f, z, 7:8, :] = lo[26 + f : 27 + f, :]
        return 0

    lax.fori_loop(0, LEV, level, 0)
    edges = Edges(idx, codes)
    even = idx[2] % 2 == 0
    for msg, top in ((msg_a, even), (msg_b, jnp.logical_not(even))):
        near = jnp.where(top, LEV - 1, 0)
        next_ = jnp.where(top, LEV - 2, 1)
        for p in range(9):
            msg[p] = x[near, p]
        e = x[next_, EDDY]
        for f in range(FIELDS):
            msg[9 + f] = edges.flux(f, x[next_, f] * e)
        s = x[next_, STRIP]
        msg[15] = edges.flux(FIELDS, s * spread(s, EDDY))


def inner_levels(idx, codes, coup, x, metric, metric_row, src, f0, a1, f1, out, sums, mix, a2):
    edges = Edges(idx, codes)
    start_z, total_z = idx[2] * LEV, (idx[5] * LEV).astype(jnp.float32)
    put_coupling(coup, mix)

    def fluxes(z, _):
        e = x[z, EDDY]
        for f in range(FIELDS):
            f0[z, f] = edges.flux(f, x[z, f] * e)
        s = x[z, STRIP]
        f0[z, FIELDS] = edges.flux(FIELDS, s * spread(s, EDDY))
        return 0

    lax.fori_loop(0, LEV, fluxes, 0)

    def first(z, _):
        e = x[z, EDDY]
        s = x[z, STRIP]
        se = spread(s, EDDY)

        def store(p, v):
            a1[z - 1, p] = v
            f1[z - 1, p] = edges.flux(p, v * (se if p == FIELDS else e))

        sweep(
            lambda p: f0[z, p],
            lambda p: f0[z - 1, p],
            lambda p: f0[z + 1, p],
            lambda p: x[z, STRIP if p == FIELDS else p],
            x[z, RATE],
            spread(s, RATE),
            coup,
            mix,
            src,
            0.0,
            store,
        )
        return 0

    lax.fori_loop(1, LEV - 1, first, 0)
    sums[...] = jnp.zeros_like(sums)

    def second(z, _):
        def store(p, v):
            a2[p] = v

        sweep(
            lambda p: f1[z - 1, p],
            lambda p: f1[z - 2, p],
            lambda p: f1[z, p],
            lambda p: a1[z - 1, p],
            x[z, RATE],
            spread(x[z, STRIP], RATE),
            coup,
            mix,
            src,
            0.0,
            store,
        )
        level_sums(z, start_z, total_z, lambda f: a2[f], a2[FIELDS], metric, metric_row, x, sums, out, z - 2)
        return 0

    lax.fori_loop(2, LEV - 2, second, 0)


def outer_levels(
    idx, codes, coup, x, from_a, from_b, metric, metric_row, src, f0, a1, f1, inner_out, inner_sums,
    out, share, sums, mix, a2, halo, fh, ah, gh, an, gn,
):
    edges = Edges(idx, codes)
    start_z, total_z = idx[2] * LEV, (idx[5] * LEV).astype(jnp.float32)
    hub = idx[5] * LEV // 4 - start_z
    put_coupling(coup, mix)
    sums[...] = inner_sums[...]
    halo[0] = from_a[...]
    halo[1] = from_b[...]
    for f in range(FIELDS):
        for z in range(2, LEV - 2):
            out[f, z] = inner_out[f, z - 2]
    even = idx[2] % 2 == 0

    def flag_of(z):
        return jnp.where(z == hub, 1.0, 0.0).astype(jnp.float32)

    def side(n, _):
        top = jnp.logical_xor(even, n == 1)
        near = jnp.where(top, LEV - 1, 0)
        next_ = jnp.where(top, LEV - 2, 1)
        third = jnp.where(top, LEV - 3, 2)
        over = jnp.where(top, LEV, -1)
        ghost = jnp.where(top, edges.high_z, edges.low_z)
        factor = jnp.where(top, edges.factors[5], edges.factors[4])
        e = halo[n, EDDY]
        s = halo[n, STRIP]
        se = spread(s, EDDY)
        for p in range(FIELDS + 1):
            v = s * se if p == FIELDS else halo[n, p] * e
            fh[p] = jnp.where(ghost, factor * f0[near, p], edges.flux(p, v))

        def store_near(p, v):
            an[p] = v
            e = spread(x[near, STRIP], EDDY) if p == FIELDS else x[near, EDDY]
            gn[p] = edges.flux(p, v * e)

        sweep(
            lambda p: f0[near, p],
            lambda p: fh[p],
            lambda p: f0[next_, p],
            lambda p: x[near, STRIP if p == FIELDS else p],
            x[near, RATE],
            spread(x[near, STRIP], RATE),
            coup,
            mix,
            src,
            flag_of(near),
            store_near,
        )

        def store_over(p, v):
            gh[p] = jnp.where(ghost, factor * gn[p], edges.flux(p, v * (se if p == FIELDS else e)))

        sweep(
            lambda p: fh[p],
            lambda p: halo[n, 9 + p],
            lambda p: f0[near, p],
            lambda p: halo[n, STRIP if p == FIELDS else p],
            halo[n, RATE],
            spread(s, RATE),
            coup,
            mix,
            src,
            flag_of(over),
            store_over,
        )

        def store_last(p, v):
            a2[p] = v

        def last(z, *levels):
            sweep(
                *levels, x[z, RATE], spread(x[z, STRIP], RATE), coup, mix, src, flag_of(z), store_last
            )
            level_sums(z, start_z, total_z, lambda f: a2[f], a2[FIELDS], metric, metric_row, x, sums, out, z)

        last(near, lambda p: gn[p], lambda p: gh[p], lambda p: f1[next_ - 1, p], lambda p: an[p])
        last(next_, lambda p: f1[next_ - 1, p], lambda p: gn[p], lambda p: f1[third - 1, p], lambda p: a1[next_ - 1, p])
        return 0

    lax.fori_loop(0, 2, side, 0)
    s1 = sums[1]
    stream = roll(s1, -1, 0)[:ROWS] - roll(s1, 1, 0)[:ROWS]
    t = sums[3, :ROWS]
    t = t + roll(t, 4 * SLOT, 1)
    t = t + roll(t, 2 * SLOT, 1)
    t = t + roll(t, SLOT, 1)
    s2 = sums[2, :ROWS]
    lane = iota((ROWS, COLS), 1)
    right = jnp.where(lane == COLS - 1, roll(t, 3, 1), roll(s2, -1, 1))
    left = jnp.where(lane == 0, roll(t, -3, 1), roll(s2, 1, 1))
    share[...] = (sums[0, :ROWS] - 0.5 * stream - 0.5 * (right - left)).T


def add_shares(parts, out):
    width = out.shape[1]
    total = parts[0:width, :]
    for i in range(1, COLS // width):
        total = total + parts[width * i : width * (i + 1), :]
    out[...] = total.T


def call(body, outs, ins, scratch=(), flops=1000000):
    return pl.pallas_call(
        body,
        out_shape=outs,
        in_specs=ins,
        out_specs=jax.tree.map(lambda _: VM, outs),
        scratch_shapes=list(scratch),
        compiler_params=PARAMS,
        cost_estimate=pl.CostEstimate(flops=flops, bytes_accessed=1 << 20, transcendentals=0),
    )


def local(adjoint_start, eddy_visc, diag_coef, coupling, metric_terms, sample_cells, sample_weights, face_codes):
    index = [lax.axis_index(a) for a in ("gx", "gy", "gz")]
    count = [lax.axis_size(a) for a in ("gx", "gy", "gz")]
    idx = jnp.stack(index + [jnp.int32(c) for c in count]).astype(jnp.int32)

    def shift(v, axis, step):
        n = lax.axis_size(axis)
        return lax.ppermute(v, axis, [(i, i + step) for i in range(n) if 0 <= i + step < n])

    def trade(v, axis, first):
        n = lax.axis_size(axis)
        pairs = [(i, i + 1) for i in range(first, n - 1, 2)]
        return lax.ppermute(v, axis, pairs + [(b, a) for a, b in pairs])

    def buf(*shape):
        return pltpu.VMEM(shape, jnp.float32)

    own, to_right, to_left = call(
        pack_y,
        (f32(LEV, ROWS, COLS), f32(2, ROWS, COLS), f32(2, ROWS, COLS)),
        [VM] * 4,
    )(adjoint_start, eddy_visc, diag_coef, metric_terms[2:3])
    from_left = shift(to_right, "gy", 1)
    from_right = shift(to_left, "gy", -1)
    src = call(functools.partial(make_source, COLS * count[1]), f32(2, EXT, COLS), [SM, VM, VM], [buf(144, 2 * COLS)])(
        idx, sample_cells.reshape(16, 128), sample_weights.reshape(16, 128)
    )
    strip, to_low, to_high = call(
        pack_x,
        (f32(LEV, ROWS, COLS), f32(LEV, ROWS, COLS), f32(LEV, ROWS, COLS)),
        [VM] * 7,
    )(own, from_left, from_right, adjoint_start, eddy_visc, diag_coef, metric_terms[1:2])
    from_low = shift(to_high, "gx", 1)
    from_high = shift(to_low, "gx", -1)
    x, metric_row, msg_a, msg_b = call(
        pack_z,
        (f32(LEV, 9, EXT, COLS), f32(FIELDS, LEV, 8, COLS), f32(16, EXT, COLS), f32(16, EXT, COLS)),
        [SM, SM] + [VM] * 6,
    )(idx, face_codes, strip, from_low, from_high, adjoint_start, eddy_visc, diag_coef)
    from_b = trade(msg_b, "gz", 1)
    from_a = trade(msg_a, "gz", 0)
    f0, a1, f1, inner_out, inner_sums = call(
        inner_levels,
        (
            f32(LEV, 7, EXT, COLS),
            f32(LEV - 2, 7, EXT, COLS),
            f32(LEV - 2, 7, EXT, COLS),
            f32(FIELDS, LEV - 4, ROWS, COLS),
            f32(4, EXT, COLS),
        ),
        [SM, SM, SM] + [VM] * 4,
        [buf(8, COLS), buf(7, EXT, COLS)],
    )(idx, face_codes, coupling, x, metric_terms, metric_row, src)
    adjoint, share = call(
        outer_levels,
        (f32(FIELDS, LEV, ROWS, COLS), f32(COLS, ROWS)),
        [SM, SM, SM] + [VM] * 11,
        [buf(4, EXT, COLS), buf(8, COLS), buf(7, EXT, COLS), buf(2, 16, EXT, COLS)] + [buf(7, EXT, COLS)] * 5,
    )(
        idx, face_codes, coupling, x, from_a, from_b, metric_terms, metric_row, src, f0, a1, f1, inner_out, inner_sums
    )
    parts = lax.all_to_all(share, "gz", 0, 0, tiled=True)
    height_grad = call(add_shares, f32(ROWS, COLS // count[2]), [VM])(parts)
    return (adjoint, height_grad)


def solution(mesh):
    return jax.shard_map(
        local,
        mesh=mesh,
        in_specs=(
            P(None, "gz", "gx", "gy"),
            P("gz", "gx", "gy"),
            P("gz", "gx", "gy"),
            P(),
            P(None, None, "gz", "gx", "gy"),
            P(),
            P(),
            P(),
        ),
        out_specs=(P(None, "gz", "gx", "gy"), P("gx", ("gy", "gz"))),
        check_vma=False,
    )
```

time: 232 us -> 69.4 us (0.30)
  the two profiles are of different devices: /device:TPU:230 before, /device:TPU:198 now
where the time goes in v1:
time: 69.4 us; the launch traced here: 69 us
  Pallas kernels  19 us (27%)
  blocking collectives  16.3 us (23%)
  starting transfers between devices  15.8 us (23%)
  waiting for transfers between devices  11.8 us (17%)
  local copies, waits for them, and re-layouts  4.45 us (6%)
  between operations  0.83 us (1%)
    all_to_all x1, blocking collectives, local(): parts = lax.all_to_all(share, 'gz', 0, 0, tiled=True)  16.3 us
    ppermute x4, starting transfers between devices, shift(): lax.ppermute(v, axis, [(i, i + step) for i in range(n) if 0 <= i + step <...  13.2 us
    ppermute x4, waiting for transfers between devices, shift(): lax.ppermute(v, axis, [(i, i + step) for i in range(n) if 0 <= i + step <...  11.8 us
    pallas_call x1, Pallas kernels, local(): call(inner_levels, (f32(LEV, 7, EXT, COLS), f32(LEV - 2, 7, EXT, COLS), f...  6.16 us
    pallas_call x1, Pallas kernels, local(): call(outer_levels, (f32(FIELDS, LEV, ROWS, COLS), f32(COLS, ROWS)), [SM,...  4.68 us
    pallas_call x1, Pallas kernels, local(): call(functools.partial(make_source, COLS * count[1]), f32(2, EXT, COLS),...  3.52 us
    ppermute x2, starting transfers between devices, trade(): return lax.ppermute(v, axis, pairs + [(b, a) for a, b in pairs])  2.6 us
    unnamed x19, local copies, waits for them, and re-layouts  2.28 us
  transfers between devices with their start and end apart: 6, of which 3 were waited for; matrix products, arithmetic and copies ran while one was open for 0% of the time, Pallas kernels for 14%

profile of v1, /device:TPU:198, one launch (start us, length us, event | category | flops | bytes accessed | tf_op | source)
XLA Modules:
  0.0 69.0 jit_solution(8030193100810793398)
XLA Ops:
  0.7 1.6 %fusion = (f32[1,6,8,32,128]{4,3,2,1,0:T(8,128)S(1)}, f32[1,6,8,32,128]{4,3,2,1,0:T(8,128)S(1)}) fusion(f32[3,6,8,32,128]{4,3,2,1,0:T(8,128)} %metric.3), kind=kLoop, calls=%fused_computation | loop fusion | bytes 3145728 | tf_op jit(solution)/shard_map/slice | solution.py:479
  2.3 1.7 %shard_map.95 = (f32[8,32,128]{2,1,0:T(8,128)S(1)}, f32[2,32,128]{2,1,0:T(8,128)S(1)}, f32[2,32,128]{2,1,0:T(8,128)S(1)}) custom-call(f32[6,8,32,128]{3,2,1,0:T(8,128)S(1)} %copy-done.1, f32[8,32,128]{2,1,0:T(8,128)S(1)} %copy-done.2, f32[8,32,128]{2,1,0:T(8,128)S(1)} %copy-done.3, f32[1,6,8,32,128]{4,3,2,1,0:T(8,128)S(1)} %get-tuple-element.39.metric), custom_call_target="tpu_custom_call" | custom-call | flops 1000000 | bytes 1048576 | tf_op jit(solution)/shard_map/pallas_call | solution.py:465
  4.0 5.5 %collective-permute-start = (f32[2,32,128]{2,1,0:T(8,128)S(1)}, f32[2,32,128]{2,1,0:T(8,128)S(1)}, u32[]{:S(2)}, u32[]{:S(2)}) collective-permute-start(f32[2,32,128]{2,1,0:T(8,128)S(1)} %get-tuple-element.20), channel_id=1, source_target_pairs={{0,8},{8,16},{16,24},{24,32},{32,40},{40,48},{48,56},{56,64},{64,7... | collective-permute-start | bytes 98312 | tf_op jit(solution)/shard_map/ppermute | solution.py:455
  9.5 1.9 %collective-permute-start.1 = (f32[2,32,128]{2,1,0:T(8,128)S(1)}, f32[2,32,128]{2,1,0:T(8,128)S(1)}, u32[]{:S(2)}, u32[]{:S(2)}) collective-permute-start(f32[2,32,128]{2,1,0:T(8,128)S(1)} %get-tuple-element.21), channel_id=1, source_target_pairs={{8,0},{16,8},{24,16},{32,24},{40,32},{48,40},{56,48},{64,56},{72,6... | collective-permute-start | bytes 98312 | tf_op jit(solution)/shard_map/ppermute | solution.py:455
  11.5 5.1 %collective-permute-done.1.from_right = f32[2,32,128]{2,1,0:T(8,128)S(1)} collective-permute-done((f32[2,32,128]{2,1,0:T(8,128)S(1)}, f32[2,32,128]{2,1,0:T(8,128)S(1)}, u32[]{:S(2)}, u32[]{:S(2)}) %collective-permute-start.1) | collective-permute-done | bytes 32800 | tf_op jit(solution)/shard_map/ppermute | solution.py:455
  16.6 1.4 %shard_map.96 = (f32[8,32,128]{2,1,0:T(8,128)S(1)}, f32[8,32,128]{2,1,0:T(8,128)}, f32[8,32,128]{2,1,0:T(8,128)}) custom-call(f32[8,32,128]{2,1,0:T(8,128)S(1)} %get-tuple-element.19.own, f32[2,32,128]{2,1,0:T(8,128)S(1)} %collective-permute-done.from_left, f32[2,32,128]{2,1,0:T(8,128)S(1)} %collective-permute-done.1.from_right, ...), custom_call_target="tpu_custom_call" | custom-call | flops 1000000 | bytes 1048576 | tf_op jit(solution)/shard_map/pallas_call | solution.py:475
  17.9 3.4 %collective-permute-start.2 = (f32[8,32,128]{2,1,0:T(8,128)}, f32[8,32,128]{2,1,0:T(8,128)}, u32[]{:S(2)}, u32[]{:S(2)}) collective-permute-start(f32[8,32,128]{2,1,0:T(8,128)} %get-tuple-element.23), channel_id=1, source_target_pairs={{0,96},{96,192},{192,288},{288,384},{384,480},{480,576},{576,672},... | collective-permute-start | bytes 393224 | tf_op jit(solution)/shard_map/ppermute | solution.py:455
  21.3 2.4 %collective-permute-start.3 = (f32[8,32,128]{2,1,0:T(8,128)}, f32[8,32,128]{2,1,0:T(8,128)}, u32[]{:S(2)}, u32[]{:S(2)}) collective-permute-start(f32[8,32,128]{2,1,0:T(8,128)} %get-tuple-element.24), channel_id=1, source_target_pairs={{96,0},{192,96},{288,192},{384,288},{480,384},{576,480},{672,576},... | collective-permute-start | bytes 393224 | tf_op jit(solution)/shard_map/ppermute | solution.py:455
  23.8 0.1 stack.15.idx
  23.9 1.2 %collective-permute-done.2.from_low = f32[8,32,128]{2,1,0:T(8,128)} collective-permute-done((f32[8,32,128]{2,1,0:T(8,128)}, f32[8,32,128]{2,1,0:T(8,128)}, u32[]{:S(2)}, u32[]{:S(2)}) %collective-permute-start.2) | collective-permute-done | bytes 131104 | tf_op jit(solution)/shard_map/ppermute | solution.py:455
  25.1 5.5 %collective-permute-done.3.from_high = f32[8,32,128]{2,1,0:T(8,128)} collective-permute-done((f32[8,32,128]{2,1,0:T(8,128)}, f32[8,32,128]{2,1,0:T(8,128)}, u32[]{:S(2)}, u32[]{:S(2)}) %collective-permute-start.3) | collective-permute-done | bytes 131104 | tf_op jit(solution)/shard_map/ppermute | solution.py:455
  30.6 0.7 copy-done.7
  31.3 1.5 %shard_map.97 = (f32[8,9,40,128]{3,2,1,0:T(8,128)S(1)}, f32[6,8,8,128]{3,2,1,0:T(8,128)S(1)}, f32[16,40,128]{2,1,0:T(8,128)S(1)}, f32[16,40,128]{2,1,0:T(8,128)S(1)}) custom-call(s32[6]{0:T(128)S(1)} %stack.15.idx, s32[6]{0:T(128)S(1)} %copy-done.7, f32[8,32,128]{2,1,0:T(8,128)S(1)} %get-tuple-element.22.strip, ...), custom_call_target="tpu_custom_call" | custom-call | flops 1000000 | bytes 1048576 | tf_op jit(solution)/shard_map/pallas_call | solution.py:482
  32.8 1.9 %collective-permute-start.4 = (f32[16,40,128]{2,1,0:T(8,128)S(1)}, f32[16,40,128]{2,1,0:T(8,128)S(1)}, u32[]{:S(2)}, u32[]{:S(2)}) collective-permute-start(f32[16,40,128]{2,1,0:T(8,128)S(1)} %get-tuple-element.26), channel_id=1, source_target_pairs={{0,1},{2,3},{4,5},{6,7},{1,0},{3,2},{5,4},{7,6},{8,9},{10,11},{12,... | collective-permute-start | bytes 983048 | tf_op jit(solution)/shard_map/ppermute | solution.py:460
  34.7 0.7 collective-permute-start.5
  35.4 0.7 copy-done.6
  36.1 3.5 %shard_map.98.src = f32[2,40,128]{2,1,0:T(8,128)S(1)} custom-call(s32[6]{0:T(128)S(1)} %stack.15.idx, s32[16,128]{1,0:T(8,128)S(1)} %bitcast.9, f32[16,128]{1,0:T(8,128)S(1)} %bitcast.10), custom_call_target="tpu_custom_call" | custom-call | flops 1000000 | bytes 1048576 | tf_op jit(solution)/shard_map/pallas_call | solution.py:472
  39.7 6.2 %shard_map.99 = (f32[8,7,40,128]{3,2,1,0:T(8,128)S(1)}, f32[6,7,40,128]{3,2,1,0:T(8,128)S(1)}, f32[6,7,40,128]{3,2,1,0:T(8,128)S(1)}, f32[6,4,32,128]{3,2,1,0:T(8,128)S(1)}, f32[4,40,128]{2,1,0:T(8,128)S(1)}) custom-call(s32[6]{0:T(128)S(1)} %stack.15.idx, s32[6]{0:T(128)S(1)} %copy-done.7, f32[6,6]{1,0:T(8,128)S(1)} %copy-done.4, ...), custom_call_target="tpu_custom_call" | custom-call | flops 1000000 | bytes 1048576 | tf_op jit(solution)/shard_map/pallas_call | solution.py:489
  45.9 4.7 %shard_map.100 = (f32[6,8,32,128]{3,2,1,0:T(8,128)}, f32[128,32]{1,0:T(8,128)S(1)}) custom-call(s32[6]{0:T(128)S(1)} %stack.15.idx, s32[6]{0:T(128)S(1)} %copy-done.7, f32[6,6]{1,0:T(8,128)S(1)} %copy-done.4, f32[8,9,40,128]{3,2,1,0:T(8,128)S(1)} %get-tuple-element.25.x, f32[16,40,128]{2,1,0:T(8,128)S(1)} %collective-permute-done.4.from_a, ...), custom_call_target="tpu_custom_call" | custom-call | flops 1000000 | bytes 1048576 | tf_op jit(solution)/shard_map/pallas_call | solution.py:501
  50.5 0.1 reshape.14
  50.6 16.3 %all_to_all.11 = f32[8,1,512]{2,1,0:T(1,128)S(1)} all-to-all(f32[8,1,512]{2,1,0:T(1,128)S(1)} %reshape.14), channel_id=1, replica_groups=mesh['gx'=8,'gy'=12,'gz'=8] {'gz'}, dimensions={0} | all-to-all | bytes 32768 | tf_op jit(solution)/shard_map/all_to_all | solution.py:509
  67.0 0.5 broadcast
  67.5 0.7 reduce
  68.3 0.7 copy.10
  (19 shorter events, 0.3 us)
Async XLA Ops:
  0.6 1.6 %copy-start.3 = (f32[8,32,128]{2,1,0:T(8,128)S(1)}, f32[8,32,128]{2,1,0:T(8,128)}, u32[]{:S(2)}) copy-start(f32[8,32,128]{2,1,0:T(8,128)} %diag.5) | copy-start | bytes 393220
  0.6 1.7 %copy-start.1 = (f32[6,8,32,128]{3,2,1,0:T(8,128)S(1)}, f32[6,8,32,128]{3,2,1,0:T(8,128)}, u32[]{:S(2)}) copy-start(f32[6,8,32,128]{3,2,1,0:T(8,128)} %adj.5) | copy-start | bytes 2359300
  0.6 1.7 %copy-start.2 = (f32[8,32,128]{2,1,0:T(8,128)S(1)}, f32[8,32,128]{2,1,0:T(8,128)}, u32[]{:S(2)}) copy-start(f32[8,32,128]{2,1,0:T(8,128)} %eddy.5) | copy-start | bytes 393220
  2.3 33.1 %copy-start.5 = (s32[2048]{0:T(1024)S(1)}, s32[2048]{0:T(1024)}, u32[]{:S(2)}) copy-start(s32[2048]{0:T(1024)} %param.13) | copy-start | bytes 24580
  2.3 37.3 %copy-start = (f32[3,6,8,32,128]{4,3,2,1,0:T(8,128)S(1)}, f32[3,6,8,32,128]{4,3,2,1,0:T(8,128)}, u32[]{:S(2)}) copy-start(f32[3,6,8,32,128]{4,3,2,1,0:T(8,128)} %metric.3) | copy-start | bytes 7077892
  2.3 37.3 %copy-start.4 = (f32[6,6]{1,0:T(8,128)S(1)}, f32[6,6]{1,0:T(8,128)}, u32[]{:S(2)}) copy-start(f32[6,6]{1,0:T(8,128)} %coup.3) | copy-start | bytes 436
  4.0 7.4 %collective-permute-start = (f32[2,32,128]{2,1,0:T(8,128)S(1)}, f32[2,32,128]{2,1,0:T(8,128)S(1)}, u32[]{:S(2)}, u32[]{:S(2)}) collective-permute-start(f32[2,32,128]{2,1,0:T(8,128)S(1)} %get-tuple-element.20), channel_id=1, source_target_pairs={{0,8},{8,16},{16,24},{24,32},{32,40},{40,48},{48,56},{56,64},{64,7... | collective-permute-start | bytes 98312 | tf_op jit(solution)/shard_map/ppermute | solution.py:455
  9.5 7.0 %collective-permute-start.1 = (f32[2,32,128]{2,1,0:T(8,128)S(1)}, f32[2,32,128]{2,1,0:T(8,128)S(1)}, u32[]{:S(2)}, u32[]{:S(2)}) collective-permute-start(f32[2,32,128]{2,1,0:T(8,128)S(1)} %get-tuple-element.21), channel_id=1, source_target_pairs={{8,0},{16,8},{24,16},{32,24},{40,32},{48,40},{56,48},{64,56},{72,6... | collective-permute-start | bytes 98312 | tf_op jit(solution)/shard_map/ppermute | solution.py:455
  17.9 7.2 %collective-permute-start.2 = (f32[8,32,128]{2,1,0:T(8,128)}, f32[8,32,128]{2,1,0:T(8,128)}, u32[]{:S(2)}, u32[]{:S(2)}) collective-permute-start(f32[8,32,128]{2,1,0:T(8,128)} %get-tuple-element.23), channel_id=1, source_target_pairs={{0,96},{96,192},{192,288},{288,384},{384,480},{480,576},{576,672},... | collective-permute-start | bytes 393224 | tf_op jit(solution)/shard_map/ppermute | solution.py:455
  21.3 9.3 %collective-permute-start.3 = (f32[8,32,128]{2,1,0:T(8,128)}, f32[8,32,128]{2,1,0:T(8,128)}, u32[]{:S(2)}, u32[]{:S(2)}) collective-permute-start(f32[8,32,128]{2,1,0:T(8,128)} %get-tuple-element.24), channel_id=1, source_target_pairs={{96,0},{192,96},{288,192},{384,288},{480,384},{576,480},{672,576},... | collective-permute-start | bytes 393224 | tf_op jit(solution)/shard_map/ppermute | solution.py:455
  30.6 0.7 copy-start.7
  32.8 13.0 %collective-permute-start.4 = (f32[16,40,128]{2,1,0:T(8,128)S(1)}, f32[16,40,128]{2,1,0:T(8,128)S(1)}, u32[]{:S(2)}, u32[]{:S(2)}) collective-permute-start(f32[16,40,128]{2,1,0:T(8,128)S(1)} %get-tuple-element.26), channel_id=1, source_target_pairs={{0,1},{2,3},{4,5},{6,7},{1,0},{3,2},{5,4},{7,6},{8,9},{10,11},{12,... | collective-permute-start | bytes 983048 | tf_op jit(solution)/shard_map/ppermute | solution.py:460
  34.7 11.1 %collective-permute-start.5 = (f32[16,40,128]{2,1,0:T(8,128)S(1)}, f32[16,40,128]{2,1,0:T(8,128)S(1)}, u32[]{:S(2)}, u32[]{:S(2)}) collective-permute-start(f32[16,40,128]{2,1,0:T(8,128)S(1)} %get-tuple-element.27), channel_id=1, source_target_pairs={{1,2},{3,4},{5,6},{2,1},{4,3},{6,5},{9,10},{11,12},{13,14},{10,9},... | collective-permute-start | bytes 983048 | tf_op jit(solution)/shard_map/ppermute | solution.py:460
  35.4 0.7 %copy-start.6 = (f32[2048]{0:T(1024)S(1)}, f32[2048]{0:T(1024)}, u32[]{:S(2)}) copy-start(f32[2048]{0:T(1024)} %param.14) | copy-start | bytes 24580

commit v2 on v0

v2 whole, which is shorter than its diff:
```python
import functools

import jax
import jax.numpy as jnp
from jax import lax
from jax.experimental import pallas as pl
from jax.experimental.pallas import tpu as pltpu
from jax.sharding import PartitionSpec as P

relax_rate = 0.9
keep_rate = 0.1

FIELDS = 6
LEV = 8
ROWS = 32
COLS = 128
EXT = 40
EDDY, RATE, STRIP = 6, 7, 8
SLOT = 16

VM = pl.BlockSpec(memory_space=pltpu.VMEM)
SM = pl.BlockSpec(memory_space=pltpu.SMEM)
HB = pl.BlockSpec(memory_space=pltpu.HBM)
PARAMS = pltpu.CompilerParams(vmem_limit_bytes=16 * 1024 * 1024)


def roll(v, shift, axis):
    return pltpu.roll(v, shift % v.shape[axis], axis)


def iota(shape, axis):
    return lax.broadcasted_iota(jnp.int32, shape, axis)


def f32(*shape):
    return jax.ShapeDtypeStruct(shape, jnp.float32)


def pack_y(adj, eddy, diag, metric, *rest):
    own, to_right, to_left, adj_buf, eddy_buf, diag_buf, metric_buf, sems = rest[-8:]
    half = LEV // 2
    copies = []
    for h in range(2):
        at = pl.ds(h * half, half)
        pairs = (
            (adj.at[:, at], adj_buf.at[:, at]),
            (eddy.at[at], eddy_buf.at[at]),
            (diag.at[at], diag_buf.at[at]),
            (metric.at[2, :, at], metric_buf.at[:, at]),
        )
        copies.append([pltpu.make_async_copy(a, b, sems.at[h, i]) for i, (a, b) in enumerate(pairs)])
    for c in copies[0] + copies[1]:
        c.start()
    lane = iota((8, COLS), 1)
    slot, j = lane // SLOT, lane % SLOT
    quad, jj = j // 4, j % 4
    edge_at = [(slot == p) & (j >= 1) & (j <= 6) for p in range(8)]
    metric_at = [(slot == p) & (j >= 8) & (j <= 9) for p in range(FIELDS)]
    for zg in range(2):
        for c in copies[zg]:
            c.wait()
        for t in range(ROWS // 8):
            rows = pl.ds(8 * t, 8)
            right = left = jnp.zeros((8, COLS), jnp.float32)
            for zq in range(4):
                z = 4 * zg + zq
                c = jnp.zeros((8, COLS), jnp.float32)
                for p in range(8):
                    if p < FIELDS:
                        v = adj_buf[p, z, rows, :]
                    elif p == EDDY:
                        v = eddy_buf[z, rows, :]
                    else:
                        v = relax_rate / diag_buf[z, rows, :]
                    c = jnp.where(edge_at[p], roll(v, SLOT * p + 4, 1), c)
                    if p < FIELDS:
                        c = jnp.where(metric_at[p], roll(metric_buf[p, z, rows, :], SLOT * p + 9, 1), c)
                own[z, rows, :] = jnp.where(j < 8, c, jnp.where(j >= 9, roll(c, 8, 1), 0.0))
                at = 4 * zq
                here = quad == zq
                right = jnp.where(here, jnp.where(jj == 0, roll(c, at - 8, 1), roll(c, at, 1)), right)
                left = jnp.where(here, jnp.where(jj == 3, roll(c, at - 6, 1), roll(c, at - 4, 1)), left)
            to_right[zg, rows, :] = right
            to_left[zg, rows, :] = left


def make_source(total_y, idx, cells, weights, src):
    start_x, start_y = idx[0] * ROWS, idx[1] * COLS
    r = iota((48, COLS), 0)
    row_x = jnp.where(r < EXT - 5, r, r - EXT) + start_x
    row_x = jnp.where(r < EXT, row_x, -1)
    l = iota((2 * COLS, COLS), 0)
    j = l - COLS
    col_y = jnp.where((j >= 1) & (j <= 6), j - 4, j + (COLS - 12))
    col_y = jnp.where(l < COLS, l, col_y) + start_y
    col_y = jnp.where((l < COLS) | ((j >= 1) & (j <= 6)) | ((j >= 9) & (j <= 14)), col_y, -1)
    acc = jnp.zeros((144, 2 * COLS), jnp.float32)
    for k in range(0, 16, 2):
        left, one = [], []
        for q in (k, k + 1):
            c = cells[q : q + 1, :]
            w = weights[q : q + 1, :]
            x = ((c.astype(jnp.float32) + 0.5) * (1.0 / total_y)).astype(jnp.int32)
            y = c - x * total_y
            high = w.astype(jnp.bfloat16).astype(jnp.float32)
            mid = (w - high).astype(jnp.bfloat16).astype(jnp.float32)
            low = w - high - mid
            hit = row_x == x
            left.append(jnp.concatenate([jnp.where(hit, v, 0.0).astype(jnp.bfloat16) for v in (low, mid, high)], 0))
            one.append(jnp.where(col_y == y, 1.0, 0.0).astype(jnp.bfloat16))
        acc = acc + lax.dot_general(
            jnp.concatenate(left, 1),
            jnp.concatenate(one, 1),
            (((1,), (1,)), ((), ())),
            preferred_element_type=jnp.float32,
        )
    total = acc[0:EXT, :] + acc[48 : 48 + EXT, :] + acc[96 : 96 + EXT, :]
    src[0] = total[:, :COLS]
    src[1] = total[:, COLS:]


HIGH_AT = [0, 3, 6, 9, 12, 15, 18, 21, 23]
LOW_AT = [6 + a for a in HIGH_AT]
HIGH_METRIC, LOW_METRIC = 26, 0


def pack_x(src, own, from_left, from_right, adj, eddy, diag, metric, strip, to_low, to_high):
    j = iota((ROWS, COLS), 1) % SLOT
    for z in range(LEV):
        zg, at = z // 4, 4 * (z % 4)
        low = roll(from_left[zg], -at, 1)
        high = roll(from_right[zg], 12 - at, 1)
        s = jnp.where(j < 4, low, jnp.where(j >= 12, high, own[z]))
        strip[z] = s
        sides = ((to_low, 0, 0, 0, HIGH_AT, HIGH_METRIC), (to_high, ROWS - 3, ROWS - 2, ROWS - 1, LOW_AT, LOW_METRIC))
        for msg, a, b, near, at, metric_at in sides:
            for p in range(FIELDS):
                msg[z, at[p] : at[p] + 3, :] = adj[p, z, a : a + 3, :]
                msg[z, metric_at + p : metric_at + p + 1, :] = metric[1, p, z, near : near + 1, :]
            msg[z, at[EDDY] : at[EDDY] + 3, :] = eddy[z, a : a + 3, :]
            msg[z, at[RATE] : at[RATE] + 2, :] = relax_rate / diag[z, b : b + 2, :]
            msg[z, at[STRIP] : at[STRIP] + 3, :] = s[a : a + 3, :]


def lanes_of(v, plane):
    return jnp.take_along_axis(v, iota(v.shape, 1) % SLOT + SLOT * plane, axis=1)


def face(codes, i):
    return jnp.where(codes[i] == 1, 1.0, jnp.where(codes[i] == 2, -1.0, 0.0)).astype(jnp.float32)


class Edges:
    def __init__(self, info):
        self.low_x, self.high_x = info[0] == 0, info[0] == info[3] - 1
        self.low_y, self.high_y = info[1] == 0, info[1] == info[4] - 1
        self.low_z, self.high_z = info[2] == 0, info[2] == info[5] - 1
        self.factors = [face(info, 6 + i) for i in range(6)]
        row, j = iota((8, COLS), 0), iota((EXT, COLS), 1) % SLOT
        self.row_low, self.row_high = (row == 7) & self.low_x, (row == 0) & self.high_x
        self.j = j
        self.ghost_low, self.ghost_high = (j == 3) & self.low_y, (j == 12) & self.high_y
        self.own_low, self.own_high = (j == 4) & self.low_y, (j == 11) & self.high_y

    def flux(self, v):
        t4 = v[32:40]
        t4 = jnp.where(self.row_low, self.factors[0] * roll(v[0:8], 7, 0), t4)
        t4 = jnp.where(self.row_high, self.factors[1] * roll(v[24:32], 1, 0), t4)
        return jnp.concatenate([v[0:32], t4], 0)


def put_coupling(coup, mix):
    slot = iota((1, COLS), 1) // SLOT
    for e in range(FIELDS):
        v = jnp.zeros((1, COLS), jnp.float32)
        for f in range(FIELDS):
            v = jnp.where(slot == f, coup[e, f], v)
        mix[e : e + 1, :] = v


def sweep(edges, center, vertical, value, rate, strip_rate, coup, mix, store, src=None, flag=None):
    lane = iota((EXT, COLS), 1)
    f2, f3 = edges.factors[2], edges.factors[3]
    v = center(FIELDS)
    up, down = roll(v, 1, 1), roll(v, -1, 1)
    fixed = jnp.where(edges.ghost_low, f2 * down, jnp.where(edges.ghost_high, f3 * up, v))
    both = jnp.where(edges.j == 3, fixed, roll(fixed, -10, 1))
    beside = vertical(FIELDS) + roll(v, -1, 0) + roll(v, 1, 0)
    beside = beside + jnp.where(edges.own_low, f2 * v, up) + jnp.where(edges.own_high, f3 * v, down)
    a = value(FIELDS)
    coupled = lanes_of(a, 0) * mix[0:1, :]
    for e in range(1, FIELDS):
        coupled = coupled + lanes_of(a, e) * mix[e : e + 1, :]
    rest = beside - coupled
    if src is not None:
        rest = rest + flag * src[1]
    store(FIELDS, keep_rate * a + strip_rate * rest)
    for f in range(FIELDS):
        v = center(f)
        end = roll(both, -(SLOT * f + 3), 1)
        left = jnp.where(lane == 0, end, roll(v, 1, 1))
        right = jnp.where(lane == COLS - 1, end, roll(v, -1, 1))
        beside = vertical(f) + roll(v, -1, 0) + roll(v, 1, 0) + right + left
        coupled = coup[0, f] * value(0)
        for e in range(1, FIELDS):
            coupled = coupled + coup[e, f] * value(e)
        rest = beside - coupled
        if f == 0 and src is not None:
            rest = rest + flag * src[0]
        store(f, keep_rate * value(f) + rate * rest)


def level_sums(z, info, field, edge_strip, strip, metric, metric_row, sums, out, zo):
    total_z = (info[5] * LEV).astype(jnp.float32)
    w = 1.0 - 0.5 * (((info[2] * LEV + z).astype(jnp.float32) + 0.5) / total_z)
    totals = None
    for f in range(FIELDS):
        a = field(f)
        own = a[:ROWS]
        out[f, zo] = own
        terms = [metric[k, f, z] * own for k in range(3)] + [metric_row[f, z] * a[ROWS:]]
        totals = terms if f == 0 else [s + t for s, t in zip(totals, terms)]
    s = strip[z, :ROWS]
    j = iota((ROWS, COLS), 1) % SLOT
    m = jnp.where(j == 3, roll(s, 3, 1), jnp.where(j == 12, roll(s, -3, 1), 0.0))
    sums[0, :ROWS] += w * totals[0]
    sums[1, :ROWS] += w * totals[1]
    sums[1, ROWS:] += w * totals[3]
    sums[2, :ROWS] += w * totals[2]
    sums[3, :ROWS] += w * (m * edge_strip[:ROWS])


def pack_z(info, strip, from_low, from_high, adj, eddy, diag, halo, metric_row, msg_a, msg_b):
    row = iota((8, COLS), 0)
    for z in range(LEV):
        for p in range(9):
            at = 2 if p == RATE else 3
            above = from_high[z, HIGH_AT[p] : HIGH_AT[p] + 8, :]
            start = LOW_AT[p] - (8 - at)
            halo[z, p] = jnp.where(row < 4, above, from_low[z, start : start + 8, :])
        for f in range(FIELDS):
            above = jnp.broadcast_to(from_high[z, HIGH_METRIC + f : HIGH_METRIC + f + 1, :], (8, COLS))
            below = jnp.broadcast_to(from_low[z, LOW_METRIC + f : LOW_METRIC + f + 1, :], (8, COLS))
            metric_row[f, z] = jnp.where(row < 4, above, below)
    edges = Edges(info)
    even = info[2] % 2 == 0

    def plane(z, p):
        own = adj[p, z] if p < FIELDS else eddy[z] if p == EDDY else relax_rate / diag[z] if p == RATE else strip[z]
        return jnp.concatenate([own, halo[z, p]], 0)

    for msg, top in ((msg_a, even), (msg_b, jnp.logical_not(even))):
        near = jnp.where(top, LEV - 1, 0)
        next_ = jnp.where(top, LEV - 2, 1)
        for p in range(9):
            msg[p] = plane(near, p)
        e = plane(next_, EDDY)
        for f in range(FIELDS):
            msg[9 + f] = edges.flux(plane(next_, f) * e)
        s = plane(next_, STRIP)
        msg[15] = edges.flux(s * lanes_of(s, EDDY))


def inner_levels(
    info, coup, adj, eddy, diag, strip, halo, metric, metric_row, src,
    f0, near1, next2, f1, rates, edge_eddy, edge_rate, out, sums, mix, a1, a2,
):
    edges = Edges(info)
    put_coupling(coup, mix)
    hub = info[5] * LEV // 4 - info[2] * LEV
    flag = jnp.where(hub == 0, 1.0, 0.0).astype(jnp.float32)

    def value(z, p):
        own = adj[p, z] if p < FIELDS else strip[z]
        return jnp.concatenate([own, halo[z, STRIP if p == FIELDS else p]], 0)

    def eddies(z):
        return jnp.concatenate([eddy[z], halo[z, EDDY]], 0)

    for z in range(LEV):
        rates[z] = jnp.concatenate([relax_rate / diag[z], halo[z, RATE]], 0)
        s = value(z, FIELDS)
        edge_eddy[z] = lanes_of(s, EDDY)
        edge_rate[z] = lanes_of(s, RATE)
        e = eddies(z)
        for f in range(FIELDS):
            f0[z, f] = edges.flux(value(z, f) * e)
        f0[z, FIELDS] = edges.flux(s * edge_eddy[z])

    def around(array, z):
        return lambda p: array[z - 1, p] + array[z + 1, p]

    def first(z, vertical, store, **more):
        sweep(edges, lambda p: f0[z, p], vertical, lambda p: value(z, p), rates[z], edge_rate[z], coup, mix, store, **more)

    def store_near(i):
        def store(p, v):
            near1[i, p] = v

        return store

    def store_inner(z):
        def store(p, v):
            a1[z, p] = v
            f1[z, p] = edges.flux(v * (edge_eddy[z] if p == FIELDS else eddies(z)))

        return store

    first(0, lambda p: f0[1, p], store_near(0), src=src, flag=flag)
    first(LEV - 1, lambda p: f0[LEV - 2, p], store_near(1))
    for z in range(1, LEV - 1):
        first(z, around(f0, z), store_inner(z))
    sums[...] = jnp.zeros_like(sums)

    def second(z, vertical, store):
        sweep(edges, lambda p: f1[z, p], vertical, lambda p: a1[z, p], rates[z], edge_rate[z], coup, mix, store)

    def store_next(i):
        def store(p, v):
            next2[i, p] = v

        return store

    def store_last(z):
        def store(p, v):
            a2[z, p] = v

        return store

    second(1, lambda p: f1[2, p], store_next(0))
    second(LEV - 2, lambda p: f1[LEV - 3, p], store_next(1))
    for z in range(2, LEV - 2):
        second(z, around(f1, z), store_last(z))
        level_sums(z, info, lambda f: a2[z, f], a2[z, FIELDS], strip, metric, metric_row, sums, out, z - 2)


def outer_levels(
    info, coup, eddy, strip, halo_rows, from_a, from_b, metric, metric_row, src,
    f0, near1, next2, f1, rates, edge_eddy, edge_rate, inner_out, inner_sums,
    out, share, sums, mix, fh, ah, gh, an, gn, a2,
):
    edges = Edges(info)
    hub = info[5] * LEV // 4 - info[2] * LEV
    put_coupling(coup, mix)
    sums[...] = inner_sums[...]
    for f in range(FIELDS):
        for z in range(2, LEV - 2):
            out[f, z] = inner_out[f, z - 2]
    even = info[2] % 2 == 0

    def flag_of(z):
        return jnp.where(z == hub, 1.0, 0.0).astype(jnp.float32)

    for n, msg in enumerate((from_a, from_b)):
        top = even if n == 0 else jnp.logical_not(even)
        i = jnp.where(top, 1, 0)
        near = jnp.where(top, LEV - 1, 0)
        next_ = jnp.where(top, LEV - 2, 1)
        over = jnp.where(top, LEV, -1)
        ghost = jnp.where(top, edges.high_z, edges.low_z)
        factor = jnp.where(top, edges.factors[5], edges.factors[4])
        eddy_over = msg[EDDY]
        s = msg[STRIP]
        edge_eddy_over = lanes_of(s, EDDY)
        eddy_near = jnp.concatenate([eddy[near], halo_rows[near, EDDY]], 0)
        for p in range(FIELDS + 1):
            v = s * edge_eddy_over if p == FIELDS else msg[p] * eddy_over
            v = jnp.where(ghost, factor * f0[near, p], edges.flux(v))
            fh[n, p] = v
            r, e = (edge_rate[near], edge_eddy[near]) if p == FIELDS else (rates[near], eddy_near)
            v = near1[i, p] + r * v
            an[n, p] = v
            gn[n, p] = edges.flux(v * e)

        def store_over(p, v):
            v = edges.flux(v * (edge_eddy_over if p == FIELDS else eddy_over))
            gh[n, p] = jnp.where(ghost, factor * gn[n, p], v)

        sweep(
            edges,
            lambda p: fh[n, p],
            lambda p: msg[9 + p] + f0[near, p],
            lambda p: msg[STRIP if p == FIELDS else p],
            msg[RATE],
            lanes_of(s, RATE),
            coup,
            mix,
            store_over,
            src,
            flag_of(over),
        )

        def after(p):
            r = edge_rate[next_] if p == FIELDS else rates[next_]
            return next2[i, p] + r * gn[n, p]

        level_sums(next_, info, after, after(FIELDS), strip, metric, metric_row, sums, out, next_)

        def store_last(p, v):
            a2[n, p] = v

        sweep(
            edges,
            lambda p: gn[n, p],
            lambda p: gh[n, p] + f1[next_, p],
            lambda p: an[n, p],
            rates[near],
            edge_rate[near],
            coup,
            mix,
            store_last,
            src,
            flag_of(near),
        )
        level_sums(near, info, lambda f: a2[n, f], a2[n, FIELDS], strip, metric, metric_row, sums, out, near)

    s1 = sums[1]
    stream = roll(s1, -1, 0)[:ROWS] - roll(s1, 1, 0)[:ROWS]
    t = sums[3, :ROWS]
    t = t + roll(t, 4 * SLOT, 1)
    t = t + roll(t, 2 * SLOT, 1)
    t = t + roll(t, SLOT, 1)
    s2 = sums[2, :ROWS]
    lane = iota((ROWS, COLS), 1)
    right = jnp.where(lane == COLS - 1, roll(t, 3, 1), roll(s2, -1, 1))
    left = jnp.where(lane == 0, roll(t, -3, 1), roll(s2, 1, 1))
    total = sums[0, :ROWS] - 0.5 * stream - 0.5 * (right - left)
    turned = jnp.concatenate([total, jnp.zeros((COLS - ROWS, COLS), jnp.float32)], 0).T
    count, width = share.shape[0], COLS // share.shape[0]
    group = iota((8, COLS), 1) // ROWS
    for k in range(count):
        v = turned[width * k : width * k + 8]
        for q in range(1, width // 8):
            v = jnp.where(group == q, roll(turned[width * k + 8 * q : width * k + 8 * q + 8], ROWS * q, 1), v)
        share[k] = v


def add_shares(parts, out):
    total = parts[0]
    for i in range(1, parts.shape[0]):
        total = total + parts[i]
    for q in range(out.shape[0] // 8):
        out[8 * q : 8 * q + 8, :] = roll(total, -ROWS * q, 1)[:, :ROWS]


def call(body, outs, ins, scratch=(), flops=1000000):
    return pl.pallas_call(
        body,
        out_shape=outs,
        in_specs=ins,
        out_specs=jax.tree.map(lambda _: VM, outs),
        scratch_shapes=list(scratch),
        compiler_params=PARAMS,
        cost_estimate=pl.CostEstimate(flops=flops, bytes_accessed=1 << 20, transcendentals=0),
    )


def local(adjoint_start, eddy_visc, diag_coef, coupling, metric_terms, sample_cells, sample_weights, face_codes):
    index = [lax.axis_index(a) for a in ("gx", "gy", "gz")]
    count = [lax.axis_size(a) for a in ("gx", "gy", "gz")]
    place = jnp.stack(index + [jnp.int32(c) for c in count]).astype(jnp.int32)
    info = jnp.concatenate([place, face_codes])
    cells, weights = sample_cells.reshape(16, 128), sample_weights.reshape(16, 128)

    def shift(v, axis, step):
        n = lax.axis_size(axis)
        return lax.ppermute(v, axis, [(i, i + step) for i in range(n) if 0 <= i + step < n])

    def trade(v, axis, first):
        n = lax.axis_size(axis)
        pairs = [(i, i + 1) for i in range(first, n - 1, 2)]
        return lax.ppermute(v, axis, pairs + [(b, a) for a, b in pairs])

    def buf(*shape):
        return pltpu.VMEM(shape, jnp.float32)

    level = (LEV, ROWS, COLS)
    own, to_right, to_left = call(
        pack_y,
        (f32(*level), f32(2, ROWS, COLS), f32(2, ROWS, COLS)),
        [HB] * 4 + [VM, VM, SM],
        [buf(FIELDS, *level), buf(*level), buf(*level), buf(FIELDS, *level), pltpu.SemaphoreType.DMA((2, 4))],
    )(adjoint_start, eddy_visc, diag_coef, metric_terms, cells, weights, coupling)
    from_left = shift(to_right, "gy", 1)
    from_right = shift(to_left, "gy", -1)
    src = call(functools.partial(make_source, COLS * count[1]), f32(2, EXT, COLS), [SM, VM, VM])(info, cells, weights)
    strip, to_low, to_high = call(pack_x, (f32(*level),) * 3, [VM] * 8)(
        src, own, from_left, from_right, adjoint_start, eddy_visc, diag_coef, metric_terms
    )
    from_low = shift(to_high, "gx", 1)
    from_high = shift(to_low, "gx", -1)
    halo, metric_row, msg_a, msg_b = call(
        pack_z,
        (f32(LEV, 9, 8, COLS), f32(FIELDS, LEV, 8, COLS), f32(16, EXT, COLS), f32(16, EXT, COLS)),
        [SM] + [VM] * 6,
    )(info, strip, from_low, from_high, adjoint_start, eddy_visc, diag_coef)
    from_b = trade(msg_b, "gz", 1)
    from_a = trade(msg_a, "gz", 0)
    ext = (EXT, COLS)
    *inner, inner_out, inner_sums = call(
        inner_levels,
        (
            f32(LEV, 7, *ext),
            f32(2, 7, *ext),
            f32(2, 7, *ext),
            f32(LEV, 7, *ext),
            f32(LEV, *ext),
            f32(LEV, *ext),
            f32(LEV, *ext),
            f32(FIELDS, LEV - 4, ROWS, COLS),
            f32(4, *ext),
        ),
        [SM, SM] + [VM] * 8,
        [buf(8, COLS), buf(LEV, 7, *ext), buf(LEV, 7, *ext)],
    )(info, coupling, adjoint_start, eddy_visc, diag_coef, strip, halo, metric_terms, metric_row, src)
    adjoint, share = call(
        outer_levels,
        (f32(FIELDS, *level), f32(count[2], 8, COLS)),
        [SM, SM] + [VM] * 17,
        [buf(4, *ext), buf(8, COLS)] + [buf(2, 7, *ext)] * 6,
    )(info, coupling, eddy_visc, strip, halo, from_a, from_b, metric_terms, metric_row, src, *inner, inner_out, inner_sums)
    parts = lax.all_to_all(share, "gz", 0, 0, tiled=True)
    height_grad = call(add_shares, f32(COLS // count[2], ROWS), [VM])(parts).T
    return (adjoint, height_grad)


def solution(mesh):
    return jax.shard_map(
        local,
        mesh=mesh,
        in_specs=(
            P(None, "gz", "gx", "gy"),
            P("gz", "gx", "gy"),
            P("gz", "gx", "gy"),
            P(),
            P(None, None, "gz", "gx", "gy"),
            P(),
            P(),
            P(),
        ),
        out_specs=(P(None, "gz", "gx", "gy"), P("gx", ("gy", "gz"))),
        check_vma=False,
    )
```

time: 232 us -> 70.8 us (0.31)
  the two profiles are of different devices: /device:TPU:230 before, /device:TPU:192 now
where the time goes in v2:
time: 70.8 us; the launch traced here: 70.2 us
  blocking collectives  23.5 us (33%)
  starting transfers between devices  14.7 us (21%)
  Pallas kernels  14.6 us (21%)
  local copies, waits for them, and re-layouts  8.7 us (12%)
  waiting for transfers between devices  7.91 us (11%)
  between operations  0.81 us (1%)
    all_to_all x1, blocking collectives, local(): parts = lax.all_to_all(share, 'gz', 0, 0, tiled=True)  23.5 us
    ppermute x4, starting transfers between devices, shift(): lax.ppermute(v, axis, [(i, i + step) for i in range(n) if 0 <= i + step <...  12.1 us
    ppermute x4, waiting for transfers between devices, shift(): lax.ppermute(v, axis, [(i, i + step) for i in range(n) if 0 <= i + step <...  7.91 us
    unnamed x30, local copies, waits for them, and re-layouts  7.38 us
    pallas_call x1, Pallas kernels, local(): call(inner_levels, (f32(LEV, 7, *ext), f32(2, 7, *ext), f32(2, 7, *ext),...  4.52 us
    pallas_call x1, Pallas kernels, local(): call(pack_y, (f32(*level), f32(2, ROWS, COLS), f32(2, ROWS, COLS)), [HB]...  3.77 us
    pallas_call x1, Pallas kernels, local(): call(outer_levels, (f32(FIELDS, *level), f32(count[2], 8, COLS)), [SM, SM...  2.9 us
    ppermute x2, starting transfers between devices, trade(): return lax.ppermute(v, axis, pairs + [(b, a) for a, b in pairs])  2.6 us
  transfers between devices with their start and end apart: 6, of which 3 were waited for; matrix products, arithmetic and copies ran while one was open for 2% of the time, Pallas kernels for 8%

profile of v2, /device:TPU:192, one launch (start us, length us, event | category | flops | bytes accessed | tf_op | source)
XLA Modules:
  0.0 70.2 jit_solution(13761852626904851217)
XLA Ops:
  0.6 1.7 %copy-done = f32[3,6,8,32,128]{4,3,2,1,0:T(8,128)S(1)} copy-done((f32[3,6,8,32,128]{4,3,2,1,0:T(8,128)S(1)}, f32[3,6,8,32,128]{4,3,2,1,0:T(8,128)}, u32[]{:S(2)}) %copy-start) | copy-done | bytes 2359320
  2.3 1.1 %copy-done.2 = f32[6,8,32,128]{3,2,1,0:T(8,128)S(1)} copy-done((f32[6,8,32,128]{3,2,1,0:T(8,128)S(1)}, f32[6,8,32,128]{3,2,1,0:T(8,128)}, u32[]{:S(2)}) %copy-start.2) | copy-done | bytes 786456
  3.4 0.9 %copy-done.4 = f32[8,32,128]{2,1,0:T(8,128)S(1)} copy-done((f32[8,32,128]{2,1,0:T(8,128)S(1)}, f32[8,32,128]{2,1,0:T(8,128)}, u32[]{:S(2)}) %copy-start.4) | copy-done | bytes 131096
  4.3 0.9 %copy-done.6 = f32[8,32,128]{2,1,0:T(8,128)S(1)} copy-done((f32[8,32,128]{2,1,0:T(8,128)S(1)}, f32[8,32,128]{2,1,0:T(8,128)}, u32[]{:S(2)}) %copy-start.6) | copy-done | bytes 131096
  5.2 0.7 copy-done.8
  5.9 0.7 copy-done.10
  6.6 0.7 copy-done.12
  7.4 3.8 %shard_map.96 = (f32[8,32,128]{2,1,0:T(8,128)S(1)}, f32[2,32,128]{2,1,0:T(8,128)}, f32[2,32,128]{2,1,0:T(8,128)}) custom-call(f32[6,8,32,128]{3,2,1,0:T(8,128)S(1)} %copy-done.2, f32[8,32,128]{2,1,0:T(8,128)S(1)} %copy-done.4, f32[8,32,128]{2,1,0:T(8,128)S(1)} %copy-done.6, f32[3,6,8,32,128]{4,3,2,1,0:T(8,128)S(1)} %copy-done, s32[16,128]{1,0:T(8,128)S(1)} %bitcast.6, ...), custom_call_target="tpu_custom_call" | custom-call | flops 1000000 | bytes 1048576 | tf_op jit(solution)/shard_map/pallas_call | solution.py:478
  11.1 5.5 %collective-permute-start = (f32[2,32,128]{2,1,0:T(8,128)}, f32[2,32,128]{2,1,0:T(8,128)}, u32[]{:S(2)}, u32[]{:S(2)}) collective-permute-start(f32[2,32,128]{2,1,0:T(8,128)} %get-tuple-element.24), channel_id=1, source_target_pairs={{0,8},{8,16},{16,24},{24,32},{32,40},{40,48},{48,56},{56,64},{64,7... | collective-permute-start | bytes 98312 | tf_op jit(solution)/shard_map/ppermute | solution.py:467
  16.6 1.9 %collective-permute-start.1 = (f32[2,32,128]{2,1,0:T(8,128)}, f32[2,32,128]{2,1,0:T(8,128)}, u32[]{:S(2)}, u32[]{:S(2)}) collective-permute-start(f32[2,32,128]{2,1,0:T(8,128)} %get-tuple-element.25), channel_id=1, source_target_pairs={{8,0},{16,8},{24,16},{32,24},{40,32},{48,40},{56,48},{64,56},{72,6... | collective-permute-start | bytes 98312 | tf_op jit(solution)/shard_map/ppermute | solution.py:467
  18.6 1.3 %concatenate.3.idx.info = s32[12]{0:T(128)} concatenate(s32[1]{0:T(128)} %bitcast, s32[1]{0:T(128)} %bitcast.1, s32[1]{0:T(128)} %bitcast.2, s32[1]{0:T(128)} %constant.13.clone.1, s32[1]{0:T(128)} %constant.14.clone.1, s32[1]{0:T(128)} %constant.13.clone.1, s32[6]{0:T(128)} %param.15), dimensions={0} | concatenate | bytes 96 | tf_op jit(solution)/shard_map/concatenate | solution.py:462
  20.6 1.0 %shard_map.95.src = f32[2,40,128]{2,1,0:T(8,128)S(1)} custom-call(s32[12]{0:T(128)S(1)} %copy-done.14, s32[16,128]{1,0:T(8,128)S(1)} %bitcast.7, f32[16,128]{1,0:T(8,128)S(1)} %bitcast.9), custom_call_target="tpu_custom_call" | custom-call | flops 1000000 | bytes 1048576 | tf_op jit(solution)/shard_map/pallas_call | solution.py:486
  21.6 2.3 %collective-permute-done.1.from_right = f32[2,32,128]{2,1,0:T(8,128)} collective-permute-done((f32[2,32,128]{2,1,0:T(8,128)}, f32[2,32,128]{2,1,0:T(8,128)}, u32[]{:S(2)}, u32[]{:S(2)}) %collective-permute-start.1) | collective-permute-done | bytes 32800 | tf_op jit(solution)/shard_map/ppermute | solution.py:467
  24.0 1.0 %shard_map.97 = (f32[8,32,128]{2,1,0:T(8,128)S(1)}, f32[8,32,128]{2,1,0:T(8,128)S(1)}, f32[8,32,128]{2,1,0:T(8,128)S(1)}) custom-call(f32[2,40,128]{2,1,0:T(8,128)S(1)} %shard_map.95.src, f32[8,32,128]{2,1,0:T(8,128)S(1)} %get-tuple-element.23.own, f32[2,32,128]{2,1,0:T(8,128)} %collective-permute-done.from_left, ...), custom_call_target="tpu_custom_call" | custom-call | flops 1000000 | bytes 1048576 | tf_op jit(solution)/shard_map/pallas_call | solution.py:487
  25.0 3.4 %collective-permute-start.2 = (f32[8,32,128]{2,1,0:T(8,128)S(1)}, f32[8,32,128]{2,1,0:T(8,128)S(1)}, u32[]{:S(2)}, u32[]{:S(2)}) collective-permute-start(f32[8,32,128]{2,1,0:T(8,128)S(1)} %get-tuple-element.27), channel_id=1, source_target_pairs={{0,96},{96,192},{192,288},{288,384},{384,480},{480,576},{576,672},... | collective-permute-start | bytes 393224 | tf_op jit(solution)/shard_map/ppermute | solution.py:467
  28.4 1.3 %collective-permute-start.3 = (f32[8,32,128]{2,1,0:T(8,128)S(1)}, f32[8,32,128]{2,1,0:T(8,128)S(1)}, u32[]{:S(2)}, u32[]{:S(2)}) collective-permute-start(f32[8,32,128]{2,1,0:T(8,128)S(1)} %get-tuple-element.28), channel_id=1, source_target_pairs={{96,0},{192,96},{288,192},{384,288},{480,384},{576,480},{672,576},... | collective-permute-start | bytes 393224 | tf_op jit(solution)/shard_map/ppermute | solution.py:467
  29.7 1.2 %collective-permute-done.2.from_low = f32[8,32,128]{2,1,0:T(8,128)S(1)} collective-permute-done((f32[8,32,128]{2,1,0:T(8,128)S(1)}, f32[8,32,128]{2,1,0:T(8,128)S(1)}, u32[]{:S(2)}, u32[]{:S(2)}) %collective-permute-start.2) | collective-permute-done | bytes 131104 | tf_op jit(solution)/shard_map/ppermute | solution.py:467
  30.9 4.4 %collective-permute-done.3.from_high = f32[8,32,128]{2,1,0:T(8,128)S(1)} collective-permute-done((f32[8,32,128]{2,1,0:T(8,128)S(1)}, f32[8,32,128]{2,1,0:T(8,128)S(1)}, u32[]{:S(2)}, u32[]{:S(2)}) %collective-permute-start.3) | collective-permute-done | bytes 131104 | tf_op jit(solution)/shard_map/ppermute | solution.py:467
  35.3 0.7 %shard_map.98 = (f32[8,9,8,128]{3,2,1,0:T(8,128)S(1)}, f32[6,8,8,128]{3,2,1,0:T(8,128)S(1)}, f32[16,40,128]{2,1,0:T(8,128)S(1)}, f32[16,40,128]{2,1,0:T(8,128)S(1)}) custom-call(s32[12]{0:T(128)S(1)} %copy-done.14, f32[8,32,128]{2,1,0:T(8,128)S(1)} %get-tuple-element.26.strip, f32[8,32,128]{2,1,0:T(8,128)S(1)} %collective-permute-done.2.from_low, ...), custom_call_target="tpu_custom_call" | custom-call | flops 1000000 | bytes 1048576 | tf_op jit(solution)/shard_map/pallas_call | solution.py:492
  36.0 1.9 %collective-permute-start.4 = (f32[16,40,128]{2,1,0:T(8,128)S(1)}, f32[16,40,128]{2,1,0:T(8,128)S(1)}, u32[]{:S(2)}, u32[]{:S(2)}) collective-permute-start(f32[16,40,128]{2,1,0:T(8,128)S(1)} %get-tuple-element.30), channel_id=1, source_target_pairs={{0,1},{2,3},{4,5},{6,7},{1,0},{3,2},{5,4},{7,6},{8,9},{10,11},{12,... | collective-permute-start | bytes 983048 | tf_op jit(solution)/shard_map/ppermute | solution.py:472
  37.9 0.7 collective-permute-start.5
  38.6 4.5 %shard_map.99 = (f32[8,7,40,128]{3,2,1,0:T(8,128)S(1)}, f32[2,7,40,128]{3,2,1,0:T(8,128)S(1)}, f32[2,7,40,128]{3,2,1,0:T(8,128)S(1)}, f32[8,7,40,128]{3,2,1,0:T(...) custom-call(s32[12]{0:T(128)S(1)} %copy-done.14, ...), custom_call_target="tpu_custom_call" | custom-call | flops 1000000 | bytes 1048576 | tf_op jit(solution)/shard_map/pallas_call | solution.py:500
  43.1 2.9 %shard_map.100 = (f32[6,8,32,128]{3,2,1,0:T(8,128)}, f32[8,8,128]{2,1,0:T(8,128)S(1)}) custom-call(s32[12]{0:T(128)S(1)} %copy-done.14, f32[6,6]{1,0:T(8,128)S(1)} %copy-done.9, f32[8,32,128]{2,1,0:T(8,128)S(1)} %copy-done.5, f32[8,32,128]{2,1,0:T(8,128)S(1)} %get-tuple-element.26.strip, f32[8,9,8,128]{3,2,1,0:T(8,128)S(1)} %get-tuple-element.29.halo.halo_rows, ...), custom_call_target="tpu_custom_call" | custom-call | flops 1000000 | bytes 1048576 | tf_op jit(solution)/shard_map/pallas_call | solution.py:516
  46.0 23.5 %all_to_all.5.parts = f32[8,8,128]{2,1,0:T(8,128)S(1)} all-to-all(f32[8,8,128]{2,1,0:T(8,128)S(1)} %get-tuple-element.43), channel_id=1, replica_groups=mesh['gx'=8,'gy'=12,'gz'=8] {'gz'}, dimensions={0} | all-to-all | bytes 65536 | tf_op jit(solution)/shard_map/all_to_all | solution.py:522
  (27 shorter events, 1.4 us)
Async XLA Ops:
  0.6 1.7 %copy-start = (f32[3,6,8,32,128]{4,3,2,1,0:T(8,128)S(1)}, f32[3,6,8,32,128]{4,3,2,1,0:T(8,128)}, u32[]{:S(2)}) copy-start(f32[3,6,8,32,128]{4,3,2,1,0:T(8,128)} %metric.7) | copy-start | bytes 7077892
  2.3 1.1 %copy-start.2 = (f32[6,8,32,128]{3,2,1,0:T(8,128)S(1)}, f32[6,8,32,128]{3,2,1,0:T(8,128)}, u32[]{:S(2)}) copy-start(f32[6,8,32,128]{3,2,1,0:T(8,128)} %adj.7) | copy-start | bytes 2359300
  3.4 0.9 %copy-start.4 = (f32[8,32,128]{2,1,0:T(8,128)S(1)}, f32[8,32,128]{2,1,0:T(8,128)}, u32[]{:S(2)}) copy-start(f32[8,32,128]{2,1,0:T(8,128)} %eddy.9) | copy-start | bytes 393220
  4.3 0.9 %copy-start.6 = (f32[8,32,128]{2,1,0:T(8,128)S(1)}, f32[8,32,128]{2,1,0:T(8,128)}, u32[]{:S(2)}) copy-start(f32[8,32,128]{2,1,0:T(8,128)} %diag.7) | copy-start | bytes 393220
  5.2 0.7 copy-start.8
  5.9 0.7 copy-start.10
  6.6 0.7 copy-start.12
  7.3 12.6 %copy-start.11 = (s32[2048]{0:T(1024)S(1)}, s32[2048]{0:T(1024)}, u32[]{:S(2)}) copy-start(s32[2048]{0:T(1024)} %param.13) | copy-start | bytes 24580
  7.3 12.6 %copy-start.13 = (f32[2048]{0:T(1024)S(1)}, f32[2048]{0:T(1024)}, u32[]{:S(2)}) copy-start(f32[2048]{0:T(1024)} %param.14) | copy-start | bytes 24580
  7.3 16.6 %copy-start.1 = (f32[3,6,8,32,128]{4,3,2,1,0:T(8,128)S(1)}, f32[3,6,8,32,128]{4,3,2,1,0:T(8,128)}, u32[]{:S(2)}) copy-start(f32[3,6,8,32,128]{4,3,2,1,0:T(8,128)} %metric.7) | copy-start | bytes 7077892
  7.3 16.6 %copy-start.3 = (f32[6,8,32,128]{3,2,1,0:T(8,128)S(1)}, f32[6,8,32,128]{3,2,1,0:T(8,128)}, u32[]{:S(2)}) copy-start(f32[6,8,32,128]{3,2,1,0:T(8,128)} %adj.7) | copy-start | bytes 2359300
  7.3 16.6 %copy-start.5 = (f32[8,32,128]{2,1,0:T(8,128)S(1)}, f32[8,32,128]{2,1,0:T(8,128)}, u32[]{:S(2)}) copy-start(f32[8,32,128]{2,1,0:T(8,128)} %eddy.9) | copy-start | bytes 393220
  7.3 16.6 %copy-start.7 = (f32[8,32,128]{2,1,0:T(8,128)S(1)}, f32[8,32,128]{2,1,0:T(8,128)}, u32[]{:S(2)}) copy-start(f32[8,32,128]{2,1,0:T(8,128)} %diag.7) | copy-start | bytes 393220
  11.1 10.5 %collective-permute-start = (f32[2,32,128]{2,1,0:T(8,128)}, f32[2,32,128]{2,1,0:T(8,128)}, u32[]{:S(2)}, u32[]{:S(2)}) collective-permute-start(f32[2,32,128]{2,1,0:T(8,128)} %get-tuple-element.24), channel_id=1, source_target_pairs={{0,8},{8,16},{16,24},{24,32},{32,40},{40,48},{48,56},{56,64},{64,7... | collective-permute-start | bytes 98312 | tf_op jit(solution)/shard_map/ppermute | solution.py:467
  16.6 7.3 %collective-permute-start.1 = (f32[2,32,128]{2,1,0:T(8,128)}, f32[2,32,128]{2,1,0:T(8,128)}, u32[]{:S(2)}, u32[]{:S(2)}) collective-permute-start(f32[2,32,128]{2,1,0:T(8,128)} %get-tuple-element.25), channel_id=1, source_target_pairs={{8,0},{16,8},{24,16},{32,24},{40,32},{48,40},{56,48},{64,56},{72,6... | collective-permute-start | bytes 98312 | tf_op jit(solution)/shard_map/ppermute | solution.py:467
  19.9 0.7 copy-start.14
  25.0 13.6 %copy-start.9 = (f32[6,6]{1,0:T(8,128)S(1)}, f32[6,6]{1,0:T(8,128)}, u32[]{:S(2)}) copy-start(f32[6,6]{1,0:T(8,128)} %coup.3) | copy-start | bytes 436
  25.0 5.9 %collective-permute-start.2 = (f32[8,32,128]{2,1,0:T(8,128)S(1)}, f32[8,32,128]{2,1,0:T(8,128)S(1)}, u32[]{:S(2)}, u32[]{:S(2)}) collective-permute-start(f32[8,32,128]{2,1,0:T(8,128)S(1)} %get-tuple-element.27), channel_id=1, source_target_pairs={{0,96},{96,192},{192,288},{288,384},{384,480},{480,576},{576,672},... | collective-permute-start | bytes 393224 | tf_op jit(solution)/shard_map/ppermute | solution.py:467
  28.4 6.9 %collective-permute-start.3 = (f32[8,32,128]{2,1,0:T(8,128)S(1)}, f32[8,32,128]{2,1,0:T(8,128)S(1)}, u32[]{:S(2)}, u32[]{:S(2)}) collective-permute-start(f32[8,32,128]{2,1,0:T(8,128)S(1)} %get-tuple-element.28), channel_id=1, source_target_pairs={{96,0},{192,96},{288,192},{384,288},{480,384},{576,480},{672,576},... | collective-permute-start | bytes 393224 | tf_op jit(solution)/shard_map/ppermute | solution.py:467
  36.0 7.2 %collective-permute-start.4 = (f32[16,40,128]{2,1,0:T(8,128)S(1)}, f32[16,40,128]{2,1,0:T(8,128)S(1)}, u32[]{:S(2)}, u32[]{:S(2)}) collective-permute-start(f32[16,40,128]{2,1,0:T(8,128)S(1)} %get-tuple-element.30), channel_id=1, source_target_pairs={{0,1},{2,3},{4,5},{6,7},{1,0},{3,2},{5,4},{7,6},{8,9},{10,11},{12,... | collective-permute-start | bytes 983048 | tf_op jit(solution)/shard_map/ppermute | solution.py:472
  37.9 5.2 %collective-permute-start.5 = (f32[16,40,128]{2,1,0:T(8,128)S(1)}, f32[16,40,128]{2,1,0:T(8,128)S(1)}, u32[]{:S(2)}, u32[]{:S(2)}) collective-permute-start(f32[16,40,128]{2,1,0:T(8,128)S(1)} %get-tuple-element.31), channel_id=1, source_target_pairs={{1,2},{3,4},{5,6},{2,1},{4,3},{6,5},{9,10},{11,12},{13,14},{10,9},... | collective-permute-start | bytes 983048 | tf_op jit(solution)/shard_map/ppermute | solution.py:472

commit v3 on v2

--- a/solution.py
+++ b/solution.py
@@ -20,8 +20,6 @@
 
 VM = pl.BlockSpec(memory_space=pltpu.VMEM)
 SM = pl.BlockSpec(memory_space=pltpu.SMEM)
-HB = pl.BlockSpec(memory_space=pltpu.HBM)
-PARAMS = pltpu.CompilerParams(vmem_limit_bytes=16 * 1024 * 1024)
 
 
 def roll(v, shift, axis):
@@ -36,29 +34,13 @@
     return jax.ShapeDtypeStruct(shape, jnp.float32)
 
 
-def pack_y(adj, eddy, diag, metric, *rest):
-    own, to_right, to_left, adj_buf, eddy_buf, diag_buf, metric_buf, sems = rest[-8:]
-    half = LEV // 2
-    copies = []
-    for h in range(2):
-        at = pl.ds(h * half, half)
-        pairs = (
-            (adj.at[:, at], adj_buf.at[:, at]),
-            (eddy.at[at], eddy_buf.at[at]),
-            (diag.at[at], diag_buf.at[at]),
-            (metric.at[2, :, at], metric_buf.at[:, at]),
-        )
-        copies.append([pltpu.make_async_copy(a, b, sems.at[h, i]) for i, (a, b) in enumerate(pairs)])
-    for c in copies[0] + copies[1]:
-        c.start()
+def pack_y(adj, eddy, diag, metric, own, to_right, to_left):
     lane = iota((8, COLS), 1)
     slot, j = lane // SLOT, lane % SLOT
     quad, jj = j // 4, j % 4
     edge_at = [(slot == p) & (j >= 1) & (j <= 6) for p in range(8)]
     metric_at = [(slot == p) & (j >= 8) & (j <= 9) for p in range(FIELDS)]
     for zg in range(2):
-        for c in copies[zg]:
-            c.wait()
         for t in range(ROWS // 8):
             rows = pl.ds(8 * t, 8)
             right = left = jnp.zeros((8, COLS), jnp.float32)
@@ -67,14 +49,14 @@
                 c = jnp.zeros((8, COLS), jnp.float32)
                 for p in range(8):
                     if p < FIELDS:
-                        v = adj_buf[p, z, rows, :]
+                        v = adj[p, z, rows, :]
                     elif p == EDDY:
-                        v = eddy_buf[z, rows, :]
+                        v = eddy[z, rows, :]
                     else:
-                        v = relax_rate / diag_buf[z, rows, :]
+                        v = relax_rate / diag[z, rows, :]
                     c = jnp.where(edge_at[p], roll(v, SLOT * p + 4, 1), c)
                     if p < FIELDS:
-                        c = jnp.where(metric_at[p], roll(metric_buf[p, z, rows, :], SLOT * p + 9, 1), c)
+                        c = jnp.where(metric_at[p], roll(metric[0, p, z, rows, :], SLOT * p + 9, 1), c)
                 own[z, rows, :] = jnp.where(j < 8, c, jnp.where(j >= 9, roll(c, 8, 1), 0.0))
                 at = 4 * zq
                 here = quad == zq
@@ -84,7 +66,21 @@
             to_left[zg, rows, :] = left
 
 
-def make_source(total_y, idx, cells, weights, src):
+MIX, PAIR = 8, 16
+
+
+def make_source(total_y, idx, codes, coup, cells, weights, src, table):
+    slot = iota((1, COLS), 1) // SLOT
+    for i in range(6):
+        factor = jnp.where(codes[i] == 1, 1.0, jnp.where(codes[i] == 2, -1.0, 0.0)).astype(jnp.float32)
+        table[i : i + 1, :] = jnp.full((1, COLS), factor)
+    for e in range(FIELDS):
+        v = jnp.zeros((1, COLS), jnp.float32)
+        for f in range(FIELDS):
+            v = jnp.where(slot == f, coup[e, f], v)
+            at = PAIR + FIELDS * e + f
+            table[at : at + 1, :] = jnp.full((1, COLS), coup[e, f])
+        table[MIX + e : MIX + e + 1, :] = v
     start_x, start_y = idx[0] * ROWS, idx[1] * COLS
     r = iota((48, COLS), 0)
     row_x = jnp.where(r < EXT - 5, r, r - EXT) + start_x
@@ -146,16 +142,12 @@
     return jnp.take_along_axis(v, iota(v.shape, 1) % SLOT + SLOT * plane, axis=1)
 
 
-def face(codes, i):
-    return jnp.where(codes[i] == 1, 1.0, jnp.where(codes[i] == 2, -1.0, 0.0)).astype(jnp.float32)
-
-
 class Edges:
-    def __init__(self, info):
+    def __init__(self, info, table):
         self.low_x, self.high_x = info[0] == 0, info[0] == info[3] - 1
         self.low_y, self.high_y = info[1] == 0, info[1] == info[4] - 1
         self.low_z, self.high_z = info[2] == 0, info[2] == info[5] - 1
-        self.factors = [face(info, 6 + i) for i in range(6)]
+        self.factors = [table[i : i + 1, :] for i in range(6)]
         row, j = iota((8, COLS), 0), iota((EXT, COLS), 1) % SLOT
         self.row_low, self.row_high = (row == 7) & self.low_x, (row == 0) & self.high_x
         self.j = j
@@ -169,17 +161,13 @@
         return jnp.concatenate([v[0:32], t4], 0)
 
 
-def put_coupling(coup, mix):
-    slot = iota((1, COLS), 1) // SLOT
-    for e in range(FIELDS):
-        v = jnp.zeros((1, COLS), jnp.float32)
-        for f in range(FIELDS):
-            v = jnp.where(slot == f, coup[e, f], v)
-        mix[e : e + 1, :] = v
-
-
-def sweep(edges, center, vertical, value, rate, strip_rate, coup, mix, store, src=None, flag=None):
+def sweep(edges, center, vertical, value, rate, strip_rate, table, store, src=None, flag=None):
     lane = iota((EXT, COLS), 1)
+
+    def pair(e, f):
+        at = PAIR + FIELDS * e + f
+        return table[at : at + 1, :]
+
     f2, f3 = edges.factors[2], edges.factors[3]
     v = center(FIELDS)
     up, down = roll(v, 1, 1), roll(v, -1, 1)
@@ -188,9 +176,9 @@
     beside = vertical(FIELDS) + roll(v, -1, 0) + roll(v, 1, 0)
     beside = beside + jnp.where(edges.own_low, f2 * v, up) + jnp.where(edges.own_high, f3 * v, down)
     a = value(FIELDS)
-    coupled = lanes_of(a, 0) * mix[0:1, :]
+    coupled = lanes_of(a, 0) * table[MIX : MIX + 1, :]
     for e in range(1, FIELDS):
-        coupled = coupled + lanes_of(a, e) * mix[e : e + 1, :]
+        coupled = coupled + lanes_of(a, e) * table[MIX + e : MIX + e + 1, :]
     rest = beside - coupled
     if src is not None:
         rest = rest + flag * src[1]
@@ -201,9 +189,9 @@
         left = jnp.where(lane == 0, end, roll(v, 1, 1))
         right = jnp.where(lane == COLS - 1, end, roll(v, -1, 1))
         beside = vertical(f) + roll(v, -1, 0) + roll(v, 1, 0) + right + left
-        coupled = coup[0, f] * value(0)
+        coupled = pair(0, f) * value(0)
         for e in range(1, FIELDS):
-            coupled = coupled + coup[e, f] * value(e)
+            coupled = coupled + pair(e, f) * value(e)
         rest = beside - coupled
         if f == 0 and src is not None:
             rest = rest + flag * src[0]
@@ -230,43 +218,45 @@
     sums[3, :ROWS] += w * (m * edge_strip[:ROWS])
 
 
-def pack_z(info, strip, from_low, from_high, adj, eddy, diag, halo, metric_row, msg_a, msg_b):
+def halo_tile(from_low, from_high, z, p):
+    at = 2 if p == RATE else 3
+    start = LOW_AT[p] - (8 - at)
+    above, below = from_high[z, pl.ds(HIGH_AT[p], 8), :], from_low[z, pl.ds(start, 8), :]
+    return jnp.where(iota((8, COLS), 0) < 4, above, below)
+
+
+def pack_z(far, info, table, strip, from_low, from_high, adj, eddy, diag, msg):
+    edges = Edges(info, table)
+    top = (info[2] % 2 == 0) != far
+
+    def plane(z, p):
+        own = adj[p, z] if p < FIELDS else eddy[z] if p == EDDY else relax_rate / diag[z] if p == RATE else strip[z]
+        return jnp.concatenate([own, halo_tile(from_low, from_high, z, p)], 0)
+
+    near = jnp.where(top, LEV - 1, 0)
+    next_ = jnp.where(top, LEV - 2, 1)
+    for p in range(9):
+        msg[p] = plane(near, p)
+    e = plane(next_, EDDY)
+    for f in range(FIELDS):
+        msg[9 + f] = edges.flux(plane(next_, f) * e)
+    s = plane(next_, STRIP)
+    msg[15] = edges.flux(s * lanes_of(s, EDDY))
+
+
+def inner_levels(
+    info, table, adj, eddy, diag, strip, from_low, from_high, metric, src,
+    f0, near1, next2, f1, rates, edge_eddy, edge_rate, out, sums, halo, metric_row, a1, a2,
+):
+    edges = Edges(info, table)
     row = iota((8, COLS), 0)
     for z in range(LEV):
         for p in range(9):
-            at = 2 if p == RATE else 3
-            above = from_high[z, HIGH_AT[p] : HIGH_AT[p] + 8, :]
-            start = LOW_AT[p] - (8 - at)
-            halo[z, p] = jnp.where(row < 4, above, from_low[z, start : start + 8, :])
+            halo[z, p] = halo_tile(from_low, from_high, z, p)
         for f in range(FIELDS):
             above = jnp.broadcast_to(from_high[z, HIGH_METRIC + f : HIGH_METRIC + f + 1, :], (8, COLS))
             below = jnp.broadcast_to(from_low[z, LOW_METRIC + f : LOW_METRIC + f + 1, :], (8, COLS))
             metric_row[f, z] = jnp.where(row < 4, above, below)
-    edges = Edges(info)
-    even = info[2] % 2 == 0
-
-    def plane(z, p):
-        own = adj[p, z] if p < FIELDS else eddy[z] if p == EDDY else relax_rate / diag[z] if p == RATE else strip[z]
-        return jnp.concatenate([own, halo[z, p]], 0)
-
-    for msg, top in ((msg_a, even), (msg_b, jnp.logical_not(even))):
-        near = jnp.where(top, LEV - 1, 0)
-        next_ = jnp.where(top, LEV - 2, 1)
-        for p in range(9):
-            msg[p] = plane(near, p)
-        e = plane(next_, EDDY)
-        for f in range(FIELDS):
-            msg[9 + f] = edges.flux(plane(next_, f) * e)
-        s = plane(next_, STRIP)
-        msg[15] = edges.flux(s * lanes_of(s, EDDY))
-
-
-def inner_levels(
-    info, coup, adj, eddy, diag, strip, halo, metric, metric_row, src,
-    f0, near1, next2, f1, rates, edge_eddy, edge_rate, out, sums, mix, a1, a2,
-):
-    edges = Edges(info)
-    put_coupling(coup, mix)
     hub = info[5] * LEV // 4 - info[2] * LEV
     flag = jnp.where(hub == 0, 1.0, 0.0).astype(jnp.float32)
 
@@ -291,7 +281,7 @@
         return lambda p: array[z - 1, p] + array[z + 1, p]
 
     def first(z, vertical, store, **more):
-        sweep(edges, lambda p: f0[z, p], vertical, lambda p: value(z, p), rates[z], edge_rate[z], coup, mix, store, **more)
+        sweep(edges, lambda p: f0[z, p], vertical, lambda p: value(z, p), rates[z], edge_rate[z], table, store, **more)
 
     def store_near(i):
         def store(p, v):
@@ -313,7 +303,7 @@
     sums[...] = jnp.zeros_like(sums)
 
     def second(z, vertical, store):
-        sweep(edges, lambda p: f1[z, p], vertical, lambda p: a1[z, p], rates[z], edge_rate[z], coup, mix, store)
+        sweep(edges, lambda p: f1[z, p], vertical, lambda p: a1[z, p], rates[z], edge_rate[z], table, store)
 
     def store_next(i):
         def store(p, v):
@@ -335,13 +325,12 @@
 
 
 def outer_levels(
-    info, coup, eddy, strip, halo_rows, from_a, from_b, metric, metric_row, src,
-    f0, near1, next2, f1, rates, edge_eddy, edge_rate, inner_out, inner_sums,
-    out, share, sums, mix, fh, ah, gh, an, gn, a2,
+    info, table, eddy, strip, from_b, from_a, metric, src,
+    f0, near1, next2, f1, rates, edge_eddy, edge_rate, inner_out, inner_sums, halo_rows, metric_row,
+    out, share, sums, fh, gh, an, gn, a2,
 ):
-    edges = Edges(info)
+    edges = Edges(info, table)
     hub = info[5] * LEV // 4 - info[2] * LEV
-    put_coupling(coup, mix)
     sums[...] = inner_sums[...]
     for f in range(FIELDS):
         for z in range(2, LEV - 2):
@@ -383,8 +372,7 @@
             lambda p: msg[STRIP if p == FIELDS else p],
             msg[RATE],
             lanes_of(s, RATE),
-            coup,
-            mix,
+            table,
             store_over,
             src,
             flag_of(over),
@@ -406,8 +394,7 @@
             lambda p: an[n, p],
             rates[near],
             edge_rate[near],
-            coup,
-            mix,
+            table,
             store_last,
             src,
             flag_of(near),
@@ -443,23 +430,22 @@
         out[8 * q : 8 * q + 8, :] = roll(total, -ROWS * q, 1)[:, :ROWS]
 
 
-def call(body, outs, ins, scratch=(), flops=1000000):
+def call(body, outs, ins, scratch=()):
     return pl.pallas_call(
         body,
         out_shape=outs,
         in_specs=ins,
         out_specs=jax.tree.map(lambda _: VM, outs),
         scratch_shapes=list(scratch),
-        compiler_params=PARAMS,
-        cost_estimate=pl.CostEstimate(flops=flops, bytes_accessed=1 << 20, transcendentals=0),
+        compiler_params=pltpu.CompilerParams(vmem_limit_bytes=16 << 20),
+        cost_estimate=pl.CostEstimate(flops=1000000, bytes_accessed=1 << 20, transcendentals=0),
     )
 
 
 def local(adjoint_start, eddy_visc, diag_coef, coupling, metric_terms, sample_cells, sample_weights, face_codes):
     index = [lax.axis_index(a) for a in ("gx", "gy", "gz")]
     count = [lax.axis_size(a) for a in ("gx", "gy", "gz")]
-    place = jnp.stack(index + [jnp.int32(c) for c in count]).astype(jnp.int32)
-    info = jnp.concatenate([place, face_codes])
+    info = jnp.stack(index + [jnp.int32(c) for c in count]).astype(jnp.int32)
     cells, weights = sample_cells.reshape(16, 128), sample_weights.reshape(16, 128)
 
     def shift(v, axis, step):
@@ -478,26 +464,27 @@
     own, to_right, to_left = call(
         pack_y,
         (f32(*level), f32(2, ROWS, COLS), f32(2, ROWS, COLS)),
-        [HB] * 4 + [VM, VM, SM],
-        [buf(FIELDS, *level), buf(*level), buf(*level), buf(FIELDS, *level), pltpu.SemaphoreType.DMA((2, 4))],
-    )(adjoint_start, eddy_visc, diag_coef, metric_terms, cells, weights, coupling)
+        [VM] * 4,
+    )(adjoint_start, eddy_visc, diag_coef, metric_terms[2:3])
     from_left = shift(to_right, "gy", 1)
     from_right = shift(to_left, "gy", -1)
-    src = call(functools.partial(make_source, COLS * count[1]), f32(2, EXT, COLS), [SM, VM, VM])(info, cells, weights)
+    src, table = call(
+        functools.partial(make_source, COLS * count[1]), (f32(2, EXT, COLS), f32(56, COLS)), [SM] * 3 + [VM] * 2
+    )(info, face_codes, coupling, cells, weights)
     strip, to_low, to_high = call(pack_x, (f32(*level),) * 3, [VM] * 8)(
         src, own, from_left, from_right, adjoint_start, eddy_visc, diag_coef, metric_terms
     )
     from_low = shift(to_high, "gx", 1)
     from_high = shift(to_low, "gx", -1)
-    halo, metric_row, msg_a, msg_b = call(
-        pack_z,
-        (f32(LEV, 9, 8, COLS), f32(FIELDS, LEV, 8, COLS), f32(16, EXT, COLS), f32(16, EXT, COLS)),
-        [SM] + [VM] * 6,
-    )(info, strip, from_low, from_high, adjoint_start, eddy_visc, diag_coef)
+    received = (from_low, from_high, adjoint_start, eddy_visc, diag_coef)
+    msg_b, msg_a = [
+        call(functools.partial(pack_z, far), f32(16, EXT, COLS), [SM] + [VM] * 7)(info, table, strip, *received)
+        for far in (True, False)
+    ]
     from_b = trade(msg_b, "gz", 1)
     from_a = trade(msg_a, "gz", 0)
     ext = (EXT, COLS)
-    *inner, inner_out, inner_sums = call(
+    inner = call(
         inner_levels,
         (
             f32(LEV, 7, *ext),
@@ -509,16 +496,18 @@
             f32(LEV, *ext),
             f32(FIELDS, LEV - 4, ROWS, COLS),
             f32(4, *ext),
+            f32(LEV, 9, 8, COLS),
+            f32(FIELDS, LEV, 8, COLS),
         ),
-        [SM, SM] + [VM] * 8,
-        [buf(8, COLS), buf(LEV, 7, *ext), buf(LEV, 7, *ext)],
-    )(info, coupling, adjoint_start, eddy_visc, diag_coef, strip, halo, metric_terms, metric_row, src)
+        [SM] + [VM] * 9,
+        [buf(LEV, 7, *ext), buf(LEV, 7, *ext)],
+    )(info, table, adjoint_start, eddy_visc, diag_coef, strip, from_low, from_high, metric_terms, src)
     adjoint, share = call(
         outer_levels,
         (f32(FIELDS, *level), f32(count[2], 8, COLS)),
-        [SM, SM] + [VM] * 17,
-        [buf(4, *ext), buf(8, COLS)] + [buf(2, 7, *ext)] * 6,
-    )(info, coupling, eddy_visc, strip, halo, from_a, from_b, metric_terms, metric_row, src, *inner, inner_out, inner_sums)
+        [SM] + [VM] * 18,
+        [buf(4, *ext)] + [buf(2, 7, *ext)] * 5,
+    )(info, table, eddy_visc, strip, from_b, from_a, metric_terms, src, *inner)
     parts = lax.all_to_all(share, "gz", 0, 0, tiled=True)
     height_grad = call(add_shares, f32(COLS // count[2], ROWS), [VM])(parts).T
     return (adjoint, height_grad)

time: 70.8 us -> 62.5 us (0.88)
  blocking collectives: 23.5 us -> 16.8 us
  local copies, waits for them, and re-layouts: 8.7 us -> 2.9 us
  starting transfers between devices: 14.7 us -> 18.6 us
    all_to_all x1, blocking collectives: 23.5 us -> 16.8 us  [local(): parts = lax.all_to_all(share, 'gz', 0, 0, tiled=True)]
    unnamed x30 -> x16, local copies, waits for them, and re-layouts: 7.38 us -> 1.46 us
    ppermute x2, starting transfers between devices: 2.6 us -> 6.5 us  [trade(): return lax.ppermute(v, axis, pairs + [(b, a) for a, b in pairs])]
    slice x0 -> x1, local copies, waits for them, and re-layouts: none -> 1.36 us  [local(): metric_terms[2:3]]
    concatenate x1 -> x0, local copies, waits for them, and re-layouts: 1.32 us -> none  [local(): info = jnp.concatenate([place, face_codes])]
    pallas_call x4 -> x5, Pallas kernels: 8.41 us -> 8.26 us  [the longest x1 2.93 us: local(): call(pack_y, (f32(*level), f32(2, ROWS, COLS), f32(2, ROWS, COLS)), [VM]...]
  transfers between devices with their start and end apart: 6 -> 6, of which waited for: 3 -> 3; matrix products, arithmetic and copies ran while one was open for 2% -> 0% of each run, Pallas kernels for 8% -> 10%
where the time goes in v3:
time: 62.5 us; the launch traced here: 62.1 us
  starting transfers between devices  18.6 us (30%)
  blocking collectives  16.8 us (27%)
  Pallas kernels  14.6 us (23%)
  waiting for transfers between devices  8.38 us (13%)
  local copies, waits for them, and re-layouts  2.9 us (5%)
  between operations  0.81 us (1%)
    all_to_all x1, blocking collectives, local(): parts = lax.all_to_all(share, 'gz', 0, 0, tiled=True)  16.8 us
    ppermute x4, starting transfers between devices, shift(): lax.ppermute(v, axis, [(i, i + step) for i in range(n) if 0 <= i + step <...  12.1 us
    ppermute x4, waiting for transfers between devices, shift(): lax.ppermute(v, axis, [(i, i + step) for i in range(n) if 0 <= i + step <...  8.38 us
    ppermute x2, starting transfers between devices, trade(): return lax.ppermute(v, axis, pairs + [(b, a) for a, b in pairs])  6.5 us
    pallas_call x1, Pallas kernels, local(): call(inner_levels, (f32(LEV, 7, *ext), f32(2, 7, *ext), f32(2, 7, *ext),...  4.72 us
    pallas_call x1, Pallas kernels, local(): call(pack_y, (f32(*level), f32(2, ROWS, COLS), f32(2, ROWS, COLS)), [VM]...  2.93 us
    pallas_call x1, Pallas kernels, local(): call(outer_levels, (f32(FIELDS, *level), f32(count[2], 8, COLS)), [SM] +...  2.9 us
    unnamed x16, local copies, waits for them, and re-layouts  1.46 us
  transfers between devices with their start and end apart: 6, of which 3 were waited for; matrix products, arithmetic and copies ran while one was open for 0% of the time, Pallas kernels for 10%

profile of v3, /device:TPU:192, one launch (start us, length us, event | category | flops | bytes accessed | tf_op | source)
XLA Modules:
  0.0 62.1 jit_solution(16154169242870949249)
XLA Ops:
  0.7 1.4 %slice.3.metric = f32[1,6,8,32,128]{4,3,2,1,0:T(8,128)S(1)} slice(f32[3,6,8,32,128]{4,3,2,1,0:T(8,128)} %metric.5), slice={[2:3], [0:6], [0:8], [0:32], [0:128]} | slice | bytes 1572864 | tf_op jit(solution)/shard_map/slice | solution.py:468
  2.1 0.1 copy-done.1
  2.1 2.9 %shard_map.96 = (f32[8,32,128]{2,1,0:T(8,128)S(1)}, f32[2,32,128]{2,1,0:T(8,128)}, f32[2,32,128]{2,1,0:T(8,128)}) custom-call(f32[6,8,32,128]{3,2,1,0:T(8,128)S(1)} %copy-done.1, f32[8,32,128]{2,1,0:T(8,128)S(1)} %copy-done.2, f32[8,32,128]{2,1,0:T(8,128)S(1)} %copy-done.3, f32[1,6,8,32,128]{4,3,2,1,0:T(8,128)S(1)} %slice.3.metric), custom_call_target="tpu_custom_call" | custom-call | flops 1000000 | bytes 1048576 | tf_op jit(solution)/shard_map/pallas_call | solution.py:464
  5.1 5.5 %collective-permute-start = (f32[2,32,128]{2,1,0:T(8,128)}, f32[2,32,128]{2,1,0:T(8,128)}, u32[]{:S(2)}, u32[]{:S(2)}) collective-permute-start(f32[2,32,128]{2,1,0:T(8,128)} %get-tuple-element.26), channel_id=1, source_target_pairs={{0,8},{8,16},{16,24},{24,32},{32,40},{40,48},{48,56},{56,64},{64,7... | collective-permute-start | bytes 98312 | tf_op jit(solution)/shard_map/ppermute | solution.py:453
  10.6 1.9 %collective-permute-start.1 = (f32[2,32,128]{2,1,0:T(8,128)}, f32[2,32,128]{2,1,0:T(8,128)}, u32[]{:S(2)}, u32[]{:S(2)}) collective-permute-start(f32[2,32,128]{2,1,0:T(8,128)} %get-tuple-element.27), channel_id=1, source_target_pairs={{8,0},{16,8},{24,16},{32,24},{40,32},{48,40},{56,48},{64,56},{72,6... | collective-permute-start | bytes 98312 | tf_op jit(solution)/shard_map/ppermute | solution.py:453
  12.5 0.1 stack.15.idx.info
  12.6 0.0 copy-start.5
  12.6 0.7 %copy-done.5 = f32[2048]{0:T(1024)S(1)} copy-done((f32[2048]{0:T(1024)S(1)}, f32[2048]{0:T(1024)}, u32[]{:S(2)}) %copy-start.5) | copy-done | bytes 8216
  13.3 0.7 %copy-done.7 = s32[6]{0:T(128)S(1)} copy-done((s32[6]{0:T(128)S(1)}, s32[6]{0:T(128)}, u32[]{:S(2)}) %copy-start.7) | copy-done | bytes 48
  14.0 1.1 %shard_map.95 = (f32[2,40,128]{2,1,0:T(8,128)S(1)}, f32[56,128]{1,0:T(8,128)S(1)}) custom-call(s32[6]{0:T(128)S(1)} %stack.15.idx.info, s32[6]{0:T(128)S(1)} %copy-done.7, f32[6,6]{1,0:T(8,128)S(1)} %copy-done.6, s32[16,128]{1,0:T(8,128)S(1)} %bitcast.6, f32[16,128]{1,0:T(8,128)S(1)} %bitcast.7), custom_call_target="tpu_custom_call" | custom-call | flops 1000000 | bytes 1048576 | tf_op jit(solution)/shard_map/pallas_call | solution.py:471
  15.1 2.8 %collective-permute-done.1.from_right = f32[2,32,128]{2,1,0:T(8,128)} collective-permute-done((f32[2,32,128]{2,1,0:T(8,128)}, f32[2,32,128]{2,1,0:T(8,128)}, u32[]{:S(2)}, u32[]{:S(2)}) %collective-permute-start.1) | collective-permute-done | bytes 32800 | tf_op jit(solution)/shard_map/ppermute | solution.py:453
  17.9 1.0 %shard_map.97 = (f32[8,32,128]{2,1,0:T(8,128)S(1)}, f32[8,32,128]{2,1,0:T(8,128)S(1)}, f32[8,32,128]{2,1,0:T(8,128)S(1)}) custom-call(f32[2,40,128]{2,1,0:T(8,128)S(1)} %get-tuple-element.24.src, f32[8,32,128]{2,1,0:T(8,128)S(1)} %get-tuple-element.25.own, f32[2,32,128]{2,1,0:T(8,128)} %collective-permute-done.from_left, ...), custom_call_target="tpu_custom_call" | custom-call | flops 1000000 | bytes 1048576 | tf_op jit(solution)/shard_map/pallas_call | solution.py:474
  18.9 3.4 %collective-permute-start.2 = (f32[8,32,128]{2,1,0:T(8,128)S(1)}, f32[8,32,128]{2,1,0:T(8,128)S(1)}, u32[]{:S(2)}, u32[]{:S(2)}) collective-permute-start(f32[8,32,128]{2,1,0:T(8,128)S(1)} %get-tuple-element.29), channel_id=1, source_target_pairs={{0,96},{96,192},{192,288},{288,384},{384,480},{480,576},{576,672},... | collective-permute-start | bytes 393224 | tf_op jit(solution)/shard_map/ppermute | solution.py:453
  22.3 1.3 %collective-permute-start.3 = (f32[8,32,128]{2,1,0:T(8,128)S(1)}, f32[8,32,128]{2,1,0:T(8,128)S(1)}, u32[]{:S(2)}, u32[]{:S(2)}) collective-permute-start(f32[8,32,128]{2,1,0:T(8,128)S(1)} %get-tuple-element.30), channel_id=1, source_target_pairs={{96,0},{192,96},{288,192},{384,288},{480,384},{576,480},{672,576},... | collective-permute-start | bytes 393224 | tf_op jit(solution)/shard_map/ppermute | solution.py:453
  23.6 1.2 %collective-permute-done.2.from_low = f32[8,32,128]{2,1,0:T(8,128)S(1)} collective-permute-done((f32[8,32,128]{2,1,0:T(8,128)S(1)}, f32[8,32,128]{2,1,0:T(8,128)S(1)}, u32[]{:S(2)}, u32[]{:S(2)}) %collective-permute-start.2) | collective-permute-done | bytes 131104 | tf_op jit(solution)/shard_map/ppermute | solution.py:453
  24.8 4.4 %collective-permute-done.3.from_high = f32[8,32,128]{2,1,0:T(8,128)S(1)} collective-permute-done((f32[8,32,128]{2,1,0:T(8,128)S(1)}, f32[8,32,128]{2,1,0:T(8,128)S(1)}, u32[]{:S(2)}, u32[]{:S(2)}) %collective-permute-start.3) | collective-permute-done | bytes 131104 | tf_op jit(solution)/shard_map/ppermute | solution.py:453
  29.2 0.7 %shard_map.98 = f32[16,40,128]{2,1,0:T(8,128)S(1)} custom-call(s32[6]{0:T(128)S(1)} %stack.15.idx.info, f32[56,128]{1,0:T(8,128)S(1)} %get-tuple-element.23.table, f32[8,32,128]{2,1,0:T(8,128)S(1)} %get-tuple-element.28.strip, f32[8,32,128]{2,1,0:T(8,128)S(1)} %collective-permute-done.2.from_low, f32[8,32,128]{2,1,0:T(8,128)S(1)} %collective-permute-done.3.from_high, ...), custom_call_target="tpu_custom_call" | custom-call | flops 1000000 | bytes 1048576 | tf_op jit(solution)/shard_map/pallas_call | solution.py:481
  29.8 0.7 %collective-permute-start.4 = (f32[16,40,128]{2,1,0:T(8,128)S(1)}, f32[16,40,128]{2,1,0:T(8,128)S(1)}, u32[]{:S(2)}, u32[]{:S(2)}) collective-permute-start(f32[16,40,128]{2,1,0:T(8,128)S(1)} %shard_map.98), channel_id=1, source_target_pairs={{1,2},{3,4},{5,6},{2,1},{4,3},{6,5},{9,10},{11,12},{13,14},{10,9},... | collective-permute-start | bytes 983048 | tf_op jit(solution)/shard_map/ppermute | solution.py:458
  30.5 0.7 %shard_map.99 = f32[16,40,128]{2,1,0:T(8,128)S(1)} custom-call(s32[6]{0:T(128)S(1)} %stack.15.idx.info, f32[56,128]{1,0:T(8,128)S(1)} %get-tuple-element.23.table, f32[8,32,128]{2,1,0:T(8,128)S(1)} %get-tuple-element.28.strip, f32[8,32,128]{2,1,0:T(8,128)S(1)} %collective-permute-done.2.from_low, f32[8,32,128]{2,1,0:T(8,128)S(1)} %collective-permute-done.3.from_high, ...), custom_call_target="tpu_custom_call" | custom-call | flops 1000000 | bytes 1048576 | tf_op jit(solution)/shard_map/pallas_call | solution.py:481
  31.2 5.8 %collective-permute-start.5 = (f32[16,40,128]{2,1,0:T(8,128)S(1)}, f32[16,40,128]{2,1,0:T(8,128)S(1)}, u32[]{:S(2)}, u32[]{:S(2)}) collective-permute-start(f32[16,40,128]{2,1,0:T(8,128)S(1)} %shard_map.99), channel_id=1, source_target_pairs={{0,1},{2,3},{4,5},{6,7},{1,0},{3,2},{5,4},{7,6},{8,9},{10,11},{12,... | collective-permute-start | bytes 983048 | tf_op jit(solution)/shard_map/ppermute | solution.py:458
  37.0 4.7 %shard_map.100 = (f32[8,7,40,128]{3,2,1,0:T(8,128)S(1)}, f32[2,7,40,128]{3,2,1,0:T(8,128)S(1)}, f32[2,7,40,128]{3,2,1,0:T(8,128)S(1)}, f32[8,7,40,128]{3,2,1,0:T...) custom-call(s32[6]{0:T(128)S(1)} %stack.15.idx.info, ...), custom_call_target="tpu_custom_call" | custom-call | flops 1000000 | bytes 1048576 | tf_op jit(solution)/shard_map/pallas_call | solution.py:487
  41.7 2.9 %shard_map.101 = (f32[6,8,32,128]{3,2,1,0:T(8,128)}, f32[8,8,128]{2,1,0:T(8,128)S(1)}) custom-call(s32[6]{0:T(128)S(1)} %stack.15.idx.info, f32[56,128]{1,0:T(8,128)S(1)} %get-tuple-element.23.table, f32[8,32,128]{2,1,0:T(8,128)S(1)} %copy-done.2, f32[8,32,128]{2,1,0:T(8,128)S(1)} %get-tuple-element.28.strip, ...), custom_call_target="tpu_custom_call" | custom-call | flops 1000000 | bytes 1048576 | tf_op jit(solution)/shard_map/pallas_call | solution.py:505
  44.6 16.8 %all_to_all.5.parts = f32[8,8,128]{2,1,0:T(8,128)S(1)} all-to-all(f32[8,8,128]{2,1,0:T(8,128)S(1)} %get-tuple-element.43), channel_id=1, replica_groups=mesh['gx'=8,'gy'=12,'gz'=8] {'gz'}, dimensions={0} | all-to-all | bytes 65536 | tf_op jit(solution)/shard_map/all_to_all | solution.py:511
  61.5 0.7 %shard_map.102 = f32[16,32]{1,0:T(8,128)} custom-call(f32[8,8,128]{2,1,0:T(8,128)S(1)} %all_to_all.5.parts), custom_call_target="tpu_custom_call" | custom-call | flops 1000000 | bytes 1048576 | tf_op jit(solution)/shard_map/pallas_call | solution.py:512
  (15 shorter events, 0.0 us)
Async XLA Ops:
  0.6 1.4 %copy-start.2 = (f32[8,32,128]{2,1,0:T(8,128)S(1)}, f32[8,32,128]{2,1,0:T(8,128)}, u32[]{:S(2)}) copy-start(f32[8,32,128]{2,1,0:T(8,128)} %eddy.11) | copy-start | bytes 393220
  0.6 1.4 %copy-start.3 = (f32[8,32,128]{2,1,0:T(8,128)S(1)}, f32[8,32,128]{2,1,0:T(8,128)}, u32[]{:S(2)}) copy-start(f32[8,32,128]{2,1,0:T(8,128)} %diag.9) | copy-start | bytes 393220
  0.7 1.5 %copy-start.1 = (f32[6,8,32,128]{3,2,1,0:T(8,128)S(1)}, f32[6,8,32,128]{3,2,1,0:T(8,128)}, u32[]{:S(2)}) copy-start(f32[6,8,32,128]{3,2,1,0:T(8,128)} %adj.9) | copy-start | bytes 2359300
  0.7 17.2 %copy-start = (f32[3,6,8,32,128]{4,3,2,1,0:T(8,128)S(1)}, f32[3,6,8,32,128]{4,3,2,1,0:T(8,128)}, u32[]{:S(2)}) copy-start(f32[3,6,8,32,128]{4,3,2,1,0:T(8,128)} %metric.5) | copy-start | bytes 7077892
  2.1 10.4 %copy-start.4 = (s32[2048]{0:T(1024)S(1)}, s32[2048]{0:T(1024)}, u32[]{:S(2)}) copy-start(s32[2048]{0:T(1024)} %param.13) | copy-start | bytes 24580
  2.1 10.4 %copy-start.6 = (f32[6,6]{1,0:T(8,128)S(1)}, f32[6,6]{1,0:T(8,128)}, u32[]{:S(2)}) copy-start(f32[6,6]{1,0:T(8,128)} %coup.1) | copy-start | bytes 436
  5.1 10.0 %collective-permute-start = (f32[2,32,128]{2,1,0:T(8,128)}, f32[2,32,128]{2,1,0:T(8,128)}, u32[]{:S(2)}, u32[]{:S(2)}) collective-permute-start(f32[2,32,128]{2,1,0:T(8,128)} %get-tuple-element.26), channel_id=1, source_target_pairs={{0,8},{8,16},{16,24},{24,32},{32,40},{40,48},{48,56},{56,64},{64,7... | collective-permute-start | bytes 98312 | tf_op jit(solution)/shard_map/ppermute | solution.py:453
  10.6 7.3 %collective-permute-start.1 = (f32[2,32,128]{2,1,0:T(8,128)}, f32[2,32,128]{2,1,0:T(8,128)}, u32[]{:S(2)}, u32[]{:S(2)}) collective-permute-start(f32[2,32,128]{2,1,0:T(8,128)} %get-tuple-element.27), channel_id=1, source_target_pairs={{8,0},{16,8},{24,16},{32,24},{40,32},{48,40},{56,48},{64,56},{72,6... | collective-permute-start | bytes 98312 | tf_op jit(solution)/shard_map/ppermute | solution.py:453
  12.6 0.7 %copy-start.5 = (f32[2048]{0:T(1024)S(1)}, f32[2048]{0:T(1024)}, u32[]{:S(2)}) copy-start(f32[2048]{0:T(1024)} %param.14) | copy-start | bytes 24580
  13.3 0.7 %copy-start.7 = (s32[6]{0:T(128)S(1)}, s32[6]{0:T(128)}, u32[]{:S(2)}) copy-start(s32[6]{0:T(128)} %codes.1) | copy-start | bytes 76
  18.9 5.9 %collective-permute-start.2 = (f32[8,32,128]{2,1,0:T(8,128)S(1)}, f32[8,32,128]{2,1,0:T(8,128)S(1)}, u32[]{:S(2)}, u32[]{:S(2)}) collective-permute-start(f32[8,32,128]{2,1,0:T(8,128)S(1)} %get-tuple-element.29), channel_id=1, source_target_pairs={{0,96},{96,192},{192,288},{288,384},{384,480},{480,576},{576,672},... | collective-permute-start | bytes 393224 | tf_op jit(solution)/shard_map/ppermute | solution.py:453
  22.3 6.9 %collective-permute-start.3 = (f32[8,32,128]{2,1,0:T(8,128)S(1)}, f32[8,32,128]{2,1,0:T(8,128)S(1)}, u32[]{:S(2)}, u32[]{:S(2)}) collective-permute-start(f32[8,32,128]{2,1,0:T(8,128)S(1)} %get-tuple-element.30), channel_id=1, source_target_pairs={{96,0},{192,96},{288,192},{384,288},{480,384},{576,480},{672,576},... | collective-permute-start | bytes 393224 | tf_op jit(solution)/shard_map/ppermute | solution.py:453
  29.8 11.9 %collective-permute-start.4 = (f32[16,40,128]{2,1,0:T(8,128)S(1)}, f32[16,40,128]{2,1,0:T(8,128)S(1)}, u32[]{:S(2)}, u32[]{:S(2)}) collective-permute-start(f32[16,40,128]{2,1,0:T(8,128)S(1)} %shard_map.98), channel_id=1, source_target_pairs={{1,2},{3,4},{5,6},{2,1},{4,3},{6,5},{9,10},{11,12},{13,14},{10,9},... | collective-permute-start | bytes 983048 | tf_op jit(solution)/shard_map/ppermute | solution.py:458
  31.2 10.6 %collective-permute-start.5 = (f32[16,40,128]{2,1,0:T(8,128)S(1)}, f32[16,40,128]{2,1,0:T(8,128)S(1)}, u32[]{:S(2)}, u32[]{:S(2)}) collective-permute-start(f32[16,40,128]{2,1,0:T(8,128)S(1)} %shard_map.99), channel_id=1, source_target_pairs={{0,1},{2,3},{4,5},{6,7},{1,0},{3,2},{5,4},{7,6},{8,9},{10,11},{12,... | collective-permute-start | bytes 983048 | tf_op jit(solution)/shard_map/ppermute | solution.py:458

commit v4 on v3

--- a/solution.py
+++ b/solution.py
@@ -34,42 +34,76 @@
     return jax.ShapeDtypeStruct(shape, jnp.float32)
 
 
-def pack_y(adj, eddy, diag, metric, own, to_right, to_left):
-    lane = iota((8, COLS), 1)
+def pipeline(tasks):
+    held = None
+    for begin, end in tasks:
+        started = begin()
+        if held is not None:
+            held[0](held[1])
+        held = (end, started)
+    held[0](held[1])
+
+
+def pack_y(adj, eddy, diag, metric, own, to_right, to_left, packed):
+    shape = (4, 8, COLS)
+    lane = iota(shape, 2)
     slot, j = lane // SLOT, lane % SLOT
     quad, jj = j // 4, j % 4
-    edge_at = [(slot == p) & (j >= 1) & (j <= 6) for p in range(8)]
-    metric_at = [(slot == p) & (j >= 8) & (j <= 9) for p in range(FIELDS)]
-    for zg in range(2):
-        for t in range(ROWS // 8):
-            rows = pl.ds(8 * t, 8)
-            right = left = jnp.zeros((8, COLS), jnp.float32)
-            for zq in range(4):
-                z = 4 * zg + zq
-                c = jnp.zeros((8, COLS), jnp.float32)
-                for p in range(8):
-                    if p < FIELDS:
-                        v = adj[p, z, rows, :]
-                    elif p == EDDY:
-                        v = eddy[z, rows, :]
-                    else:
-                        v = relax_rate / diag[z, rows, :]
-                    c = jnp.where(edge_at[p], roll(v, SLOT * p + 4, 1), c)
-                    if p < FIELDS:
-                        c = jnp.where(metric_at[p], roll(metric[0, p, z, rows, :], SLOT * p + 9, 1), c)
-                own[z, rows, :] = jnp.where(j < 8, c, jnp.where(j >= 9, roll(c, 8, 1), 0.0))
-                at = 4 * zq
-                here = quad == zq
-                right = jnp.where(here, jnp.where(jj == 0, roll(c, at - 8, 1), roll(c, at, 1)), right)
-                left = jnp.where(here, jnp.where(jj == 3, roll(c, at - 6, 1), roll(c, at - 4, 1)), left)
-            to_right[zg, rows, :] = right
-            to_left[zg, rows, :] = left
+
+    def block(zg, t):
+        return pl.ds(4 * zg, 4), pl.ds(8 * t, 8)
+
+    def gather(zg, t):
+        zs, rows = block(zg, t)
+
+        def planes(p):
+            if p >= 8:
+                return roll(metric[0, p - 8, zs, rows, :], SLOT * (p - 8) + 9, 2)
+            v = adj[p, zs, rows, :] if p < FIELDS else eddy[zs, rows, :] if p == EDDY else relax_rate / diag[zs, rows, :]
+            return roll(v, SLOT * p + 4, 2)
+
+        def choose(p, v, c):
+            if p >= 8:
+                return jnp.where((slot == p - 8) & (j >= 8) & (j <= 9), v, c)
+            return jnp.where((slot == p) & (j >= 1) & (j <= 6), v, c)
+
+        c = jnp.zeros(shape, jnp.float32)
+        ahead = [planes(0), planes(1), planes(2)]
+        for p in range(14):
+            if p + 3 < 14:
+                ahead.append(planes(p + 3))
+            c = choose(p, ahead[p], c)
+        packed[zs, rows, :] = c
+
+    def send(zg, t):
+        zs, rows = block(zg, t)
+        c = packed[zs, rows, :]
+        c8 = roll(c, 8, 2)
+        right = left = jnp.zeros((8, COLS), jnp.float32)
+        moved = []
+        for zq in range(4):
+            at = 4 * zq
+            moved.append([roll(c[zq], at + by, 1) for by in (-8, 0, -6, -4)])
+        own[zs, rows, :] = jnp.where(j < 8, c, jnp.where(j >= 9, c8, 0.0))
+        for zq in range(4):
+            r0, r1, l0, l1 = moved[zq]
+            here = quad[0] == zq
+            right = jnp.where(here, jnp.where(jj[0] == 0, r0, r1), right)
+            left = jnp.where(here, jnp.where(jj[0] == 3, l0, l1), left)
+        to_right[zg, rows, :] = right
+        to_left[zg, rows, :] = left
+
+    blocks = [(zg, t) for zg in range(2) for t in range(ROWS // 8)]
+    for zg, t in blocks:
+        gather(zg, t)
+    for zg, t in blocks:
+        send(zg, t)
 
 
 MIX, PAIR = 8, 16
 
 
-def make_source(total_y, idx, codes, coup, cells, weights, src, table):
+def make_source(total_y, idx, codes, coup, cells, weights, after, src, table):
     slot = iota((1, COLS), 1) // SLOT
     for i in range(6):
         factor = jnp.where(codes[i] == 1, 1.0, jnp.where(codes[i] == 2, -1.0, 0.0)).astype(jnp.float32)
@@ -120,7 +154,7 @@
 HIGH_METRIC, LOW_METRIC = 26, 0
 
 
-def pack_x(src, own, from_left, from_right, adj, eddy, diag, metric, strip, to_low, to_high):
+def pack_x(own, from_left, from_right, adj, eddy, diag, metric, strip, to_low, to_high):
     j = iota((ROWS, COLS), 1) % SLOT
     for z in range(LEV):
         zg, at = z // 4, 4 * (z % 4)
@@ -161,41 +195,94 @@
         return jnp.concatenate([v[0:32], t4], 0)
 
 
-def sweep(edges, center, vertical, value, rate, strip_rate, table, store, src=None, flag=None):
+class Level:
+    def __init__(self, center, vertical, value, rate, edge_rate, ends, lateral, store, src=None, flag=None):
+        self.center, self.vertical, self.value = center, vertical, value
+        self.rate, self.edge_rate, self.ends, self.lateral = rate, edge_rate, ends, lateral
+        self.store, self.src, self.flag = store, src, flag
+
+
+def prepare(edges, strips, ends, lateral):
+    f2, f3 = edges.factors[2], edges.factors[3]
+
+    def task(at, strip):
+        def end(moved):
+            v, up, down = moved
+            ends[at] = jnp.where(edges.ghost_low, f2 * down, jnp.where(edges.ghost_high, f3 * up, v))
+            lateral[at] = jnp.where(edges.own_low, f2 * v, up) + jnp.where(edges.own_high, f3 * v, down)
+
+        def begin():
+            v = strip()
+            return v, roll(v, 1, 1), roll(v, -1, 1)
+
+        return begin, end
+
+    def turn(at, _):
+        def begin():
+            v = ends[at]
+            return v, roll(v, -10, 1)
+
+        def end(moved):
+            ends[at] = jnp.where(edges.j == 3, *moved)
+
+        return begin, end
+
+    pipeline([task(*s) for s in strips])
+    pipeline([turn(*s) for s in strips])
+
+
+def sweep(levels, table):
     lane = iota((EXT, COLS), 1)
+    half = FIELDS // 2
 
     def pair(e, f):
         at = PAIR + FIELDS * e + f
         return table[at : at + 1, :]
 
-    f2, f3 = edges.factors[2], edges.factors[3]
-    v = center(FIELDS)
-    up, down = roll(v, 1, 1), roll(v, -1, 1)
-    fixed = jnp.where(edges.ghost_low, f2 * down, jnp.where(edges.ghost_high, f3 * up, v))
-    both = jnp.where(edges.j == 3, fixed, roll(fixed, -10, 1))
-    beside = vertical(FIELDS) + roll(v, -1, 0) + roll(v, 1, 0)
-    beside = beside + jnp.where(edges.own_low, f2 * v, up) + jnp.where(edges.own_high, f3 * v, down)
-    a = value(FIELDS)
-    coupled = lanes_of(a, 0) * table[MIX : MIX + 1, :]
-    for e in range(1, FIELDS):
-        coupled = coupled + lanes_of(a, e) * table[MIX + e : MIX + e + 1, :]
-    rest = beside - coupled
-    if src is not None:
-        rest = rest + flag * src[1]
-    store(FIELDS, keep_rate * a + strip_rate * rest)
-    for f in range(FIELDS):
-        v = center(f)
-        end = roll(both, -(SLOT * f + 3), 1)
-        left = jnp.where(lane == 0, end, roll(v, 1, 1))
-        right = jnp.where(lane == COLS - 1, end, roll(v, -1, 1))
-        beside = vertical(f) + roll(v, -1, 0) + roll(v, 1, 0) + right + left
-        coupled = pair(0, f) * value(0)
-        for e in range(1, FIELDS):
-            coupled = coupled + pair(e, f) * value(e)
-        rest = beside - coupled
-        if f == 0 and src is not None:
-            rest = rest + flag * src[0]
-        store(f, keep_rate * value(f) + rate * rest)
+    def field(level, f):
+        def begin():
+            v = level.center(f)
+            return v, roll(level.ends(), -(SLOT * f + 3), 1), roll(v, 1, 1), roll(v, -1, 1)
+
+        def end(moved):
+            v, edge, left, right = moved
+            left = jnp.where(lane == 0, edge, left)
+            right = jnp.where(lane == COLS - 1, edge, right)
+            beside = level.vertical(f) + roll(v, -1, 0) + roll(v, 1, 0) + right + left
+            coupled = pair(0, f) * level.value(0)
+            for e in range(1, FIELDS):
+                coupled = coupled + pair(e, f) * level.value(e)
+            rest = beside - coupled
+            if f == 0 and level.src is not None:
+                rest = rest + level.flag * level.src[0]
+            level.store(f, keep_rate * level.value(f) + level.rate() * rest)
+
+        return begin, end
+
+    def strip(level):
+        sums = []
+
+        def mixed(first):
+            def begin():
+                a = level.value(FIELDS)
+                return [lanes_of(a, e) for e in range(first, first + half)]
+
+            def end(moved):
+                terms = [v * table[MIX + first + i : MIX + first + i + 1, :] for i, v in enumerate(moved)]
+                sums.append(terms[0] + terms[1] + terms[2])
+
+            return begin, end
+
+        def end(_):
+            v = level.center(FIELDS)
+            rest = level.vertical(FIELDS) + roll(v, -1, 0) + roll(v, 1, 0) + level.lateral() - (sums[0] + sums[1])
+            if level.src is not None:
+                rest = rest + level.flag * level.src[1]
+            level.store(FIELDS, keep_rate * level.value(FIELDS) + level.edge_rate() * rest)
+
+        return [mixed(0), mixed(half), (lambda: None, end)]
+
+    pipeline([task for level in levels for task in strip(level) + [field(level, f) for f in range(FIELDS)]])
 
 
 def level_sums(z, info, field, edge_strip, strip, metric, metric_row, sums, out, zo):
@@ -246,7 +333,7 @@
 
 def inner_levels(
     info, table, adj, eddy, diag, strip, from_low, from_high, metric, src,
-    f0, near1, next2, f1, rates, edge_eddy, edge_rate, out, sums, halo, metric_row, a1, a2,
+    f0, near1, next2, f1, rates, edge_eddy, edge_rate, out, sums, halo, metric_row, a1, a2, ends, lateral,
 ):
     edges = Edges(info, table)
     row = iota((8, COLS), 0)
@@ -272,62 +359,74 @@
         s = value(z, FIELDS)
         edge_eddy[z] = lanes_of(s, EDDY)
         edge_rate[z] = lanes_of(s, RATE)
+    for z in range(LEV):
         e = eddies(z)
         for f in range(FIELDS):
             f0[z, f] = edges.flux(value(z, f) * e)
-        f0[z, FIELDS] = edges.flux(s * edge_eddy[z])
-
-    def around(array, z):
+        f0[z, FIELDS] = edges.flux(value(z, FIELDS) * edge_eddy[z])
+
+    def strips_of(array, zs):
+        return [(z, lambda z=z: array[z, FIELDS]) for z in zs]
+
+    def level(z, flux, value, vertical, store, **more):
+        return Level(
+            lambda p: flux[z, p],
+            vertical,
+            lambda p: value(z, p),
+            lambda: rates[z],
+            lambda: edge_rate[z],
+            lambda: ends[z],
+            lambda: lateral[z],
+            store,
+            **more,
+        )
+
+    def store_first(z):
+        def store(p, v):
+            if z in (0, LEV - 1):
+                near1[z // (LEV - 1), p] = v
+            else:
+                a1[z, p] = v
+                f1[z, p] = edges.flux(v * (edge_eddy[z] if p == FIELDS else eddies(z)))
+
+        return store
+
+    def store_second(z):
+        def store(p, v):
+            if z in (1, LEV - 2):
+                next2[z // (LEV - 2), p] = v
+            else:
+                a2[z, p] = v
+
+        return store
+
+    def around(array, z, low, high):
+        if z == low:
+            return lambda p: array[z + 1, p]
+        if z == high:
+            return lambda p: array[z - 1, p]
         return lambda p: array[z - 1, p] + array[z + 1, p]
 
-    def first(z, vertical, store, **more):
-        sweep(edges, lambda p: f0[z, p], vertical, lambda p: value(z, p), rates[z], edge_rate[z], table, store, **more)
-
-    def store_near(i):
-        def store(p, v):
-            near1[i, p] = v
-
-        return store
-
-    def store_inner(z):
-        def store(p, v):
-            a1[z, p] = v
-            f1[z, p] = edges.flux(v * (edge_eddy[z] if p == FIELDS else eddies(z)))
-
-        return store
-
-    first(0, lambda p: f0[1, p], store_near(0), src=src, flag=flag)
-    first(LEV - 1, lambda p: f0[LEV - 2, p], store_near(1))
-    for z in range(1, LEV - 1):
-        first(z, around(f0, z), store_inner(z))
+    prepare(edges, strips_of(f0, range(LEV)), ends, lateral)
+    sweep(
+        [
+            level(z, f0, value, around(f0, z, 0, LEV - 1), store_first(z), **({"src": src, "flag": flag} if z == 0 else {}))
+            for z in range(LEV)
+        ],
+        table,
+    )
+    inside = range(1, LEV - 1)
+    prepare(edges, strips_of(f1, inside), ends, lateral)
+    sweep([level(z, f1, lambda z, p: a1[z, p], around(f1, z, 1, LEV - 2), store_second(z)) for z in inside], table)
     sums[...] = jnp.zeros_like(sums)
-
-    def second(z, vertical, store):
-        sweep(edges, lambda p: f1[z, p], vertical, lambda p: a1[z, p], rates[z], edge_rate[z], table, store)
-
-    def store_next(i):
-        def store(p, v):
-            next2[i, p] = v
-
-        return store
-
-    def store_last(z):
-        def store(p, v):
-            a2[z, p] = v
-
-        return store
-
-    second(1, lambda p: f1[2, p], store_next(0))
-    second(LEV - 2, lambda p: f1[LEV - 3, p], store_next(1))
     for z in range(2, LEV - 2):
-        second(z, around(f1, z), store_last(z))
         level_sums(z, info, lambda f: a2[z, f], a2[z, FIELDS], strip, metric, metric_row, sums, out, z - 2)
 
 
 def outer_levels(
     info, table, eddy, strip, from_b, from_a, metric, src,
     f0, near1, next2, f1, rates, edge_eddy, edge_rate, inner_out, inner_sums, halo_rows, metric_row,
-    out, share, sums, fh, gh, an, gn, a2,
+    out, share, sums, fh, gh, an, gn, a2, edge_over, ends, lateral,
 ):
     edges = Edges(info, table)
     hub = info[5] * LEV // 4 - info[2] * LEV
@@ -340,94 +439,97 @@
     def flag_of(z):
         return jnp.where(z == hub, 1.0, 0.0).astype(jnp.float32)
 
-    for n, msg in enumerate((from_a, from_b)):
+    def side(n, msg):
         top = even if n == 0 else jnp.logical_not(even)
-        i = jnp.where(top, 1, 0)
-        near = jnp.where(top, LEV - 1, 0)
-        next_ = jnp.where(top, LEV - 2, 1)
-        over = jnp.where(top, LEV, -1)
+        near, next_ = jnp.where(top, LEV - 1, 0), jnp.where(top, LEV - 2, 1)
         ghost = jnp.where(top, edges.high_z, edges.low_z)
         factor = jnp.where(top, edges.factors[5], edges.factors[4])
-        eddy_over = msg[EDDY]
-        s = msg[STRIP]
-        edge_eddy_over = lanes_of(s, EDDY)
+        return n, msg, jnp.where(top, 1, 0), near, next_, jnp.where(top, LEV, -1), ghost, factor
+
+    sides = [side(0, from_a), side(1, from_b)]
+    for n, msg, *_ in sides:
+        edge_over[n, 0] = lanes_of(msg[STRIP], EDDY)
+        edge_over[n, 1] = lanes_of(msg[STRIP], RATE)
+    for n, msg, i, near, next_, over, ghost, factor in sides:
         eddy_near = jnp.concatenate([eddy[near], halo_rows[near, EDDY]], 0)
-        for p in range(FIELDS + 1):
-            v = s * edge_eddy_over if p == FIELDS else msg[p] * eddy_over
+        for p in (FIELDS, *range(FIELDS)):
+            v = msg[STRIP] * edge_over[n, 0] if p == FIELDS else msg[p] * msg[EDDY]
             v = jnp.where(ghost, factor * f0[near, p], edges.flux(v))
             fh[n, p] = v
             r, e = (edge_rate[near], edge_eddy[near]) if p == FIELDS else (rates[near], eddy_near)
             v = near1[i, p] + r * v
             an[n, p] = v
             gn[n, p] = edges.flux(v * e)
-
-        def store_over(p, v):
-            v = edges.flux(v * (edge_eddy_over if p == FIELDS else eddy_over))
+    prepare(edges, [(n, lambda n=n: fh[n, FIELDS]) for n in range(2)], ends, lateral)
+    prepare(edges, [(2 + n, lambda n=n: gn[n, FIELDS]) for n in range(2)], ends, lateral)
+
+    def over_level(n, msg, i, near, next_, over, ghost, factor):
+        def store(p, v):
+            v = edges.flux(v * (edge_over[n, 0] if p == FIELDS else msg[EDDY]))
             gh[n, p] = jnp.where(ghost, factor * gn[n, p], v)
 
-        sweep(
-            edges,
+        return Level(
             lambda p: fh[n, p],
             lambda p: msg[9 + p] + f0[near, p],
             lambda p: msg[STRIP if p == FIELDS else p],
-            msg[RATE],
-            lanes_of(s, RATE),
-            table,
-            store_over,
+            lambda: msg[RATE],
+            lambda: edge_over[n, 1],
+            lambda: ends[n],
+            lambda: lateral[n],
+            store,
             src,
             flag_of(over),
         )
 
-        def after(p):
-            r = edge_rate[next_] if p == FIELDS else rates[next_]
-            return next2[i, p] + r * gn[n, p]
-
-        level_sums(next_, info, after, after(FIELDS), strip, metric, metric_row, sums, out, next_)
-
-        def store_last(p, v):
+    def near_level(n, msg, i, near, next_, over, ghost, factor):
+        def store(p, v):
             a2[n, p] = v
 
-        sweep(
-            edges,
+        return Level(
             lambda p: gn[n, p],
             lambda p: gh[n, p] + f1[next_, p],
             lambda p: an[n, p],
-            rates[near],
-            edge_rate[near],
-            table,
-            store_last,
+            lambda: rates[near],
+            lambda: edge_rate[near],
+            lambda: ends[2 + n],
+            lambda: lateral[2 + n],
+            store,
             src,
             flag_of(near),
         )
+
+    sweep([over_level(*s) for s in sides], table)
+    for n, msg, i, near, next_, over, ghost, factor in sides:
+
+        def after(p):
+            return next2[i, p] + (edge_rate[next_] if p == FIELDS else rates[next_]) * gn[n, p]
+
+        level_sums(next_, info, after, after(FIELDS), strip, metric, metric_row, sums, out, next_)
+    sweep([near_level(*s) for s in sides], table)
+    for n, msg, i, near, *_ in sides:
         level_sums(near, info, lambda f: a2[n, f], a2[n, FIELDS], strip, metric, metric_row, sums, out, near)
 
     s1 = sums[1]
     stream = roll(s1, -1, 0)[:ROWS] - roll(s1, 1, 0)[:ROWS]
     t = sums[3, :ROWS]
-    t = t + roll(t, 4 * SLOT, 1)
-    t = t + roll(t, 2 * SLOT, 1)
-    t = t + roll(t, SLOT, 1)
     s2 = sums[2, :ROWS]
     lane = iota((ROWS, COLS), 1)
-    right = jnp.where(lane == COLS - 1, roll(t, 3, 1), roll(s2, -1, 1))
-    left = jnp.where(lane == 0, roll(t, -3, 1), roll(s2, 1, 1))
+    right, left = roll(s2, -1, 1), roll(s2, 1, 1)
+    high = [roll(t, COLS - 1 - (SLOT * f + 12), 1) for f in range(FIELDS)]
+    low = [roll(t, -(SLOT * f + 3), 1) for f in range(FIELDS)]
+    right = jnp.where(lane == COLS - 1, (high[0] + high[1] + high[2]) + (high[3] + high[4] + high[5]), right)
+    left = jnp.where(lane == 0, (low[0] + low[1] + low[2]) + (low[3] + low[4] + low[5]), left)
     total = sums[0, :ROWS] - 0.5 * stream - 0.5 * (right - left)
     turned = jnp.concatenate([total, jnp.zeros((COLS - ROWS, COLS), jnp.float32)], 0).T
-    count, width = share.shape[0], COLS // share.shape[0]
-    group = iota((8, COLS), 1) // ROWS
-    for k in range(count):
-        v = turned[width * k : width * k + 8]
-        for q in range(1, width // 8):
-            v = jnp.where(group == q, roll(turned[width * k + 8 * q : width * k + 8 * q + 8], ROWS * q, 1), v)
-        share[k] = v
+    for k in range(share.shape[0]):
+        share[k] = turned[share.shape[1] * k : share.shape[1] * (k + 1)]
 
 
 def add_shares(parts, out):
     total = parts[0]
     for i in range(1, parts.shape[0]):
         total = total + parts[i]
-    for q in range(out.shape[0] // 8):
-        out[8 * q : 8 * q + 8, :] = roll(total, -ROWS * q, 1)[:, :ROWS]
+    out[...] = total[:, :ROWS]
 
 
 def call(body, outs, ins, scratch=()):
@@ -465,17 +567,18 @@
         pack_y,
         (f32(*level), f32(2, ROWS, COLS), f32(2, ROWS, COLS)),
         [VM] * 4,
+        [buf(*level)],
     )(adjoint_start, eddy_visc, diag_coef, metric_terms[2:3])
     from_left = shift(to_right, "gy", 1)
     from_right = shift(to_left, "gy", -1)
-    src, table = call(
-        functools.partial(make_source, COLS * count[1]), (f32(2, EXT, COLS), f32(56, COLS)), [SM] * 3 + [VM] * 2
-    )(info, face_codes, coupling, cells, weights)
-    strip, to_low, to_high = call(pack_x, (f32(*level),) * 3, [VM] * 8)(
-        src, own, from_left, from_right, adjoint_start, eddy_visc, diag_coef, metric_terms
+    strip, to_low, to_high = call(pack_x, (f32(*level),) * 3, [VM] * 7)(
+        own, from_left, from_right, adjoint_start, eddy_visc, diag_coef, metric_terms
     )
     from_low = shift(to_high, "gx", 1)
     from_high = shift(to_low, "gx", -1)
+    src, table = call(
+        functools.partial(make_source, COLS * count[1]), (f32(2, EXT, COLS), f32(56, COLS)), [SM] * 3 + [VM] * 3
+    )(info, face_codes, coupling, cells, weights, strip)
     received = (from_low, from_high, adjoint_start, eddy_visc, diag_coef)
     msg_b, msg_a = [
         call(functools.partial(pack_z, far), f32(16, EXT, COLS), [SM] + [VM] * 7)(info, table, strip, *received)
@@ -500,13 +603,13 @@
             f32(FIELDS, LEV, 8, COLS),
         ),
         [SM] + [VM] * 9,
-        [buf(LEV, 7, *ext), buf(LEV, 7, *ext)],
+        [buf(LEV, 7, *ext), buf(LEV, 7, *ext), buf(LEV, *ext), buf(LEV, *ext)],
     )(info, table, adjoint_start, eddy_visc, diag_coef, strip, from_low, from_high, metric_terms, src)
     adjoint, share = call(
         outer_levels,
-        (f32(FIELDS, *level), f32(count[2], 8, COLS)),
+        (f32(FIELDS, *level), f32(count[2], COLS // count[2], COLS)),
         [SM] + [VM] * 18,
-        [buf(4, *ext)] + [buf(2, 7, *ext)] * 5,
+        [buf(4, *ext)] + [buf(2, 7, *ext)] * 5 + [buf(2, 2, *ext), buf(4, *ext), buf(4, *ext)],
     )(info, table, eddy_visc, strip, from_b, from_a, metric_terms, src, *inner)
     parts = lax.all_to_all(share, "gz", 0, 0, tiled=True)
     height_grad = call(add_shares, f32(COLS // count[2], ROWS), [VM])(parts).T

time: 62.5 us -> 60.8 us (0.973)
  Pallas kernels: 14.6 us -> 12.1 us
    pallas_call x1, Pallas kernels: 2.93 us -> 0.66 us  [local(): call(pack_y, (f32(*level), f32(2, ROWS, COLS), f32(2, ROWS, COLS)), [VM]...]
    pallas_call x2, Pallas kernels: 1.32 us -> 2.17 us  [local(): call(functools.partial(pack_z, far), f32(16, EXT, COLS), [SM] + [VM] * 7)]
    ppermute x4, starting transfers between devices: 12.1 us -> 12.7 us  [shift(): lax.ppermute(v, axis, [(i, i + step) for i in range(n) if 0 <= i + step <...]
    pallas_call x1, Pallas kernels: 4.72 us -> 4.09 us  [local(): call(inner_levels, (f32(LEV, 7, *ext), f32(2, 7, *ext), f32(2, 7, *ext),...]
  transfers between devices with their start and end apart: 6 -> 6, of which waited for: 3 -> 2; matrix products, arithmetic and copies ran while one was open for 0% -> 0% of each run, Pallas kernels for 10% -> 10%
where the time goes in v4:
time: 60.8 us; the launch traced here: 60.4 us
  starting transfers between devices  19.2 us (32%)
  blocking collectives  17 us (28%)
  Pallas kernels  12.1 us (20%)
  waiting for transfers between devices  8.37 us (14%)
  local copies, waits for them, and re-layouts  2.9 us (5%)
  between operations  0.8 us (1%)
    all_to_all x1, blocking collectives, local(): parts = lax.all_to_all(share, 'gz', 0, 0, tiled=True)  17 us
    ppermute x4, starting transfers between devices, shift(): lax.ppermute(v, axis, [(i, i + step) for i in range(n) if 0 <= i + step <...  12.7 us
    ppermute x4, waiting for transfers between devices, shift(): lax.ppermute(v, axis, [(i, i + step) for i in range(n) if 0 <= i + step <...  8.37 us
    ppermute x2, starting transfers between devices, trade(): return lax.ppermute(v, axis, pairs + [(b, a) for a, b in pairs])  6.5 us
    pallas_call x1, Pallas kernels, local(): call(inner_levels, (f32(LEV, 7, *ext), f32(2, 7, *ext), f32(2, 7, *ext),...  4.09 us
    pallas_call x1, Pallas kernels, local(): call(outer_levels, (f32(FIELDS, *level), f32(count[2], COLS // count[2],...  2.59 us
    pallas_call x2, Pallas kernels, local(): call(functools.partial(pack_z, far), f32(16, EXT, COLS), [SM] + [VM] * 7)  2.17 us
    unnamed x16, local copies, waits for them, and re-layouts  1.46 us
  transfers between devices with their start and end apart: 6, of which 2 were waited for; matrix products, arithmetic and copies ran while one was open for 0% of the time, Pallas kernels for 10%

profile of v4, /device:TPU:192, one launch (start us, length us, event | category | flops | bytes accessed | tf_op | source)
XLA Modules:
  0.0 60.4 jit_solution(11923948193300755872)
XLA Ops:
  0.7 1.4 %slice.3.metric = f32[1,6,8,32,128]{4,3,2,1,0:T(8,128)S(1)} slice(f32[3,6,8,32,128]{4,3,2,1,0:T(8,128)} %metric.5), slice={[2:3], [0:6], [0:8], [0:32], [0:128]} | slice | bytes 1572864 | tf_op jit(solution)/shard_map/slice | solution.py:571
  2.1 0.1 copy-done.1
  2.1 0.7 %shard_map.95 = (f32[8,32,128]{2,1,0:T(8,128)S(1)}, f32[2,32,128]{2,1,0:T(8,128)S(1)}, f32[2,32,128]{2,1,0:T(8,128)S(1)}) custom-call(f32[6,8,32,128]{3,2,1,0:T(8,128)S(1)} %copy-done.1, f32[8,32,128]{2,1,0:T(8,128)S(1)} %copy-done.2, f32[8,32,128]{2,1,0:T(8,128)S(1)} %copy-done.3, f32[1,6,8,32,128]{4,3,2,1,0:T(8,128)S(1)} %slice.3.metric), custom_call_target="tpu_custom_call" | custom-call | flops 1000000 | bytes 1048576 | tf_op jit(solution)/shard_map/pallas_call | solution.py:566
  2.8 5.5 %collective-permute-start = (f32[2,32,128]{2,1,0:T(8,128)S(1)}, f32[2,32,128]{2,1,0:T(8,128)S(1)}, u32[]{:S(2)}, u32[]{:S(2)}) collective-permute-start(f32[2,32,128]{2,1,0:T(8,128)S(1)} %get-tuple-element.24), channel_id=1, source_target_pairs={{0,8},{8,16},{16,24},{24,32},{32,40},{40,48},{48,56},{56,64},{64,7... | collective-permute-start | bytes 98312 | tf_op jit(solution)/shard_map/ppermute | solution.py:555
  8.3 1.9 %collective-permute-start.1 = (f32[2,32,128]{2,1,0:T(8,128)S(1)}, f32[2,32,128]{2,1,0:T(8,128)S(1)}, u32[]{:S(2)}, u32[]{:S(2)}) collective-permute-start(f32[2,32,128]{2,1,0:T(8,128)S(1)} %get-tuple-element.25), channel_id=1, source_target_pairs={{8,0},{16,8},{24,16},{32,24},{40,32},{48,40},{56,48},{64,56},{72,6... | collective-permute-start | bytes 98312 | tf_op jit(solution)/shard_map/ppermute | solution.py:555
  10.2 0.0 collective-permute-done.from_left
  10.3 5.1 %collective-permute-done.1.from_right = f32[2,32,128]{2,1,0:T(8,128)S(1)} collective-permute-done((f32[2,32,128]{2,1,0:T(8,128)S(1)}, f32[2,32,128]{2,1,0:T(8,128)S(1)}, u32[]{:S(2)}, u32[]{:S(2)}) %collective-permute-start.1) | collective-permute-done | bytes 32800 | tf_op jit(solution)/shard_map/ppermute | solution.py:555
  15.3 0.8 %shard_map.96 = (f32[8,32,128]{2,1,0:T(8,128)S(1)}, f32[8,32,128]{2,1,0:T(8,128)}, f32[8,32,128]{2,1,0:T(8,128)}) custom-call(f32[8,32,128]{2,1,0:T(8,128)S(1)} %get-tuple-element.23.own, f32[2,32,128]{2,1,0:T(8,128)S(1)} %collective-permute-done.from_left, f32[2,32,128]{2,1,0:T(8,128)S(1)} %collective-permute-done.1.from_right, ...), custom_call_target="tpu_custom_call" | custom-call | flops 1000000 | bytes 1048576 | tf_op jit(solution)/shard_map/pallas_call | solution.py:574
  16.2 4.0 %collective-permute-start.2 = (f32[8,32,128]{2,1,0:T(8,128)}, f32[8,32,128]{2,1,0:T(8,128)}, u32[]{:S(2)}, u32[]{:S(2)}) collective-permute-start(f32[8,32,128]{2,1,0:T(8,128)} %get-tuple-element.28), channel_id=1, source_target_pairs={{0,96},{96,192},{192,288},{288,384},{384,480},{480,576},{576,672},... | collective-permute-start | bytes 393224 | tf_op jit(solution)/shard_map/ppermute | solution.py:555
  20.2 1.3 %collective-permute-start.3 = (f32[8,32,128]{2,1,0:T(8,128)}, f32[8,32,128]{2,1,0:T(8,128)}, u32[]{:S(2)}, u32[]{:S(2)}) collective-permute-start(f32[8,32,128]{2,1,0:T(8,128)} %get-tuple-element.29), channel_id=1, source_target_pairs={{96,0},{192,96},{288,192},{384,288},{480,384},{576,480},{672,576},... | collective-permute-start | bytes 393224 | tf_op jit(solution)/shard_map/ppermute | solution.py:555
  21.5 0.1 stack.15.idx.info
  21.6 0.0 copy-start.5
  21.6 0.7 %copy-done.5 = f32[2048]{0:T(1024)S(1)} copy-done((f32[2048]{0:T(1024)S(1)}, f32[2048]{0:T(1024)}, u32[]{:S(2)}) %copy-start.5) | copy-done | bytes 8216
  22.3 0.7 %copy-done.7 = s32[6]{0:T(128)S(1)} copy-done((s32[6]{0:T(128)S(1)}, s32[6]{0:T(128)}, u32[]{:S(2)}) %copy-start.7) | copy-done | bytes 48
  23.0 1.1 %shard_map.97 = (f32[2,40,128]{2,1,0:T(8,128)S(1)}, f32[56,128]{1,0:T(8,128)S(1)}) custom-call(s32[6]{0:T(128)S(1)} %stack.15.idx.info, s32[6]{0:T(128)S(1)} %copy-done.7, f32[6,6]{1,0:T(8,128)S(1)} %copy-done.6, s32[16,128]{1,0:T(8,128)S(1)} %bitcast.6, f32[16,128]{1,0:T(8,128)S(1)} %bitcast.7, f32[8,32,128]{2,1,0:T(8,128)S(1)} %get-tuple-element.26.after.strip), custom_call_target="tpu_custom_call" | custom-call | flops 1000000 | bytes 1048576 | tf_op jit(solution)/shard_map/pallas_call | solution.py:579
  24.1 3.3 %collective-permute-done.3.from_high = f32[8,32,128]{2,1,0:T(8,128)} collective-permute-done((f32[8,32,128]{2,1,0:T(8,128)}, f32[8,32,128]{2,1,0:T(8,128)}, u32[]{:S(2)}, u32[]{:S(2)}) %collective-permute-start.3) | collective-permute-done | bytes 131104 | tf_op jit(solution)/shard_map/ppermute | solution.py:555
  27.4 1.1 %shard_map.98 = f32[16,40,128]{2,1,0:T(8,128)S(1)} custom-call(s32[6]{0:T(128)S(1)} %stack.15.idx.info, f32[56,128]{1,0:T(8,128)S(1)} %get-tuple-element.27.table, f32[8,32,128]{2,1,0:T(8,128)S(1)} %get-tuple-element.26.after.strip, f32[8,32,128]{2,1,0:T(8,128)} %collective-permute-done.2.from_low, f32[8,32,128]{2,1,0:T(8,128)} %collective-permute-done.3.from_high, ...), custom_call_target="tpu_custom_call" | custom-call | flops 1000000 | bytes 1048576 | tf_op jit(solution)/shard_map/pallas_call | solution.py:584
  28.5 0.7 %collective-permute-start.4 = (f32[16,40,128]{2,1,0:T(8,128)S(1)}, f32[16,40,128]{2,1,0:T(8,128)S(1)}, u32[]{:S(2)}, u32[]{:S(2)}) collective-permute-start(f32[16,40,128]{2,1,0:T(8,128)S(1)} %shard_map.98), channel_id=1, source_target_pairs={{1,2},{3,4},{5,6},{2,1},{4,3},{6,5},{9,10},{11,12},{13,14},{10,9},... | collective-permute-start | bytes 983048 | tf_op jit(solution)/shard_map/ppermute | solution.py:560
  29.1 1.1 %shard_map.99 = f32[16,40,128]{2,1,0:T(8,128)S(1)} custom-call(s32[6]{0:T(128)S(1)} %stack.15.idx.info, f32[56,128]{1,0:T(8,128)S(1)} %get-tuple-element.27.table, f32[8,32,128]{2,1,0:T(8,128)S(1)} %get-tuple-element.26.after.strip, f32[8,32,128]{2,1,0:T(8,128)} %collective-permute-done.2.from_low, f32[8,32,128]{2,1,0:T(8,128)} %collective-permute-done.3.from_high, ...), custom_call_target="tpu_custom_call" | custom-call | flops 1000000 | bytes 1048576 | tf_op jit(solution)/shard_map/pallas_call | solution.py:584
  30.2 5.8 %collective-permute-start.5 = (f32[16,40,128]{2,1,0:T(8,128)S(1)}, f32[16,40,128]{2,1,0:T(8,128)S(1)}, u32[]{:S(2)}, u32[]{:S(2)}) collective-permute-start(f32[16,40,128]{2,1,0:T(8,128)S(1)} %shard_map.99), channel_id=1, source_target_pairs={{0,1},{2,3},{4,5},{6,7},{1,0},{3,2},{5,4},{7,6},{8,9},{10,11},{12,... | collective-permute-start | bytes 983048 | tf_op jit(solution)/shard_map/ppermute | solution.py:560
  36.1 4.1 %shard_map.100 = (f32[8,7,40,128]{3,2,1,0:T(8,128)S(1)}, f32[2,7,40,128]{3,2,1,0:T(8,128)S(1)}, f32[2,7,40,128]{3,2,1,0:T(8,128)S(1)}, f32[8,7,40,128]{3,2,1,0:T...) custom-call(s32[6]{0:T(128)S(1)} %stack.15.idx.info, ...), custom_call_target="tpu_custom_call" | custom-call | flops 1000000 | bytes 1048576 | tf_op jit(solution)/shard_map/pallas_call | solution.py:590
  40.2 2.6 %shard_map.101 = (f32[6,8,32,128]{3,2,1,0:T(8,128)}, f32[8,16,128]{2,1,0:T(8,128)S(1)}) custom-call(s32[6]{0:T(128)S(1)} %stack.15.idx.info, f32[56,128]{1,0:T(8,128)S(1)} %get-tuple-element.27.table, f32[8,32,128]{2,1,0:T(8,128)S(1)} %copy-done.2, f32[8,32,128]{2,1,0:T(8,128)S(1)} %get-tuple-element.26.after.strip, ...), custom_call_target="tpu_custom_call" | custom-call | flops 1000000 | bytes 1048576 | tf_op jit(solution)/shard_map/pallas_call | solution.py:608
  42.8 17.0 %all_to_all.5.parts = f32[8,16,128]{2,1,0:T(8,128)S(1)} all-to-all(f32[8,16,128]{2,1,0:T(8,128)S(1)} %get-tuple-element.43), channel_id=1, replica_groups=mesh['gx'=8,'gy'=12,'gz'=8] {'gz'}, dimensions={0} | all-to-all | bytes 131072 | tf_op jit(solution)/shard_map/all_to_all | solution.py:614
  59.8 0.6 %shard_map.102 = f32[16,32]{1,0:T(8,128)} custom-call(f32[8,16,128]{2,1,0:T(8,128)S(1)} %all_to_all.5.parts), custom_call_target="tpu_custom_call" | custom-call | flops 1000000 | bytes 1048576 | tf_op jit(solution)/shard_map/pallas_call | solution.py:615
  (15 shorter events, 0.0 us)
Async XLA Ops:
  0.6 1.4 %copy-start.2 = (f32[8,32,128]{2,1,0:T(8,128)S(1)}, f32[8,32,128]{2,1,0:T(8,128)}, u32[]{:S(2)}) copy-start(f32[8,32,128]{2,1,0:T(8,128)} %eddy.11) | copy-start | bytes 393220
  0.6 1.4 %copy-start.3 = (f32[8,32,128]{2,1,0:T(8,128)S(1)}, f32[8,32,128]{2,1,0:T(8,128)}, u32[]{:S(2)}) copy-start(f32[8,32,128]{2,1,0:T(8,128)} %diag.9) | copy-start | bytes 393220
  0.7 1.5 %copy-start.1 = (f32[6,8,32,128]{3,2,1,0:T(8,128)S(1)}, f32[6,8,32,128]{3,2,1,0:T(8,128)}, u32[]{:S(2)}) copy-start(f32[6,8,32,128]{3,2,1,0:T(8,128)} %adj.9) | copy-start | bytes 2359300
  0.7 14.7 %copy-start = (f32[3,6,8,32,128]{4,3,2,1,0:T(8,128)S(1)}, f32[3,6,8,32,128]{4,3,2,1,0:T(8,128)}, u32[]{:S(2)}) copy-start(f32[3,6,8,32,128]{4,3,2,1,0:T(8,128)} %metric.5) | copy-start | bytes 7077892
  2.8 7.4 %collective-permute-start = (f32[2,32,128]{2,1,0:T(8,128)S(1)}, f32[2,32,128]{2,1,0:T(8,128)S(1)}, u32[]{:S(2)}, u32[]{:S(2)}) collective-permute-start(f32[2,32,128]{2,1,0:T(8,128)S(1)} %get-tuple-element.24), channel_id=1, source_target_pairs={{0,8},{8,16},{16,24},{24,32},{32,40},{40,48},{48,56},{56,64},{64,7... | collective-permute-start | bytes 98312 | tf_op jit(solution)/shard_map/ppermute | solution.py:555
  8.3 7.0 %collective-permute-start.1 = (f32[2,32,128]{2,1,0:T(8,128)S(1)}, f32[2,32,128]{2,1,0:T(8,128)S(1)}, u32[]{:S(2)}, u32[]{:S(2)}) collective-permute-start(f32[2,32,128]{2,1,0:T(8,128)S(1)} %get-tuple-element.25), channel_id=1, source_target_pairs={{8,0},{16,8},{24,16},{32,24},{40,32},{48,40},{56,48},{64,56},{72,6... | collective-permute-start | bytes 98312 | tf_op jit(solution)/shard_map/ppermute | solution.py:555
  15.3 6.3 %copy-start.4 = (s32[2048]{0:T(1024)S(1)}, s32[2048]{0:T(1024)}, u32[]{:S(2)}) copy-start(s32[2048]{0:T(1024)} %param.13) | copy-start | bytes 24580
  15.3 6.3 %copy-start.6 = (f32[6,6]{1,0:T(8,128)S(1)}, f32[6,6]{1,0:T(8,128)}, u32[]{:S(2)}) copy-start(f32[6,6]{1,0:T(8,128)} %coup.1) | copy-start | bytes 436
  16.2 7.9 %collective-permute-start.2 = (f32[8,32,128]{2,1,0:T(8,128)}, f32[8,32,128]{2,1,0:T(8,128)}, u32[]{:S(2)}, u32[]{:S(2)}) collective-permute-start(f32[8,32,128]{2,1,0:T(8,128)} %get-tuple-element.28), channel_id=1, source_target_pairs={{0,96},{96,192},{192,288},{288,384},{384,480},{480,576},{576,672},... | collective-permute-start | bytes 393224 | tf_op jit(solution)/shard_map/ppermute | solution.py:555
  20.2 7.2 %collective-permute-start.3 = (f32[8,32,128]{2,1,0:T(8,128)}, f32[8,32,128]{2,1,0:T(8,128)}, u32[]{:S(2)}, u32[]{:S(2)}) collective-permute-start(f32[8,32,128]{2,1,0:T(8,128)} %get-tuple-element.29), channel_id=1, source_target_pairs={{96,0},{192,96},{288,192},{384,288},{480,384},{576,480},{672,576},... | collective-permute-start | bytes 393224 | tf_op jit(solution)/shard_map/ppermute | solution.py:555
  21.6 0.7 %copy-start.5 = (f32[2048]{0:T(1024)S(1)}, f32[2048]{0:T(1024)}, u32[]{:S(2)}) copy-start(f32[2048]{0:T(1024)} %param.14) | copy-start | bytes 24580
  22.3 0.7 %copy-start.7 = (s32[6]{0:T(128)S(1)}, s32[6]{0:T(128)}, u32[]{:S(2)}) copy-start(s32[6]{0:T(128)} %codes.1) | copy-start | bytes 76
  28.5 11.7 %collective-permute-start.4 = (f32[16,40,128]{2,1,0:T(8,128)S(1)}, f32[16,40,128]{2,1,0:T(8,128)S(1)}, u32[]{:S(2)}, u32[]{:S(2)}) collective-permute-start(f32[16,40,128]{2,1,0:T(8,128)S(1)} %shard_map.98), channel_id=1, source_target_pairs={{1,2},{3,4},{5,6},{2,1},{4,3},{6,5},{9,10},{11,12},{13,14},{10,9},... | collective-permute-start | bytes 983048 | tf_op jit(solution)/shard_map/ppermute | solution.py:560
  30.2 9.9 %collective-permute-start.5 = (f32[16,40,128]{2,1,0:T(8,128)S(1)}, f32[16,40,128]{2,1,0:T(8,128)S(1)}, u32[]{:S(2)}, u32[]{:S(2)}) collective-permute-start(f32[16,40,128]{2,1,0:T(8,128)S(1)} %shard_map.99), channel_id=1, source_target_pairs={{0,1},{2,3},{4,5},{6,7},{1,0},{3,2},{5,4},{7,6},{8,9},{10,11},{12,... | collective-permute-start | bytes 983048 | tf_op jit(solution)/shard_map/ppermute | solution.py:560

commit v5 on v4

--- a/solution.py
+++ b/solution.py
@@ -44,7 +44,20 @@
     held[0](held[1])
 
 
-def pack_y(adj, eddy, diag, metric, own, to_right, to_left, packed):
+class Either:
+    def __init__(self, condition, first, second):
+        self.condition, self.first, self.second = condition, first, second
+
+    def __getitem__(self, at):
+        return jnp.where(self.condition, self.first[at], self.second[at])
+
+
+def two_sides(even, from_a, from_b):
+    return Either(even, from_b, from_a), Either(even, from_a, from_b)
+
+
+def pack_y(adj, eddy, diag, metric, own, msg_a, msg_b, packed):
+    even = lax.axis_index("gy") % 2 == 0
     shape = (4, 8, COLS)
     lane = iota(shape, 2)
     slot, j = lane // SLOT, lane % SLOT
@@ -90,8 +103,8 @@
             here = quad[0] == zq
             right = jnp.where(here, jnp.where(jj[0] == 0, r0, r1), right)
             left = jnp.where(here, jnp.where(jj[0] == 3, l0, l1), left)
-        to_right[zg, rows, :] = right
-        to_left[zg, rows, :] = left
+        msg_a[zg, rows, :] = jnp.where(even, right, left)
+        msg_b[zg, rows, :] = jnp.where(even, left, right)
 
     blocks = [(zg, t) for zg in range(2) for t in range(ROWS // 8)]
     for zg, t in blocks:
@@ -154,7 +167,9 @@
 HIGH_METRIC, LOW_METRIC = 26, 0
 
 
-def pack_x(own, from_left, from_right, adj, eddy, diag, metric, strip, to_low, to_high):
+def pack_x(info, own, from_a, from_b, adj, eddy, diag, metric, strip, msg_a, msg_b, to_low, to_high):
+    from_left, from_right = two_sides(info[1] % 2 == 0, from_a, from_b)
+    even = info[0] % 2 == 0
     j = iota((ROWS, COLS), 1) % SLOT
     for z in range(LEV):
         zg, at = z // 4, 4 * (z % 4)
@@ -170,6 +185,10 @@
             msg[z, at[EDDY] : at[EDDY] + 3, :] = eddy[z, a : a + 3, :]
             msg[z, at[RATE] : at[RATE] + 2, :] = relax_rate / diag[z, b : b + 2, :]
             msg[z, at[STRIP] : at[STRIP] + 3, :] = s[a : a + 3, :]
+    for z in range(LEV):
+        low, high = to_low[z], to_high[z]
+        msg_a[z] = jnp.where(even, high, low)
+        msg_b[z] = jnp.where(even, low, high)
 
 
 def lanes_of(v, plane):
@@ -312,7 +331,8 @@
     return jnp.where(iota((8, COLS), 0) < 4, above, below)
 
 
-def pack_z(far, info, table, strip, from_low, from_high, adj, eddy, diag, msg):
+def pack_z(far, info, table, strip, from_a, from_b, adj, eddy, diag, msg):
+    from_low, from_high = two_sides(info[0] % 2 == 0, from_a, from_b)
     edges = Edges(info, table)
     top = (info[2] % 2 == 0) != far
 
@@ -332,9 +352,10 @@
 
 
 def inner_levels(
-    info, table, adj, eddy, diag, strip, from_low, from_high, metric, src,
+    info, table, adj, eddy, diag, strip, from_a, from_b, metric, src,
     f0, near1, next2, f1, rates, edge_eddy, edge_rate, out, sums, halo, metric_row, a1, a2, ends, lateral,
 ):
+    from_low, from_high = two_sides(info[0] % 2 == 0, from_a, from_b)
     edges = Edges(info, table)
     row = iota((8, COLS), 0)
     for z in range(LEV):
@@ -550,10 +571,6 @@
     info = jnp.stack(index + [jnp.int32(c) for c in count]).astype(jnp.int32)
     cells, weights = sample_cells.reshape(16, 128), sample_weights.reshape(16, 128)
 
-    def shift(v, axis, step):
-        n = lax.axis_size(axis)
-        return lax.ppermute(v, axis, [(i, i + step) for i in range(n) if 0 <= i + step < n])
-
     def trade(v, axis, first):
         n = lax.axis_size(axis)
         pairs = [(i, i + 1) for i in range(first, n - 1, 2)]
@@ -563,23 +580,21 @@
         return pltpu.VMEM(shape, jnp.float32)
 
     level = (LEV, ROWS, COLS)
-    own, to_right, to_left = call(
+    own, msg_a, msg_b = call(
         pack_y,
         (f32(*level), f32(2, ROWS, COLS), f32(2, ROWS, COLS)),
         [VM] * 4,
         [buf(*level)],
     )(adjoint_start, eddy_visc, diag_coef, metric_terms[2:3])
-    from_left = shift(to_right, "gy", 1)
-    from_right = shift(to_left, "gy", -1)
-    strip, to_low, to_high = call(pack_x, (f32(*level),) * 3, [VM] * 7)(
-        own, from_left, from_right, adjoint_start, eddy_visc, diag_coef, metric_terms
+    beside = trade(msg_a, "gy", 0), trade(msg_b, "gy", 1)
+    strip, msg_a, msg_b = call(pack_x, (f32(*level),) * 3, [SM] + [VM] * 7, [buf(*level)] * 2)(
+        info, own, *beside, adjoint_start, eddy_visc, diag_coef, metric_terms
     )
-    from_low = shift(to_high, "gx", 1)
-    from_high = shift(to_low, "gx", -1)
+    beside = trade(msg_a, "gx", 0), trade(msg_b, "gx", 1)
     src, table = call(
         functools.partial(make_source, COLS * count[1]), (f32(2, EXT, COLS), f32(56, COLS)), [SM] * 3 + [VM] * 3
     )(info, face_codes, coupling, cells, weights, strip)
-    received = (from_low, from_high, adjoint_start, eddy_visc, diag_coef)
+    received = (*beside, adjoint_start, eddy_visc, diag_coef)
     msg_b, msg_a = [
         call(functools.partial(pack_z, far), f32(16, EXT, COLS), [SM] + [VM] * 7)(info, table, strip, *received)
         for far in (True, False)
@@ -604,7 +619,7 @@
         ),
         [SM] + [VM] * 9,
         [buf(LEV, 7, *ext), buf(LEV, 7, *ext), buf(LEV, *ext), buf(LEV, *ext)],
-    )(info, table, adjoint_start, eddy_visc, diag_coef, strip, from_low, from_high, metric_terms, src)
+    )(info, table, adjoint_start, eddy_visc, diag_coef, strip, *beside, metric_terms, src)
     adjoint, share = call(
         outer_levels,
         (f32(FIELDS, *level), f32(count[2], COLS // count[2], COLS)),

time: 60.8 us -> 59.7 us (0.982)
  the two profiles are of different devices: /device:TPU:192 before, /device:TPU:196 now
where the time goes in v5:
time: 59.7 us; the launch traced here: 59.3 us
  starting transfers between devices  21.3 us (36%)
  blocking collectives  17.8 us (30%)
  Pallas kernels  12 us (20%)
  waiting for transfers between devices  5.87 us (10%)
  local copies, waits for them, and re-layouts  1.56 us (3%)
  between operations  0.83 us (1%)
    ppermute x6, starting transfers between devices, trade(): return lax.ppermute(v, axis, pairs + [(b, a) for a, b in pairs])  21.3 us
    all_to_all x1, blocking collectives, local(): parts = lax.all_to_all(share, 'gz', 0, 0, tiled=True)  17.8 us
    ppermute x6, waiting for transfers between devices, trade(): return lax.ppermute(v, axis, pairs + [(b, a) for a, b in pairs])  5.87 us
    pallas_call x1, Pallas kernels, local(): call(inner_levels, (f32(LEV, 7, *ext), f32(2, 7, *ext), f32(2, 7, *ext),...  4.06 us
    pallas_call x1, Pallas kernels, local(): call(outer_levels, (f32(FIELDS, *level), f32(count[2], COLS // count[2],...  2.6 us
    slice x1, local copies, waits for them, and re-layouts, local(): metric_terms[2:3]  1.36 us
    pallas_call x2, Pallas kernels, local(): call(functools.partial(pack_z, far), f32(16, EXT, COLS), [SM] + [VM] * 7)  1.33 us
    pallas_call x1, Pallas kernels, local(): call(pack_y, (f32(*level), f32(2, ROWS, COLS), f32(2, ROWS, COLS)), [VM]...  1.29 us
  transfers between devices with their start and end apart: 6, of which 3 were waited for; matrix products, arithmetic and copies ran while one was open for 0% of the time, Pallas kernels for 10%

profile of v5, /device:TPU:196, one launch (start us, length us, event | category | flops | bytes accessed | tf_op | source)
XLA Modules:
  0.0 59.3 jit_solution(17239926014862820393)
XLA Ops:
  0.7 1.4 %slice.3.metric = f32[1,6,8,32,128]{4,3,2,1,0:T(8,128)S(1)} slice(f32[3,6,8,32,128]{4,3,2,1,0:T(8,128)} %metric.5), slice={[2:3], [0:6], [0:8], [0:32], [0:128]} | slice | bytes 1572864 | tf_op jit(solution)/shard_map/slice | solution.py:588
  2.1 0.1 copy-done.1
  2.1 1.3 %shard_map.95 = (f32[8,32,128]{2,1,0:T(8,128)S(1)}, f32[2,32,128]{2,1,0:T(8,128)}, f32[2,32,128]{2,1,0:T(8,128)}) custom-call(f32[6,8,32,128]{3,2,1,0:T(8,128)S(1)} %copy-done.1, f32[8,32,128]{2,1,0:T(8,128)S(1)} %copy-done.2, f32[8,32,128]{2,1,0:T(8,128)S(1)} %copy-done.3, f32[1,6,8,32,128]{4,3,2,1,0:T(8,128)S(1)} %slice.3.metric), custom_call_target="tpu_custom_call" | custom-call | flops 1000000 | bytes 1048576 | tf_op jit(solution)/shard_map/pallas_call | solution.py:583
  3.4 1.9 %collective-permute-start = (f32[2,32,128]{2,1,0:T(8,128)}, f32[2,32,128]{2,1,0:T(8,128)}, u32[]{:S(2)}, u32[]{:S(2)}) collective-permute-start(f32[2,32,128]{2,1,0:T(8,128)} %get-tuple-element.24), channel_id=1, source_target_pairs={{0,8},{16,24},{32,40},{48,56},{64,72},{80,88},{8,0},{24,16},{40,32... | collective-permute-start | bytes 98312 | tf_op jit(solution)/shard_map/ppermute | solution.py:577
  5.4 7.9 %collective-permute-start.1 = (f32[2,32,128]{2,1,0:T(8,128)}, f32[2,32,128]{2,1,0:T(8,128)}, u32[]{:S(2)}, u32[]{:S(2)}) collective-permute-start(f32[2,32,128]{2,1,0:T(8,128)} %get-tuple-element.25), channel_id=1, source_target_pairs={{8,16},{24,32},{40,48},{56,64},{72,80},{16,8},{32,24},{48,40},{64,... | collective-permute-start | bytes 98312 | tf_op jit(solution)/shard_map/ppermute | solution.py:577
  13.2 0.1 stack.15.info.idx
  13.3 0.0 collective-permute-done.from_a
  13.3 2.1 %collective-permute-done.1.from_b = f32[2,32,128]{2,1,0:T(8,128)} collective-permute-done((f32[2,32,128]{2,1,0:T(8,128)}, f32[2,32,128]{2,1,0:T(8,128)}, u32[]{:S(2)}, u32[]{:S(2)}) %collective-permute-start.1) | collective-permute-done | bytes 32800 | tf_op jit(solution)/shard_map/ppermute | solution.py:577
  15.4 0.0 copy-start.7
  15.4 1.0 %shard_map.96 = (f32[8,32,128]{2,1,0:T(8,128)S(1)}, f32[8,32,128]{2,1,0:T(8,128)S(1)}, f32[8,32,128]{2,1,0:T(8,128)S(1)}) custom-call(s32[6]{0:T(128)S(1)} %stack.15.info.idx, f32[8,32,128]{2,1,0:T(8,128)S(1)} %get-tuple-element.23.own, f32[2,32,128]{2,1,0:T(8,128)} %collective-permute-done.from_a, f32[2,32,128]{2,1,0:T(8,128)} %collective-permute-done.1.from_b, ...), custom_call_target="tpu_custom_call" | custom-call | flops 1000000 | bytes 1048576 | tf_op jit(solution)/shard_map/pallas_call | solution.py:590
  16.4 3.1 %collective-permute-start.2 = (f32[8,32,128]{2,1,0:T(8,128)S(1)}, f32[8,32,128]{2,1,0:T(8,128)S(1)}, u32[]{:S(2)}, u32[]{:S(2)}) collective-permute-start(f32[8,32,128]{2,1,0:T(8,128)S(1)} %get-tuple-element.28), channel_id=1, source_target_pairs={{0,96},{192,288},{384,480},{576,672},{96,0},{288,192},{480,384},{6... | collective-permute-start | bytes 393224 | tf_op jit(solution)/shard_map/ppermute | solution.py:577
  19.5 1.9 %collective-permute-start.3 = (f32[8,32,128]{2,1,0:T(8,128)S(1)}, f32[8,32,128]{2,1,0:T(8,128)S(1)}, u32[]{:S(2)}, u32[]{:S(2)}) collective-permute-start(f32[8,32,128]{2,1,0:T(8,128)S(1)} %get-tuple-element.29), channel_id=1, source_target_pairs={{96,192},{288,384},{480,576},{192,96},{384,288},{576,480},{97,193}... | collective-permute-start | bytes 393224 | tf_op jit(solution)/shard_map/ppermute | solution.py:577
  21.5 1.1 %shard_map.97 = (f32[2,40,128]{2,1,0:T(8,128)S(1)}, f32[56,128]{1,0:T(8,128)S(1)}) custom-call(s32[6]{0:T(128)S(1)} %stack.15.info.idx, s32[6]{0:T(128)S(1)} %copy-done.7, f32[6,6]{1,0:T(8,128)S(1)} %copy-done.6, s32[16,128]{1,0:T(8,128)S(1)} %bitcast.6, f32[16,128]{1,0:T(8,128)S(1)} %bitcast.7, f32[8,32,128]{2,1,0:T(8,128)S(1)} %get-tuple-element.26.after.strip), custom_call_target="tpu_custom_call" | custom-call | flops 1000000 | bytes 1048576 | tf_op jit(solution)/shard_map/pallas_call | solution.py:594
  22.6 0.7 %collective-permute-done.2.from_a = f32[8,32,128]{2,1,0:T(8,128)S(1)} collective-permute-done((f32[8,32,128]{2,1,0:T(8,128)S(1)}, f32[8,32,128]{2,1,0:T(8,128)S(1)}, u32[]{:S(2)}, u32[]{:S(2)}) %collective-permute-start.2) | collective-permute-done | bytes 131104 | tf_op jit(solution)/shard_map/ppermute | solution.py:577
  23.3 3.1 %collective-permute-done.3.from_b = f32[8,32,128]{2,1,0:T(8,128)S(1)} collective-permute-done((f32[8,32,128]{2,1,0:T(8,128)S(1)}, f32[8,32,128]{2,1,0:T(8,128)S(1)}, u32[]{:S(2)}, u32[]{:S(2)}) %collective-permute-start.3) | collective-permute-done | bytes 131104 | tf_op jit(solution)/shard_map/ppermute | solution.py:577
  26.4 0.7 %shard_map.98 = f32[16,40,128]{2,1,0:T(8,128)S(1)} custom-call(s32[6]{0:T(128)S(1)} %stack.15.info.idx, f32[56,128]{1,0:T(8,128)S(1)} %get-tuple-element.27.table, f32[8,32,128]{2,1,0:T(8,128)S(1)} %get-tuple-element.26.after.strip, f32[8,32,128]{2,1,0:T(8,128)S(1)} %collective-permute-done.2.from_a, f32[8,32,128]{2,1,0:T(8,128)S(1)} %collective-permute-done.3.from_b, ...), custom_call_target="tpu_custom_call" | custom-call | flops 1000000 | bytes 1048576 | tf_op jit(solution)/shard_map/pallas_call | solution.py:599
  27.1 0.7 %collective-permute-start.4 = (f32[16,40,128]{2,1,0:T(8,128)S(1)}, f32[16,40,128]{2,1,0:T(8,128)S(1)}, u32[]{:S(2)}, u32[]{:S(2)}) collective-permute-start(f32[16,40,128]{2,1,0:T(8,128)S(1)} %shard_map.98), channel_id=1, source_target_pairs={{1,2},{3,4},{5,6},{2,1},{4,3},{6,5},{9,10},{11,12},{13,14},{10,9},... | collective-permute-start | bytes 983048 | tf_op jit(solution)/shard_map/ppermute | solution.py:577
  27.7 0.7 %shard_map.99 = f32[16,40,128]{2,1,0:T(8,128)S(1)} custom-call(s32[6]{0:T(128)S(1)} %stack.15.info.idx, f32[56,128]{1,0:T(8,128)S(1)} %get-tuple-element.27.table, f32[8,32,128]{2,1,0:T(8,128)S(1)} %get-tuple-element.26.after.strip, f32[8,32,128]{2,1,0:T(8,128)S(1)} %collective-permute-done.2.from_a, f32[8,32,128]{2,1,0:T(8,128)S(1)} %collective-permute-done.3.from_b, ...), custom_call_target="tpu_custom_call" | custom-call | flops 1000000 | bytes 1048576 | tf_op jit(solution)/shard_map/pallas_call | solution.py:599
  28.4 5.8 %collective-permute-start.5 = (f32[16,40,128]{2,1,0:T(8,128)S(1)}, f32[16,40,128]{2,1,0:T(8,128)S(1)}, u32[]{:S(2)}, u32[]{:S(2)}) collective-permute-start(f32[16,40,128]{2,1,0:T(8,128)S(1)} %shard_map.99), channel_id=1, source_target_pairs={{0,1},{2,3},{4,5},{6,7},{1,0},{3,2},{5,4},{7,6},{8,9},{10,11},{12,... | collective-permute-start | bytes 983048 | tf_op jit(solution)/shard_map/ppermute | solution.py:577
  34.3 4.1 %shard_map.100 = (f32[8,7,40,128]{3,2,1,0:T(8,128)S(1)}, f32[2,7,40,128]{3,2,1,0:T(8,128)S(1)}, f32[2,7,40,128]{3,2,1,0:T(8,128)S(1)}, f32[8,7,40,128]{3,2,1,0:T...) custom-call(s32[6]{0:T(128)S(1)} %stack.15.info.idx, ...), custom_call_target="tpu_custom_call" | custom-call | flops 1000000 | bytes 1048576 | tf_op jit(solution)/shard_map/pallas_call | solution.py:605
  38.3 0.0 collective-permute-done.4.from_b
  38.3 2.6 %shard_map.101 = (f32[6,8,32,128]{3,2,1,0:T(8,128)}, f32[8,16,128]{2,1,0:T(8,128)S(1)}) custom-call(s32[6]{0:T(128)S(1)} %stack.15.info.idx, f32[56,128]{1,0:T(8,128)S(1)} %get-tuple-element.27.table, f32[8,32,128]{2,1,0:T(8,128)S(1)} %copy-done.2, f32[8,32,128]{2,1,0:T(8,128)S(1)} %get-tuple-element.26.after.strip, ...), custom_call_target="tpu_custom_call" | custom-call | flops 1000000 | bytes 1048576 | tf_op jit(solution)/shard_map/pallas_call | solution.py:623
  40.9 17.8 %all_to_all.5.parts = f32[8,16,128]{2,1,0:T(8,128)S(1)} all-to-all(f32[8,16,128]{2,1,0:T(8,128)S(1)} %get-tuple-element.43), channel_id=1, replica_groups=mesh['gx'=8,'gy'=12,'gz'=8] {'gz'}, dimensions={0} | all-to-all | bytes 131072 | tf_op jit(solution)/shard_map/all_to_all | solution.py:629
  58.7 0.6 %shard_map.102 = f32[16,32]{1,0:T(8,128)} custom-call(f32[8,16,128]{2,1,0:T(8,128)S(1)} %all_to_all.5.parts), custom_call_target="tpu_custom_call" | custom-call | flops 1000000 | bytes 1048576 | tf_op jit(solution)/shard_map/pallas_call | solution.py:630
  (15 shorter events, 0.0 us)
Async XLA Ops:
  0.6 1.4 %copy-start.2 = (f32[8,32,128]{2,1,0:T(8,128)S(1)}, f32[8,32,128]{2,1,0:T(8,128)}, u32[]{:S(2)}) copy-start(f32[8,32,128]{2,1,0:T(8,128)} %eddy.11) | copy-start | bytes 393220
  0.6 1.4 %copy-start.3 = (f32[8,32,128]{2,1,0:T(8,128)S(1)}, f32[8,32,128]{2,1,0:T(8,128)}, u32[]{:S(2)}) copy-start(f32[8,32,128]{2,1,0:T(8,128)} %diag.9) | copy-start | bytes 393220
  0.7 1.5 %copy-start.1 = (f32[6,8,32,128]{3,2,1,0:T(8,128)S(1)}, f32[6,8,32,128]{3,2,1,0:T(8,128)}, u32[]{:S(2)}) copy-start(f32[6,8,32,128]{3,2,1,0:T(8,128)} %adj.9) | copy-start | bytes 2359300
  0.7 14.8 %copy-start = (f32[3,6,8,32,128]{4,3,2,1,0:T(8,128)S(1)}, f32[3,6,8,32,128]{4,3,2,1,0:T(8,128)}, u32[]{:S(2)}) copy-start(f32[3,6,8,32,128]{4,3,2,1,0:T(8,128)} %metric.5) | copy-start | bytes 7077892
  3.4 9.9 %collective-permute-start = (f32[2,32,128]{2,1,0:T(8,128)}, f32[2,32,128]{2,1,0:T(8,128)}, u32[]{:S(2)}, u32[]{:S(2)}) collective-permute-start(f32[2,32,128]{2,1,0:T(8,128)} %get-tuple-element.24), channel_id=1, source_target_pairs={{0,8},{16,24},{32,40},{48,56},{64,72},{80,88},{8,0},{24,16},{40,32... | collective-permute-start | bytes 98312 | tf_op jit(solution)/shard_map/ppermute | solution.py:577
  5.4 10.1 %collective-permute-start.1 = (f32[2,32,128]{2,1,0:T(8,128)}, f32[2,32,128]{2,1,0:T(8,128)}, u32[]{:S(2)}, u32[]{:S(2)}) collective-permute-start(f32[2,32,128]{2,1,0:T(8,128)} %get-tuple-element.25), channel_id=1, source_target_pairs={{8,16},{24,32},{40,48},{56,64},{72,80},{16,8},{32,24},{48,40},{64,... | collective-permute-start | bytes 98312 | tf_op jit(solution)/shard_map/ppermute | solution.py:577
  15.4 6.1 %copy-start.4 = (s32[2048]{0:T(1024)S(1)}, s32[2048]{0:T(1024)}, u32[]{:S(2)}) copy-start(s32[2048]{0:T(1024)} %param.13) | copy-start | bytes 24580
  15.4 6.1 %copy-start.5 = (f32[2048]{0:T(1024)S(1)}, f32[2048]{0:T(1024)}, u32[]{:S(2)}) copy-start(f32[2048]{0:T(1024)} %param.14) | copy-start | bytes 24580
  15.4 6.1 %copy-start.6 = (f32[6,6]{1,0:T(8,128)S(1)}, f32[6,6]{1,0:T(8,128)}, u32[]{:S(2)}) copy-start(f32[6,6]{1,0:T(8,128)} %coup.1) | copy-start | bytes 436
  15.4 6.1 %copy-start.7 = (s32[6]{0:T(128)S(1)}, s32[6]{0:T(128)}, u32[]{:S(2)}) copy-start(s32[6]{0:T(128)} %codes.1) | copy-start | bytes 76
  16.4 6.9 %collective-permute-start.2 = (f32[8,32,128]{2,1,0:T(8,128)S(1)}, f32[8,32,128]{2,1,0:T(8,128)S(1)}, u32[]{:S(2)}, u32[]{:S(2)}) collective-permute-start(f32[8,32,128]{2,1,0:T(8,128)S(1)} %get-tuple-element.28), channel_id=1, source_target_pairs={{0,96},{192,288},{384,480},{576,672},{96,0},{288,192},{480,384},{6... | collective-permute-start | bytes 393224 | tf_op jit(solution)/shard_map/ppermute | solution.py:577
  19.5 6.9 %collective-permute-start.3 = (f32[8,32,128]{2,1,0:T(8,128)S(1)}, f32[8,32,128]{2,1,0:T(8,128)S(1)}, u32[]{:S(2)}, u32[]{:S(2)}) collective-permute-start(f32[8,32,128]{2,1,0:T(8,128)S(1)} %get-tuple-element.29), channel_id=1, source_target_pairs={{96,192},{288,384},{480,576},{192,96},{384,288},{576,480},{97,193}... | collective-permute-start | bytes 393224 | tf_op jit(solution)/shard_map/ppermute | solution.py:577
  27.1 11.2 %collective-permute-start.4 = (f32[16,40,128]{2,1,0:T(8,128)S(1)}, f32[16,40,128]{2,1,0:T(8,128)S(1)}, u32[]{:S(2)}, u32[]{:S(2)}) collective-permute-start(f32[16,40,128]{2,1,0:T(8,128)S(1)} %shard_map.98), channel_id=1, source_target_pairs={{1,2},{3,4},{5,6},{2,1},{4,3},{6,5},{9,10},{11,12},{13,14},{10,9},... | collective-permute-start | bytes 983048 | tf_op jit(solution)/shard_map/ppermute | solution.py:577
  28.4 9.9 %collective-permute-start.5 = (f32[16,40,128]{2,1,0:T(8,128)S(1)}, f32[16,40,128]{2,1,0:T(8,128)S(1)}, u32[]{:S(2)}, u32[]{:S(2)}) collective-permute-start(f32[16,40,128]{2,1,0:T(8,128)S(1)} %shard_map.99), channel_id=1, source_target_pairs={{0,1},{2,3},{4,5},{6,7},{1,0},{3,2},{5,4},{7,6},{8,9},{10,11},{12,... | collective-permute-start | bytes 983048 | tf_op jit(solution)/shard_map/ppermute | solution.py:577

commit v6 on v5

--- a/solution.py
+++ b/solution.py
@@ -44,6 +44,10 @@
     held[0](held[1])
 
 
+def place():
+    return [lax.axis_index(a) for a in ("gx", "gy", "gz")] + [lax.axis_size(a) for a in ("gx", "gy", "gz")]
+
+
 class Either:
     def __init__(self, condition, first, second):
         self.condition, self.first, self.second = condition, first, second
@@ -57,7 +61,7 @@
 
 
 def pack_y(adj, eddy, diag, metric, own, msg_a, msg_b, packed):
-    even = lax.axis_index("gy") % 2 == 0
+    even = place()[1] % 2 == 0
     shape = (4, 8, COLS)
     lane = iota(shape, 2)
     slot, j = lane // SLOT, lane % SLOT
@@ -116,7 +120,7 @@
 MIX, PAIR = 8, 16
 
 
-def make_source(total_y, idx, codes, coup, cells, weights, after, src, table):
+def make_source(codes, coup, cells, weights, after, src, table):
     slot = iota((1, COLS), 1) // SLOT
     for i in range(6):
         factor = jnp.where(codes[i] == 1, 1.0, jnp.where(codes[i] == 2, -1.0, 0.0)).astype(jnp.float32)
@@ -128,7 +132,8 @@
             at = PAIR + FIELDS * e + f
             table[at : at + 1, :] = jnp.full((1, COLS), coup[e, f])
         table[MIX + e : MIX + e + 1, :] = v
-    start_x, start_y = idx[0] * ROWS, idx[1] * COLS
+    info = place()
+    start_x, start_y, total_y = info[0] * ROWS, info[1] * COLS, info[4] * COLS
     r = iota((48, COLS), 0)
     row_x = jnp.where(r < EXT - 5, r, r - EXT) + start_x
     row_x = jnp.where(r < EXT, row_x, -1)
@@ -167,7 +172,8 @@
 HIGH_METRIC, LOW_METRIC = 26, 0
 
 
-def pack_x(info, own, from_a, from_b, adj, eddy, diag, metric, strip, msg_a, msg_b, to_low, to_high):
+def pack_x(own, from_a, from_b, adj, eddy, diag, metric, strip, msg_a, msg_b, to_low, to_high):
+    info = place()
     from_left, from_right = two_sides(info[1] % 2 == 0, from_a, from_b)
     even = info[0] % 2 == 0
     j = iota((ROWS, COLS), 1) % SLOT
@@ -305,8 +311,8 @@
 
 
 def level_sums(z, info, field, edge_strip, strip, metric, metric_row, sums, out, zo):
-    total_z = (info[5] * LEV).astype(jnp.float32)
-    w = 1.0 - 0.5 * (((info[2] * LEV + z).astype(jnp.float32) + 0.5) / total_z)
+    total_z = info[5] * LEV
+    w = 1.0 - 0.5 * ((jnp.int32(info[2] * LEV + z).astype(jnp.float32) + 0.5) / total_z)
     totals = None
     for f in range(FIELDS):
         a = field(f)
@@ -331,7 +337,8 @@
     return jnp.where(iota((8, COLS), 0) < 4, above, below)
 
 
-def pack_z(far, info, table, strip, from_a, from_b, adj, eddy, diag, msg):
+def pack_z(far, table, strip, from_a, from_b, adj, eddy, diag, msg):
+    info = place()
     from_low, from_high = two_sides(info[0] % 2 == 0, from_a, from_b)
     edges = Edges(info, table)
     top = (info[2] % 2 == 0) != far
@@ -352,9 +359,10 @@
 
 
 def inner_levels(
-    info, table, adj, eddy, diag, strip, from_a, from_b, metric, src,
+    table, adj, eddy, diag, strip, from_a, from_b, metric, src,
     f0, near1, next2, f1, rates, edge_eddy, edge_rate, out, sums, halo, metric_row, a1, a2, ends, lateral,
 ):
+    info = place()
     from_low, from_high = two_sides(info[0] % 2 == 0, from_a, from_b)
     edges = Edges(info, table)
     row = iota((8, COLS), 0)
@@ -445,10 +453,11 @@
 
 
 def outer_levels(
-    info, table, eddy, strip, from_b, from_a, metric, src,
+    table, eddy, strip, from_b, from_a, metric, src,
     f0, near1, next2, f1, rates, edge_eddy, edge_rate, inner_out, inner_sums, halo_rows, metric_row,
     out, share, sums, fh, gh, an, gn, a2, edge_over, ends, lateral,
 ):
+    info = place()
     edges = Edges(info, table)
     hub = info[5] * LEV // 4 - info[2] * LEV
     sums[...] = inner_sums[...]
@@ -566,9 +575,7 @@
 
 
 def local(adjoint_start, eddy_visc, diag_coef, coupling, metric_terms, sample_cells, sample_weights, face_codes):
-    index = [lax.axis_index(a) for a in ("gx", "gy", "gz")]
-    count = [lax.axis_size(a) for a in ("gx", "gy", "gz")]
-    info = jnp.stack(index + [jnp.int32(c) for c in count]).astype(jnp.int32)
+    slices = lax.axis_size("gz")
     cells, weights = sample_cells.reshape(16, 128), sample_weights.reshape(16, 128)
 
     def trade(v, axis, first):
@@ -587,16 +594,16 @@
         [buf(*level)],
     )(adjoint_start, eddy_visc, diag_coef, metric_terms[2:3])
     beside = trade(msg_a, "gy", 0), trade(msg_b, "gy", 1)
-    strip, msg_a, msg_b = call(pack_x, (f32(*level),) * 3, [SM] + [VM] * 7, [buf(*level)] * 2)(
-        info, own, *beside, adjoint_start, eddy_visc, diag_coef, metric_terms
+    strip, msg_a, msg_b = call(pack_x, (f32(*level),) * 3, [VM] * 7, [buf(*level)] * 2)(
+        own, *beside, adjoint_start, eddy_visc, diag_coef, metric_terms
     )
     beside = trade(msg_a, "gx", 0), trade(msg_b, "gx", 1)
     src, table = call(
-        functools.partial(make_source, COLS * count[1]), (f32(2, EXT, COLS), f32(56, COLS)), [SM] * 3 + [VM] * 3
-    )(info, face_codes, coupling, cells, weights, strip)
+        make_source, (f32(2, EXT, COLS), f32(56, COLS)), [SM] * 2 + [VM] * 3
+    )(face_codes, coupling, cells, weights, strip)
     received = (*beside, adjoint_start, eddy_visc, diag_coef)
     msg_b, msg_a = [
-        call(functools.partial(pack_z, far), f32(16, EXT, COLS), [SM] + [VM] * 7)(info, table, strip, *received)
+        call(functools.partial(pack_z, far), f32(16, EXT, COLS), [VM] * 7)(table, strip, *received)
         for far in (True, False)
     ]
     from_b = trade(msg_b, "gz", 1)
@@ -617,17 +624,17 @@
             f32(LEV, 9, 8, COLS),
             f32(FIELDS, LEV, 8, COLS),
         ),
-        [SM] + [VM] * 9,
+        [VM] * 9,
         [buf(LEV, 7, *ext), buf(LEV, 7, *ext), buf(LEV, *ext), buf(LEV, *ext)],
-    )(info, table, adjoint_start, eddy_visc, diag_coef, strip, *beside, metric_terms, src)
+    )(table, adjoint_start, eddy_visc, diag_coef, strip, *beside, metric_terms, src)
     adjoint, share = call(
         outer_levels,
-        (f32(FIELDS, *level), f32(count[2], COLS // count[2], COLS)),
-        [SM] + [VM] * 18,
+        (f32(FIELDS, *level), f32(slices, COLS // slices, COLS)),
+        [VM] * 18,
         [buf(4, *ext)] + [buf(2, 7, *ext)] * 5 + [buf(2, 2, *ext), buf(4, *ext), buf(4, *ext)],
-    )(info, table, eddy_visc, strip, from_b, from_a, metric_terms, src, *inner)
+    )(table, eddy_visc, strip, from_b, from_a, metric_terms, src, *inner)
     parts = lax.all_to_all(share, "gz", 0, 0, tiled=True)
-    height_grad = call(add_shares, f32(COLS // count[2], ROWS), [VM])(parts).T
+    height_grad = call(add_shares, f32(COLS // slices, ROWS), [VM])(parts).T
     return (adjoint, height_grad)
 
 

time: 59.7 us -> 58.6 us (0.982)
  the two profiles are of different devices: /device:TPU:196 before, /device:TPU:198 now
where the time goes in v6:
time: 58.6 us; the launch traced here: 58.3 us
  starting transfers between devices  23.1 us (39%)
  blocking collectives  19 us (32%)
  Pallas kernels  8.33 us (14%)
  waiting for transfers between devices  5.6 us (10%)
  local copies, waits for them, and re-layouts  1.48 us (3%)
  between operations  0.84 us (1%)
    ppermute x6, starting transfers between devices, trade(): return lax.ppermute(v, axis, pairs + [(b, a) for a, b in pairs])  23.1 us
    all_to_all x1, blocking collectives, local(): parts = lax.all_to_all(share, 'gz', 0, 0, tiled=True)  19 us
    ppermute x6, waiting for transfers between devices, trade(): return lax.ppermute(v, axis, pairs + [(b, a) for a, b in pairs])  5.6 us
    pallas_call x1, Pallas kernels, local(): call(inner_levels, (f32(LEV, 7, *ext), f32(2, 7, *ext), f32(2, 7, *ext),...  3.45 us
    pallas_call x1, Pallas kernels, local(): call(outer_levels, (f32(FIELDS, *level), f32(slices, COLS // slices, COLS...  2.06 us
    slice x1, local copies, waits for them, and re-layouts, local(): metric_terms[2:3]  1.36 us
  transfers between devices with their start and end apart: 6, of which 2 were waited for; matrix products, arithmetic and copies ran while one was open for 0% of the time, Pallas kernels for 8%

profile of v6, /device:TPU:198, one launch (start us, length us, event | category | flops | bytes accessed | tf_op | source)
XLA Modules:
  0.0 58.3 jit_solution(5915156826566645872)
XLA Ops:
  0.7 1.4 %slice.3.metric = f32[1,6,8,32,128]{4,3,2,1,0:T(8,128)S(1)} slice(f32[3,6,8,32,128]{4,3,2,1,0:T(8,128)} %metric.5), slice={[2:3], [0:6], [0:8], [0:32], [0:128]} | slice | bytes 1572864 | tf_op jit(solution)/shard_map/slice | solution.py:595
  2.1 0.1 copy-done.1
  2.1 0.7 %shard_map.95 = (f32[8,32,128]{2,1,0:T(8,128)S(1)}, f32[2,32,128]{2,1,0:T(8,128)S(1)}, f32[2,32,128]{2,1,0:T(8,128)S(1)}) custom-call(f32[6,8,32,128]{3,2,1,0:T(8,128)S(1)} %copy-done.1, f32[8,32,128]{2,1,0:T(8,128)S(1)} %copy-done.2, f32[8,32,128]{2,1,0:T(8,128)S(1)} %copy-done.3, f32[1,6,8,32,128]{4,3,2,1,0:T(8,128)S(1)} %slice.3.metric), custom_call_target="tpu_custom_call" | custom-call | flops 1000000 | bytes 1048576 | tf_op jit(solution)/shard_map/pallas_call | solution.py:590
  2.8 1.9 %collective-permute-start = (f32[2,32,128]{2,1,0:T(8,128)S(1)}, f32[2,32,128]{2,1,0:T(8,128)S(1)}, u32[]{:S(2)}, u32[]{:S(2)}) collective-permute-start(f32[2,32,128]{2,1,0:T(8,128)S(1)} %get-tuple-element.24), channel_id=1, source_target_pairs={{0,8},{16,24},{32,40},{48,56},{64,72},{80,88},{8,0},{24,16},{40,32... | collective-permute-start | bytes 98312 | tf_op jit(solution)/shard_map/ppermute | solution.py:584
  4.7 7.9 %collective-permute-start.1 = (f32[2,32,128]{2,1,0:T(8,128)S(1)}, f32[2,32,128]{2,1,0:T(8,128)S(1)}, u32[]{:S(2)}, u32[]{:S(2)}) collective-permute-start(f32[2,32,128]{2,1,0:T(8,128)S(1)} %get-tuple-element.25), channel_id=1, source_target_pairs={{8,16},{24,32},{40,48},{56,64},{72,80},{16,8},{32,24},{48,40},{64,... | collective-permute-start | bytes 98312 | tf_op jit(solution)/shard_map/ppermute | solution.py:584
  12.6 0.0 collective-permute-done.from_a
  12.6 1.9 %collective-permute-done.1.from_b = f32[2,32,128]{2,1,0:T(8,128)S(1)} collective-permute-done((f32[2,32,128]{2,1,0:T(8,128)S(1)}, f32[2,32,128]{2,1,0:T(8,128)S(1)}, u32[]{:S(2)}, u32[]{:S(2)}) %collective-permute-start.1) | collective-permute-done | bytes 32800 | tf_op jit(solution)/shard_map/ppermute | solution.py:584
  14.5 0.0 copy-start.7
  14.5 0.2 shard_map.96
  14.7 2.7 %collective-permute-start.2 = (f32[8,32,128]{2,1,0:T(8,128)S(1)}, f32[8,32,128]{2,1,0:T(8,128)S(1)}, u32[]{:S(2)}, u32[]{:S(2)}) collective-permute-start(f32[8,32,128]{2,1,0:T(8,128)S(1)} %get-tuple-element.28), channel_id=1, source_target_pairs={{0,96},{192,288},{384,480},{576,672},{96,0},{288,192},{480,384},{6... | collective-permute-start | bytes 393224 | tf_op jit(solution)/shard_map/ppermute | solution.py:584
  17.4 4.1 %collective-permute-start.3 = (f32[8,32,128]{2,1,0:T(8,128)S(1)}, f32[8,32,128]{2,1,0:T(8,128)S(1)}, u32[]{:S(2)}, u32[]{:S(2)}) collective-permute-start(f32[8,32,128]{2,1,0:T(8,128)S(1)} %get-tuple-element.29), channel_id=1, source_target_pairs={{96,192},{288,384},{480,576},{192,96},{384,288},{576,480},{97,193}... | collective-permute-start | bytes 393224 | tf_op jit(solution)/shard_map/ppermute | solution.py:584
  21.5 1.1 %shard_map.97 = (f32[2,40,128]{2,1,0:T(8,128)S(1)}, f32[56,128]{1,0:T(8,128)S(1)}) custom-call(s32[6]{0:T(128)S(1)} %copy-done.7, f32[6,6]{1,0:T(8,128)S(1)} %copy-done.6, s32[16,128]{1,0:T(8,128)S(1)} %bitcast.3, f32[16,128]{1,0:T(8,128)S(1)} %bitcast.4, f32[8,32,128]{2,1,0:T(8,128)S(1)} %get-tuple-element.26.after.strip), custom_call_target="tpu_custom_call" | custom-call | flops 1000000 | bytes 1048576 | tf_op jit(solution)/shard_map/pallas_call | solution.py:601
  22.7 0.0 collective-permute-done.2.from_a
  22.7 3.7 %collective-permute-done.3.from_b = f32[8,32,128]{2,1,0:T(8,128)S(1)} collective-permute-done((f32[8,32,128]{2,1,0:T(8,128)S(1)}, f32[8,32,128]{2,1,0:T(8,128)S(1)}, u32[]{:S(2)}, u32[]{:S(2)}) %collective-permute-start.3) | collective-permute-done | bytes 131104 | tf_op jit(solution)/shard_map/ppermute | solution.py:584
  26.4 0.1 shard_map.98
  26.5 0.7 %collective-permute-start.4 = (f32[16,40,128]{2,1,0:T(8,128)S(1)}, f32[16,40,128]{2,1,0:T(8,128)S(1)}, u32[]{:S(2)}, u32[]{:S(2)}) collective-permute-start(f32[16,40,128]{2,1,0:T(8,128)S(1)} %shard_map.98), channel_id=1, source_target_pairs={{1,2},{3,4},{5,6},{2,1},{4,3},{6,5},{9,10},{11,12},{13,14},{10,9},... | collective-permute-start | bytes 983048 | tf_op jit(solution)/shard_map/ppermute | solution.py:584
  27.2 0.1 shard_map.99
  27.3 5.8 %collective-permute-start.5 = (f32[16,40,128]{2,1,0:T(8,128)S(1)}, f32[16,40,128]{2,1,0:T(8,128)S(1)}, u32[]{:S(2)}, u32[]{:S(2)}) collective-permute-start(f32[16,40,128]{2,1,0:T(8,128)S(1)} %shard_map.99), channel_id=1, source_target_pairs={{0,1},{2,3},{4,5},{6,7},{1,0},{3,2},{5,4},{7,6},{8,9},{10,11},{12,... | collective-permute-start | bytes 983048 | tf_op jit(solution)/shard_map/ppermute | solution.py:584
  33.2 3.4 %shard_map.100 = (f32[8,7,40,128]{3,2,1,0:T(8,128)S(1)}, f32[2,7,40,128]{3,2,1,0:T(8,128)S(1)}, f32[2,7,40,128]{3,2,1,0:T(8,128)S(1)}, f32[8,7,40,128]{3,2,1,0:T...) custom-call(f32[56,128]{1,0:T(8,128)S(1)} %get-tuple-element.27.tabl, ...), custom_call_target="tpu_custom_call" | custom-call | flops 1000000 | bytes 1048576 | tf_op jit(solution)/shard_map/pallas_call | solution.py:612
  36.6 0.0 collective-permute-done.4.from_b
  36.6 0.0 collective-permute-done.5.from_a
  36.6 2.1 %shard_map.101 = (f32[6,8,32,128]{3,2,1,0:T(8,128)}, f32[8,16,128]{2,1,0:T(8,128)S(1)}) custom-call(f32[56,128]{1,0:T(8,128)S(1)} %get-tuple-element.27.table, f32[8,32,128]{2,1,0:T(8,128)S(1)} %copy-done.2, f32[8,32,128]{2,1,0:T(8,128)S(1)} %get-tuple-element.26.after.strip, f32[16,40,128]{2,1,0:T(8,128)S(1)} %collective-permute-done.4.from_b, ...), custom_call_target="tpu_custom_call" | custom-call | flops 1000000 | bytes 1048576 | tf_op jit(solution)/shard_map/pallas_call | solution.py:630
  38.7 19.0 %all_to_all.5.parts = f32[8,16,128]{2,1,0:T(8,128)S(1)} all-to-all(f32[8,16,128]{2,1,0:T(8,128)S(1)} %get-tuple-element.43), channel_id=1, replica_groups=mesh['gx'=8,'gy'=12,'gz'=8] {'gz'}, dimensions={0} | all-to-all | bytes 131072 | tf_op jit(solution)/shard_map/all_to_all | solution.py:636
  57.7 0.6 %shard_map.102 = f32[16,32]{1,0:T(8,128)} custom-call(f32[8,16,128]{2,1,0:T(8,128)S(1)} %all_to_all.5.parts), custom_call_target="tpu_custom_call" | custom-call | flops 1000000 | bytes 1048576 | tf_op jit(solution)/shard_map/pallas_call | solution.py:637
  (14 shorter events, 0.0 us)
Async XLA Ops:
  0.6 1.4 %copy-start.2 = (f32[8,32,128]{2,1,0:T(8,128)S(1)}, f32[8,32,128]{2,1,0:T(8,128)}, u32[]{:S(2)}) copy-start(f32[8,32,128]{2,1,0:T(8,128)} %eddy.11) | copy-start | bytes 393220
  0.6 1.4 %copy-start.3 = (f32[8,32,128]{2,1,0:T(8,128)S(1)}, f32[8,32,128]{2,1,0:T(8,128)}, u32[]{:S(2)}) copy-start(f32[8,32,128]{2,1,0:T(8,128)} %diag.9) | copy-start | bytes 393220
  0.7 1.5 %copy-start.1 = (f32[6,8,32,128]{3,2,1,0:T(8,128)S(1)}, f32[6,8,32,128]{3,2,1,0:T(8,128)}, u32[]{:S(2)}) copy-start(f32[6,8,32,128]{3,2,1,0:T(8,128)} %adj.9) | copy-start | bytes 2359300
  0.7 13.8 %copy-start = (f32[3,6,8,32,128]{4,3,2,1,0:T(8,128)S(1)}, f32[3,6,8,32,128]{4,3,2,1,0:T(8,128)}, u32[]{:S(2)}) copy-start(f32[3,6,8,32,128]{4,3,2,1,0:T(8,128)} %metric.5) | copy-start | bytes 7077892
  2.8 9.8 %collective-permute-start = (f32[2,32,128]{2,1,0:T(8,128)S(1)}, f32[2,32,128]{2,1,0:T(8,128)S(1)}, u32[]{:S(2)}, u32[]{:S(2)}) collective-permute-start(f32[2,32,128]{2,1,0:T(8,128)S(1)} %get-tuple-element.24), channel_id=1, source_target_pairs={{0,8},{16,24},{32,40},{48,56},{64,72},{80,88},{8,0},{24,16},{40,32... | collective-permute-start | bytes 98312 | tf_op jit(solution)/shard_map/ppermute | solution.py:584
  4.7 9.7 %collective-permute-start.1 = (f32[2,32,128]{2,1,0:T(8,128)S(1)}, f32[2,32,128]{2,1,0:T(8,128)S(1)}, u32[]{:S(2)}, u32[]{:S(2)}) collective-permute-start(f32[2,32,128]{2,1,0:T(8,128)S(1)} %get-tuple-element.25), channel_id=1, source_target_pairs={{8,16},{24,32},{40,48},{56,64},{72,80},{16,8},{32,24},{48,40},{64,... | collective-permute-start | bytes 98312 | tf_op jit(solution)/shard_map/ppermute | solution.py:584
  14.5 7.0 %copy-start.4 = (s32[2048]{0:T(1024)S(1)}, s32[2048]{0:T(1024)}, u32[]{:S(2)}) copy-start(s32[2048]{0:T(1024)} %param.13) | copy-start | bytes 24580
  14.5 7.0 %copy-start.5 = (f32[2048]{0:T(1024)S(1)}, f32[2048]{0:T(1024)}, u32[]{:S(2)}) copy-start(f32[2048]{0:T(1024)} %param.14) | copy-start | bytes 24580
  14.5 7.0 %copy-start.6 = (f32[6,6]{1,0:T(8,128)S(1)}, f32[6,6]{1,0:T(8,128)}, u32[]{:S(2)}) copy-start(f32[6,6]{1,0:T(8,128)} %coup.1) | copy-start | bytes 436
  14.5 7.0 %copy-start.7 = (s32[6]{0:T(128)S(1)}, s32[6]{0:T(128)}, u32[]{:S(2)}) copy-start(s32[6]{0:T(128)} %codes.1) | copy-start | bytes 76
  14.7 8.0 %collective-permute-start.2 = (f32[8,32,128]{2,1,0:T(8,128)S(1)}, f32[8,32,128]{2,1,0:T(8,128)S(1)}, u32[]{:S(2)}, u32[]{:S(2)}) collective-permute-start(f32[8,32,128]{2,1,0:T(8,128)S(1)} %get-tuple-element.28), channel_id=1, source_target_pairs={{0,96},{192,288},{384,480},{576,672},{96,0},{288,192},{480,384},{6... | collective-permute-start | bytes 393224 | tf_op jit(solution)/shard_map/ppermute | solution.py:584
  17.4 9.0 %collective-permute-start.3 = (f32[8,32,128]{2,1,0:T(8,128)S(1)}, f32[8,32,128]{2,1,0:T(8,128)S(1)}, u32[]{:S(2)}, u32[]{:S(2)}) collective-permute-start(f32[8,32,128]{2,1,0:T(8,128)S(1)} %get-tuple-element.29), channel_id=1, source_target_pairs={{96,192},{288,384},{480,576},{192,96},{384,288},{576,480},{97,193}... | collective-permute-start | bytes 393224 | tf_op jit(solution)/shard_map/ppermute | solution.py:584
  26.5 10.1 %collective-permute-start.4 = (f32[16,40,128]{2,1,0:T(8,128)S(1)}, f32[16,40,128]{2,1,0:T(8,128)S(1)}, u32[]{:S(2)}, u32[]{:S(2)}) collective-permute-start(f32[16,40,128]{2,1,0:T(8,128)S(1)} %shard_map.98), channel_id=1, source_target_pairs={{1,2},{3,4},{5,6},{2,1},{4,3},{6,5},{9,10},{11,12},{13,14},{10,9},... | collective-permute-start | bytes 983048 | tf_op jit(solution)/shard_map/ppermute | solution.py:584
  27.3 9.3 %collective-permute-start.5 = (f32[16,40,128]{2,1,0:T(8,128)S(1)}, f32[16,40,128]{2,1,0:T(8,128)S(1)}, u32[]{:S(2)}, u32[]{:S(2)}) collective-permute-start(f32[16,40,128]{2,1,0:T(8,128)S(1)} %shard_map.99), channel_id=1, source_target_pairs={{0,1},{2,3},{4,5},{6,7},{1,0},{3,2},{5,4},{7,6},{8,9},{10,11},{12,... | collective-permute-start | bytes 983048 | tf_op jit(solution)/shard_map/ppermute | solution.py:584

commit v7 on v6

--- a/solution.py
+++ b/solution.py
@@ -172,7 +172,7 @@
 HIGH_METRIC, LOW_METRIC = 26, 0
 
 
-def pack_x(own, from_a, from_b, adj, eddy, diag, metric, strip, msg_a, msg_b, to_low, to_high):
+def pack_x(own, from_b, from_a, adj, eddy, diag, metric, strip, msg_a, msg_b, to_low, to_high):
     info = place()
     from_left, from_right = two_sides(info[1] % 2 == 0, from_a, from_b)
     even = info[0] % 2 == 0
@@ -337,7 +337,7 @@
     return jnp.where(iota((8, COLS), 0) < 4, above, below)
 
 
-def pack_z(far, table, strip, from_a, from_b, adj, eddy, diag, msg):
+def pack_z(far, table, strip, from_b, from_a, adj, eddy, diag, msg):
     info = place()
     from_low, from_high = two_sides(info[0] % 2 == 0, from_a, from_b)
     edges = Edges(info, table)
@@ -359,7 +359,7 @@
 
 
 def inner_levels(
-    table, adj, eddy, diag, strip, from_a, from_b, metric, src,
+    table, adj, eddy, diag, strip, from_b, from_a, metric, src,
     f0, near1, next2, f1, rates, edge_eddy, edge_rate, out, sums, halo, metric_row, a1, a2, ends, lateral,
 ):
     info = place()
@@ -593,11 +593,11 @@
         [VM] * 4,
         [buf(*level)],
     )(adjoint_start, eddy_visc, diag_coef, metric_terms[2:3])
-    beside = trade(msg_a, "gy", 0), trade(msg_b, "gy", 1)
+    beside = trade(msg_b, "gy", 1), trade(msg_a, "gy", 0)
     strip, msg_a, msg_b = call(pack_x, (f32(*level),) * 3, [VM] * 7, [buf(*level)] * 2)(
         own, *beside, adjoint_start, eddy_visc, diag_coef, metric_terms
     )
-    beside = trade(msg_a, "gx", 0), trade(msg_b, "gx", 1)
+    beside = trade(msg_b, "gx", 1), trade(msg_a, "gx", 0)
     src, table = call(
         make_source, (f32(2, EXT, COLS), f32(56, COLS)), [SM] * 2 + [VM] * 3
     )(face_codes, coupling, cells, weights, strip)

time: 58.6 us -> 57.1 us (0.974)
  the two profiles are of different devices: /device:TPU:198 before, /device:TPU:130 now
where the time goes in v7:
time: 57.1 us; the launch traced here: 56.8 us
  starting transfers between devices  21.6 us (38%)
  blocking collectives  18.9 us (33%)
  Pallas kernels  8.33 us (15%)
  waiting for transfers between devices  5.64 us (10%)
  local copies, waits for them, and re-layouts  1.48 us (3%)
  between operations  0.84 us (1%)
    ppermute x6, starting transfers between devices, trade(): return lax.ppermute(v, axis, pairs + [(b, a) for a, b in pairs])  21.6 us
    all_to_all x1, blocking collectives, local(): parts = lax.all_to_all(share, 'gz', 0, 0, tiled=True)  18.9 us
    ppermute x6, waiting for transfers between devices, trade(): return lax.ppermute(v, axis, pairs + [(b, a) for a, b in pairs])  5.64 us
    pallas_call x1, Pallas kernels, local(): call(inner_levels, (f32(LEV, 7, *ext), f32(2, 7, *ext), f32(2, 7, *ext),...  3.45 us
    pallas_call x1, Pallas kernels, local(): call(outer_levels, (f32(FIELDS, *level), f32(slices, COLS // slices, COLS...  2.06 us
    slice x1, local copies, waits for them, and re-layouts, local(): metric_terms[2:3]  1.36 us
  transfers between devices with their start and end apart: 6, of which 3 were waited for; matrix products, arithmetic and copies ran while one was open for 0% of the time, Pallas kernels for 8%

profile of v7, /device:TPU:130, one launch (start us, length us, event | category | flops | bytes accessed | tf_op | source)
XLA Modules:
  0.0 56.8 jit_solution(13246993249442454622)
XLA Ops:
  0.7 1.4 %slice.3.metric = f32[1,6,8,32,128]{4,3,2,1,0:T(8,128)S(1)} slice(f32[3,6,8,32,128]{4,3,2,1,0:T(8,128)} %metric.5), slice={[2:3], [0:6], [0:8], [0:32], [0:128]} | slice | bytes 1572864 | tf_op jit(solution)/shard_map/slice | solution.py:595
  2.1 0.1 copy-done.1
  2.1 0.7 %shard_map.95 = (f32[8,32,128]{2,1,0:T(8,128)S(1)}, f32[2,32,128]{2,1,0:T(8,128)S(1)}, f32[2,32,128]{2,1,0:T(8,128)S(1)}) custom-call(f32[6,8,32,128]{3,2,1,0:T(8,128)S(1)} %copy-done.1, f32[8,32,128]{2,1,0:T(8,128)S(1)} %copy-done.2, f32[8,32,128]{2,1,0:T(8,128)S(1)} %copy-done.3, f32[1,6,8,32,128]{4,3,2,1,0:T(8,128)S(1)} %slice.3.metric), custom_call_target="tpu_custom_call" | custom-call | flops 1000000 | bytes 1048576 | tf_op jit(solution)/shard_map/pallas_call | solution.py:590
  2.8 1.9 %collective-permute-start = (f32[2,32,128]{2,1,0:T(8,128)S(1)}, f32[2,32,128]{2,1,0:T(8,128)S(1)}, u32[]{:S(2)}, u32[]{:S(2)}) collective-permute-start(f32[2,32,128]{2,1,0:T(8,128)S(1)} %get-tuple-element.24), channel_id=1, source_target_pairs={{8,16},{24,32},{40,48},{56,64},{72,80},{16,8},{32,24},{48,40},{64,... | collective-permute-start | bytes 98312 | tf_op jit(solution)/shard_map/ppermute | solution.py:584
  4.7 7.9 %collective-permute-start.1 = (f32[2,32,128]{2,1,0:T(8,128)S(1)}, f32[2,32,128]{2,1,0:T(8,128)S(1)}, u32[]{:S(2)}, u32[]{:S(2)}) collective-permute-start(f32[2,32,128]{2,1,0:T(8,128)S(1)} %get-tuple-element.25), channel_id=1, source_target_pairs={{0,8},{16,24},{32,40},{48,56},{64,72},{80,88},{8,0},{24,16},{40,32... | collective-permute-start | bytes 98312 | tf_op jit(solution)/shard_map/ppermute | solution.py:584
  12.6 0.0 collective-permute-done.from_b
  12.6 1.9 %collective-permute-done.1.from_a = f32[2,32,128]{2,1,0:T(8,128)S(1)} collective-permute-done((f32[2,32,128]{2,1,0:T(8,128)S(1)}, f32[2,32,128]{2,1,0:T(8,128)S(1)}, u32[]{:S(2)}, u32[]{:S(2)}) %collective-permute-start.1) | collective-permute-done | bytes 32800 | tf_op jit(solution)/shard_map/ppermute | solution.py:584
  14.5 0.0 copy-start.7
  14.5 0.2 shard_map.96
  14.7 3.4 %collective-permute-start.2 = (f32[8,32,128]{2,1,0:T(8,128)S(1)}, f32[8,32,128]{2,1,0:T(8,128)S(1)}, u32[]{:S(2)}, u32[]{:S(2)}) collective-permute-start(f32[8,32,128]{2,1,0:T(8,128)S(1)} %get-tuple-element.28), channel_id=1, source_target_pairs={{96,192},{288,384},{480,576},{192,96},{384,288},{576,480},{97,193}... | collective-permute-start | bytes 393224 | tf_op jit(solution)/shard_map/ppermute | solution.py:584
  18.1 1.9 %collective-permute-start.3 = (f32[8,32,128]{2,1,0:T(8,128)S(1)}, f32[8,32,128]{2,1,0:T(8,128)S(1)}, u32[]{:S(2)}, u32[]{:S(2)}) collective-permute-start(f32[8,32,128]{2,1,0:T(8,128)S(1)} %get-tuple-element.29), channel_id=1, source_target_pairs={{0,96},{192,288},{384,480},{576,672},{96,0},{288,192},{480,384},{6... | collective-permute-start | bytes 393224 | tf_op jit(solution)/shard_map/ppermute | solution.py:584
  20.1 1.1 %shard_map.97 = (f32[2,40,128]{2,1,0:T(8,128)S(1)}, f32[56,128]{1,0:T(8,128)S(1)}) custom-call(s32[6]{0:T(128)S(1)} %copy-done.7, f32[6,6]{1,0:T(8,128)S(1)} %copy-done.6, s32[16,128]{1,0:T(8,128)S(1)} %bitcast.3, f32[16,128]{1,0:T(8,128)S(1)} %bitcast.4, f32[8,32,128]{2,1,0:T(8,128)S(1)} %get-tuple-element.26.after.strip), custom_call_target="tpu_custom_call" | custom-call | flops 1000000 | bytes 1048576 | tf_op jit(solution)/shard_map/pallas_call | solution.py:601
  21.2 0.4 collective-permute-done.2.from_b
  21.6 3.4 %collective-permute-done.3.from_a = f32[8,32,128]{2,1,0:T(8,128)S(1)} collective-permute-done((f32[8,32,128]{2,1,0:T(8,128)S(1)}, f32[8,32,128]{2,1,0:T(8,128)S(1)}, u32[]{:S(2)}, u32[]{:S(2)}) %collective-permute-start.3) | collective-permute-done | bytes 131104 | tf_op jit(solution)/shard_map/ppermute | solution.py:584
  25.0 0.1 shard_map.98
  25.1 0.7 %collective-permute-start.4 = (f32[16,40,128]{2,1,0:T(8,128)S(1)}, f32[16,40,128]{2,1,0:T(8,128)S(1)}, u32[]{:S(2)}, u32[]{:S(2)}) collective-permute-start(f32[16,40,128]{2,1,0:T(8,128)S(1)} %shard_map.98), channel_id=1, source_target_pairs={{1,2},{3,4},{5,6},{2,1},{4,3},{6,5},{9,10},{11,12},{13,14},{10,9},... | collective-permute-start | bytes 983048 | tf_op jit(solution)/shard_map/ppermute | solution.py:584
  25.8 0.1 shard_map.99
  25.9 5.8 %collective-permute-start.5 = (f32[16,40,128]{2,1,0:T(8,128)S(1)}, f32[16,40,128]{2,1,0:T(8,128)S(1)}, u32[]{:S(2)}, u32[]{:S(2)}) collective-permute-start(f32[16,40,128]{2,1,0:T(8,128)S(1)} %shard_map.99), channel_id=1, source_target_pairs={{0,1},{2,3},{4,5},{6,7},{1,0},{3,2},{5,4},{7,6},{8,9},{10,11},{12,... | collective-permute-start | bytes 983048 | tf_op jit(solution)/shard_map/ppermute | solution.py:584
  31.7 3.4 %shard_map.100 = (f32[8,7,40,128]{3,2,1,0:T(8,128)S(1)}, f32[2,7,40,128]{3,2,1,0:T(8,128)S(1)}, f32[2,7,40,128]{3,2,1,0:T(8,128)S(1)}, f32[8,7,40,128]{3,2,1,0:T...) custom-call(f32[56,128]{1,0:T(8,128)S(1)} %get-tuple-element.27.tabl, ...), custom_call_target="tpu_custom_call" | custom-call | flops 1000000 | bytes 1048576 | tf_op jit(solution)/shard_map/pallas_call | solution.py:612
  35.2 0.0 collective-permute-done.4.from_b
  35.2 0.0 collective-permute-done.5.from_a
  35.2 2.1 %shard_map.101 = (f32[6,8,32,128]{3,2,1,0:T(8,128)}, f32[8,16,128]{2,1,0:T(8,128)S(1)}) custom-call(f32[56,128]{1,0:T(8,128)S(1)} %get-tuple-element.27.table, f32[8,32,128]{2,1,0:T(8,128)S(1)} %copy-done.2, f32[8,32,128]{2,1,0:T(8,128)S(1)} %get-tuple-element.26.after.strip, f32[16,40,128]{2,1,0:T(8,128)S(1)} %collective-permute-done.4.from_b, ...), custom_call_target="tpu_custom_call" | custom-call | flops 1000000 | bytes 1048576 | tf_op jit(solution)/shard_map/pallas_call | solution.py:630
  37.3 18.9 %all_to_all.5.parts = f32[8,16,128]{2,1,0:T(8,128)S(1)} all-to-all(f32[8,16,128]{2,1,0:T(8,128)S(1)} %get-tuple-element.43), channel_id=1, replica_groups=mesh['gx'=8,'gy'=12,'gz'=8] {'gz'}, dimensions={0} | all-to-all | bytes 131072 | tf_op jit(solution)/shard_map/all_to_all | solution.py:636
  56.2 0.6 %shard_map.102 = f32[16,32]{1,0:T(8,128)} custom-call(f32[8,16,128]{2,1,0:T(8,128)S(1)} %all_to_all.5.parts), custom_call_target="tpu_custom_call" | custom-call | flops 1000000 | bytes 1048576 | tf_op jit(solution)/shard_map/pallas_call | solution.py:637
  (14 shorter events, 0.0 us)
Async XLA Ops:
  0.6 1.4 %copy-start.2 = (f32[8,32,128]{2,1,0:T(8,128)S(1)}, f32[8,32,128]{2,1,0:T(8,128)}, u32[]{:S(2)}) copy-start(f32[8,32,128]{2,1,0:T(8,128)} %eddy.11) | copy-start | bytes 393220
  0.6 1.4 %copy-start.3 = (f32[8,32,128]{2,1,0:T(8,128)S(1)}, f32[8,32,128]{2,1,0:T(8,128)}, u32[]{:S(2)}) copy-start(f32[8,32,128]{2,1,0:T(8,128)} %diag.9) | copy-start | bytes 393220
  0.7 1.5 %copy-start.1 = (f32[6,8,32,128]{3,2,1,0:T(8,128)S(1)}, f32[6,8,32,128]{3,2,1,0:T(8,128)}, u32[]{:S(2)}) copy-start(f32[6,8,32,128]{3,2,1,0:T(8,128)} %adj.9) | copy-start | bytes 2359300
  0.7 13.8 %copy-start = (f32[3,6,8,32,128]{4,3,2,1,0:T(8,128)S(1)}, f32[3,6,8,32,128]{4,3,2,1,0:T(8,128)}, u32[]{:S(2)}) copy-start(f32[3,6,8,32,128]{4,3,2,1,0:T(8,128)} %metric.5) | copy-start | bytes 7077892
  2.8 9.8 %collective-permute-start = (f32[2,32,128]{2,1,0:T(8,128)S(1)}, f32[2,32,128]{2,1,0:T(8,128)S(1)}, u32[]{:S(2)}, u32[]{:S(2)}) collective-permute-start(f32[2,32,128]{2,1,0:T(8,128)S(1)} %get-tuple-element.24), channel_id=1, source_target_pairs={{8,16},{24,32},{40,48},{56,64},{72,80},{16,8},{32,24},{48,40},{64,... | collective-permute-start | bytes 98312 | tf_op jit(solution)/shard_map/ppermute | solution.py:584
  4.7 9.7 %collective-permute-start.1 = (f32[2,32,128]{2,1,0:T(8,128)S(1)}, f32[2,32,128]{2,1,0:T(8,128)S(1)}, u32[]{:S(2)}, u32[]{:S(2)}) collective-permute-start(f32[2,32,128]{2,1,0:T(8,128)S(1)} %get-tuple-element.25), channel_id=1, source_target_pairs={{0,8},{16,24},{32,40},{48,56},{64,72},{80,88},{8,0},{24,16},{40,32... | collective-permute-start | bytes 98312 | tf_op jit(solution)/shard_map/ppermute | solution.py:584
  14.5 5.5 %copy-start.4 = (s32[2048]{0:T(1024)S(1)}, s32[2048]{0:T(1024)}, u32[]{:S(2)}) copy-start(s32[2048]{0:T(1024)} %param.13) | copy-start | bytes 24580
  14.5 5.6 %copy-start.5 = (f32[2048]{0:T(1024)S(1)}, f32[2048]{0:T(1024)}, u32[]{:S(2)}) copy-start(f32[2048]{0:T(1024)} %param.14) | copy-start | bytes 24580
  14.5 5.6 %copy-start.6 = (f32[6,6]{1,0:T(8,128)S(1)}, f32[6,6]{1,0:T(8,128)}, u32[]{:S(2)}) copy-start(f32[6,6]{1,0:T(8,128)} %coup.1) | copy-start | bytes 436
  14.5 5.6 %copy-start.7 = (s32[6]{0:T(128)S(1)}, s32[6]{0:T(128)}, u32[]{:S(2)}) copy-start(s32[6]{0:T(128)} %codes.1) | copy-start | bytes 76
  14.7 6.9 %collective-permute-start.2 = (f32[8,32,128]{2,1,0:T(8,128)S(1)}, f32[8,32,128]{2,1,0:T(8,128)S(1)}, u32[]{:S(2)}, u32[]{:S(2)}) collective-permute-start(f32[8,32,128]{2,1,0:T(8,128)S(1)} %get-tuple-element.28), channel_id=1, source_target_pairs={{96,192},{288,384},{480,576},{192,96},{384,288},{576,480},{97,193}... | collective-permute-start | bytes 393224 | tf_op jit(solution)/shard_map/ppermute | solution.py:584
  18.1 6.9 %collective-permute-start.3 = (f32[8,32,128]{2,1,0:T(8,128)S(1)}, f32[8,32,128]{2,1,0:T(8,128)S(1)}, u32[]{:S(2)}, u32[]{:S(2)}) collective-permute-start(f32[8,32,128]{2,1,0:T(8,128)S(1)} %get-tuple-element.29), channel_id=1, source_target_pairs={{0,96},{192,288},{384,480},{576,672},{96,0},{288,192},{480,384},{6... | collective-permute-start | bytes 393224 | tf_op jit(solution)/shard_map/ppermute | solution.py:584
  25.1 10.1 %collective-permute-start.4 = (f32[16,40,128]{2,1,0:T(8,128)S(1)}, f32[16,40,128]{2,1,0:T(8,128)S(1)}, u32[]{:S(2)}, u32[]{:S(2)}) collective-permute-start(f32[16,40,128]{2,1,0:T(8,128)S(1)} %shard_map.98), channel_id=1, source_target_pairs={{1,2},{3,4},{5,6},{2,1},{4,3},{6,5},{9,10},{11,12},{13,14},{10,9},... | collective-permute-start | bytes 983048 | tf_op jit(solution)/shard_map/ppermute | solution.py:584
  25.9 9.3 %collective-permute-start.5 = (f32[16,40,128]{2,1,0:T(8,128)S(1)}, f32[16,40,128]{2,1,0:T(8,128)S(1)}, u32[]{:S(2)}, u32[]{:S(2)}) collective-permute-start(f32[16,40,128]{2,1,0:T(8,128)S(1)} %shard_map.99), channel_id=1, source_target_pairs={{0,1},{2,3},{4,5},{6,7},{1,0},{3,2},{5,4},{7,6},{8,9},{10,11},{12,... | collective-permute-start | bytes 983048 | tf_op jit(solution)/shard_map/ppermute | solution.py:584

commit v8 on v7

--- a/solution.py
+++ b/solution.py
@@ -330,6 +330,10 @@
     sums[3, :ROWS] += w * (m * edge_strip[:ROWS])
 
 
+TILES = 15 * 32
+MESSAGE = TILES + 7 * 8
+
+
 def halo_tile(from_low, from_high, z, p):
     at = 2 if p == RATE else 3
     start = LOW_AT[p] - (8 - at)
@@ -349,13 +353,46 @@
 
     near = jnp.where(top, LEV - 1, 0)
     next_ = jnp.where(top, LEV - 2, 1)
+    row, j = iota((8, COLS), 0), iota((EXT, COLS), 1) % SLOT
+    s = plane(next_, STRIP)
+    second = edges.flux(s * lanes_of(s, EDDY))
+    held = None
     for p in range(9):
-        msg[p] = plane(near, p)
+        v = plane(near, p)
+        if p == STRIP:
+            v = jnp.where(j == 0, roll(second, -3, 1), jnp.where(j == 15, roll(second, 3, 1), v))
+        msg[32 * p : 32 * p + 32, :] = v[:ROWS]
+        tile = v[ROWS:]
+        if p % 2 == 1:
+            moved = jnp.where(row < 4, roll(tile, 2, 0), roll(tile, -2, 0))
+            tile = jnp.where((row >= 2) & (row < 6), moved, held)
+        if p % 2 == 1 or p == 8:
+            at = TILES + 8 * (p // 2)
+            msg[at : at + 8, :] = tile
+        held = tile
     e = plane(next_, EDDY)
     for f in range(FIELDS):
-        msg[9 + f] = edges.flux(plane(next_, f) * e)
-    s = plane(next_, STRIP)
-    msg[15] = edges.flux(s * lanes_of(s, EDDY))
+        v = edges.flux(plane(next_, f) * e)
+        msg[32 * (9 + f) : 32 * (10 + f), :] = v[:ROWS]
+        tile, k = v[ROWS:], f % 4
+        if k > 0:
+            tile = jnp.where(row == k, roll(tile, k, 0), jnp.where(row == 7 - k, roll(tile, -k, 0), held))
+        if k == 3 or f == FIELDS - 1:
+            at = TILES + 8 * (5 + f // 4)
+            msg[at : at + 8, :] = tile
+        held = tile
+
+
+def unpack_z(msg, planes):
+    row, j = iota((8, COLS), 0), iota((EXT, COLS), 1) % SLOT
+    for p in range(15):
+        at, k = (TILES + 8 * (p // 2), 2 * (p % 2)) if p < 9 else (TILES + 8 * (5 + (p - 9) // 4), (p - 9) % 4)
+        tile = msg[at : at + 8, :]
+        if k > 0:
+            tile = jnp.where(row < 4, roll(tile, -k, 0), roll(tile, k, 0))
+        planes[p] = jnp.concatenate([msg[32 * p : 32 * p + 32, :], tile], 0)
+    s = planes[STRIP]
+    planes[15] = jnp.where(j == 3, roll(s, 3, 1), jnp.where(j == 12, roll(s, -3, 1), 0.0))
 
 
 def inner_levels(
@@ -455,7 +492,7 @@
 def outer_levels(
     table, eddy, strip, from_b, from_a, metric, src,
     f0, near1, next2, f1, rates, edge_eddy, edge_rate, inner_out, inner_sums, halo_rows, metric_row,
-    out, share, sums, fh, gh, an, gn, a2, edge_over, ends, lateral,
+    out, share, sums, halo_a, halo_b, fh, gh, an, gn, a2, edge_over, ends, lateral,
 ):
     info = place()
     edges = Edges(info, table)
@@ -476,7 +513,9 @@
         factor = jnp.where(top, edges.factors[5], edges.factors[4])
         return n, msg, jnp.where(top, 1, 0), near, next_, jnp.where(top, LEV, -1), ghost, factor
 
-    sides = [side(0, from_a), side(1, from_b)]
+    unpack_z(from_a, halo_a)
+    unpack_z(from_b, halo_b)
+    sides = [side(0, halo_a), side(1, halo_b)]
     for n, msg, *_ in sides:
         edge_over[n, 0] = lanes_of(msg[STRIP], EDDY)
         edge_over[n, 1] = lanes_of(msg[STRIP], RATE)
@@ -603,7 +642,7 @@
     )(face_codes, coupling, cells, weights, strip)
     received = (*beside, adjoint_start, eddy_visc, diag_coef)
     msg_b, msg_a = [
-        call(functools.partial(pack_z, far), f32(16, EXT, COLS), [VM] * 7)(table, strip, *received)
+        call(functools.partial(pack_z, far), f32(MESSAGE, COLS), [VM] * 7)(table, strip, *received)
         for far in (True, False)
     ]
     from_b = trade(msg_b, "gz", 1)
@@ -631,7 +670,7 @@
         outer_levels,
         (f32(FIELDS, *level), f32(slices, COLS // slices, COLS)),
         [VM] * 18,
-        [buf(4, *ext)] + [buf(2, 7, *ext)] * 5 + [buf(2, 2, *ext), buf(4, *ext), buf(4, *ext)],
+        [buf(4, *ext), buf(16, *ext), buf(16, *ext)] + [buf(2, 7, *ext)] * 5 + [buf(2, 2, *ext), buf(4, *ext), buf(4, *ext)],
     )(table, eddy_visc, strip, from_b, from_a, metric_terms, src, *inner)
     parts = lax.all_to_all(share, "gz", 0, 0, tiled=True)
     height_grad = call(add_shares, f32(COLS // slices, ROWS), [VM])(parts).T

time: 57.1 us -> 56 us (0.981)
  the two profiles are of different devices: /device:TPU:130 before, /device:TPU:128 now
where the time goes in v8:
time: 56 us; the launch traced here: 55.7 us
  starting transfers between devices  23.1 us (41%)
  blocking collectives  18.3 us (33%)
  Pallas kernels  8.42 us (15%)
  waiting for transfers between devices  3.63 us (6%)
  local copies, waits for them, and re-layouts  1.48 us (3%)
  between operations  0.84 us (2%)
    ppermute x6, starting transfers between devices, trade(): return lax.ppermute(v, axis, pairs + [(b, a) for a, b in pairs])  23.1 us
    all_to_all x1, blocking collectives, local(): parts = lax.all_to_all(share, 'gz', 0, 0, tiled=True)  18.3 us
    ppermute x6, waiting for transfers between devices, trade(): return lax.ppermute(v, axis, pairs + [(b, a) for a, b in pairs])  3.63 us
    pallas_call x1, Pallas kernels, local(): call(inner_levels, (f32(LEV, 7, *ext), f32(2, 7, *ext), f32(2, 7, *ext),...  3.41 us
    pallas_call x1, Pallas kernels, local(): call(outer_levels, (f32(FIELDS, *level), f32(slices, COLS // slices, COLS...  2.07 us
    slice x1, local copies, waits for them, and re-layouts, local(): metric_terms[2:3]  1.36 us
    pallas_call x1, Pallas kernels, local(): call(make_source, (f32(2, EXT, COLS), f32(56, COLS)), [SM] * 2 + [VM] * 3)  1.12 us
  transfers between devices with their start and end apart: 6, of which 2 were waited for; matrix products, arithmetic and copies ran while one was open for 0% of the time, Pallas kernels for 8%

profile of v8, /device:TPU:128, one launch (start us, length us, event | category | flops | bytes accessed | tf_op | source)
XLA Modules:
  0.0 55.7 jit_solution(11657870565338933457)
XLA Ops:
  0.7 1.4 %slice.3.metric = f32[1,6,8,32,128]{4,3,2,1,0:T(8,128)S(1)} slice(f32[3,6,8,32,128]{4,3,2,1,0:T(8,128)} %metric.5), slice={[2:3], [0:6], [0:8], [0:32], [0:128]} | slice | bytes 1572864 | tf_op jit(solution)/shard_map/slice | solution.py:634
  2.1 0.1 copy-done.1
  2.1 0.7 %shard_map.95 = (f32[8,32,128]{2,1,0:T(8,128)S(1)}, f32[2,32,128]{2,1,0:T(8,128)S(1)}, f32[2,32,128]{2,1,0:T(8,128)S(1)}) custom-call(f32[6,8,32,128]{3,2,1,0:T(8,128)S(1)} %copy-done.1, f32[8,32,128]{2,1,0:T(8,128)S(1)} %copy-done.2, f32[8,32,128]{2,1,0:T(8,128)S(1)} %copy-done.3, f32[1,6,8,32,128]{4,3,2,1,0:T(8,128)S(1)} %slice.3.metric), custom_call_target="tpu_custom_call" | custom-call | flops 1000000 | bytes 1048576 | tf_op jit(solution)/shard_map/pallas_call | solution.py:629
  2.8 1.9 %collective-permute-start = (f32[2,32,128]{2,1,0:T(8,128)S(1)}, f32[2,32,128]{2,1,0:T(8,128)S(1)}, u32[]{:S(2)}, u32[]{:S(2)}) collective-permute-start(f32[2,32,128]{2,1,0:T(8,128)S(1)} %get-tuple-element.24), channel_id=1, source_target_pairs={{8,16},{24,32},{40,48},{56,64},{72,80},{16,8},{32,24},{48,40},{64,... | collective-permute-start | bytes 98312 | tf_op jit(solution)/shard_map/ppermute | solution.py:623
  4.7 7.9 %collective-permute-start.1 = (f32[2,32,128]{2,1,0:T(8,128)S(1)}, f32[2,32,128]{2,1,0:T(8,128)S(1)}, u32[]{:S(2)}, u32[]{:S(2)}) collective-permute-start(f32[2,32,128]{2,1,0:T(8,128)S(1)} %get-tuple-element.25), channel_id=1, source_target_pairs={{0,8},{16,24},{32,40},{48,56},{64,72},{80,88},{8,0},{24,16},{40,32... | collective-permute-start | bytes 98312 | tf_op jit(solution)/shard_map/ppermute | solution.py:623
  12.6 0.0 collective-permute-done.from_b
  12.6 1.9 %collective-permute-done.1.from_a = f32[2,32,128]{2,1,0:T(8,128)S(1)} collective-permute-done((f32[2,32,128]{2,1,0:T(8,128)S(1)}, f32[2,32,128]{2,1,0:T(8,128)S(1)}, u32[]{:S(2)}, u32[]{:S(2)}) %collective-permute-start.1) | collective-permute-done | bytes 32800 | tf_op jit(solution)/shard_map/ppermute | solution.py:623
  14.5 0.0 copy-start.7
  14.5 0.2 shard_map.96
  14.7 0.7 %collective-permute-start.2 = (f32[8,32,128]{2,1,0:T(8,128)S(1)}, f32[8,32,128]{2,1,0:T(8,128)S(1)}, u32[]{:S(2)}, u32[]{:S(2)}) collective-permute-start(f32[8,32,128]{2,1,0:T(8,128)S(1)} %get-tuple-element.28), channel_id=1, source_target_pairs={{96,192},{288,384},{480,576},{192,96},{384,288},{576,480},{97,193}... | collective-permute-start | bytes 393224 | tf_op jit(solution)/shard_map/ppermute | solution.py:623
  15.4 6.1 %collective-permute-start.3 = (f32[8,32,128]{2,1,0:T(8,128)S(1)}, f32[8,32,128]{2,1,0:T(8,128)S(1)}, u32[]{:S(2)}, u32[]{:S(2)}) collective-permute-start(f32[8,32,128]{2,1,0:T(8,128)S(1)} %get-tuple-element.29), channel_id=1, source_target_pairs={{0,96},{192,288},{384,480},{576,672},{96,0},{288,192},{480,384},{6... | collective-permute-start | bytes 393224 | tf_op jit(solution)/shard_map/ppermute | solution.py:623
  21.5 1.1 %shard_map.97 = (f32[2,40,128]{2,1,0:T(8,128)S(1)}, f32[56,128]{1,0:T(8,128)S(1)}) custom-call(s32[6]{0:T(128)S(1)} %copy-done.7, f32[6,6]{1,0:T(8,128)S(1)} %copy-done.6, s32[16,128]{1,0:T(8,128)S(1)} %bitcast.3, f32[16,128]{1,0:T(8,128)S(1)} %bitcast.4, f32[8,32,128]{2,1,0:T(8,128)S(1)} %get-tuple-element.26.after.strip), custom_call_target="tpu_custom_call" | custom-call | flops 1000000 | bytes 1048576 | tf_op jit(solution)/shard_map/pallas_call | solution.py:640
  22.7 0.0 collective-permute-done.2.from_b
  22.7 1.7 %collective-permute-done.3.from_a = f32[8,32,128]{2,1,0:T(8,128)S(1)} collective-permute-done((f32[8,32,128]{2,1,0:T(8,128)S(1)}, f32[8,32,128]{2,1,0:T(8,128)S(1)}, u32[]{:S(2)}, u32[]{:S(2)}) %collective-permute-start.3) | collective-permute-done | bytes 131104 | tf_op jit(solution)/shard_map/ppermute | solution.py:623
  24.4 0.2 shard_map.98
  24.6 0.7 %collective-permute-start.4 = (f32[536,128]{1,0:T(8,128)S(1)}, f32[536,128]{1,0:T(8,128)S(1)}, u32[]{:S(2)}, u32[]{:S(2)}) collective-permute-start(f32[536,128]{1,0:T(8,128)S(1)} %shard_map.98), channel_id=1, source_target_pairs={{1,2},{3,4},{5,6},{2,1},{4,3},{6,5},{9,10},{11,12},{13,14},{10,9},... | collective-permute-start | bytes 823304 | tf_op jit(solution)/shard_map/ppermute | solution.py:623
  25.3 0.2 shard_map.99
  25.5 5.8 %collective-permute-start.5 = (f32[536,128]{1,0:T(8,128)S(1)}, f32[536,128]{1,0:T(8,128)S(1)}, u32[]{:S(2)}, u32[]{:S(2)}) collective-permute-start(f32[536,128]{1,0:T(8,128)S(1)} %shard_map.99), channel_id=1, source_target_pairs={{0,1},{2,3},{4,5},{6,7},{1,0},{3,2},{5,4},{7,6},{8,9},{10,11},{12,... | collective-permute-start | bytes 823304 | tf_op jit(solution)/shard_map/ppermute | solution.py:623
  31.3 3.4 %shard_map.100 = (f32[8,7,40,128]{3,2,1,0:T(8,128)S(1)}, f32[2,7,40,128]{3,2,1,0:T(8,128)S(1)}, f32[2,7,40,128]{3,2,1,0:T(8,128)S(1)}, f32[8,7,40,128]{3,2,1,0:T...) custom-call(f32[56,128]{1,0:T(8,128)S(1)} %get-tuple-element.27.tabl, ...), custom_call_target="tpu_custom_call" | custom-call | flops 1000000 | bytes 1048576 | tf_op jit(solution)/shard_map/pallas_call | solution.py:651
  34.8 0.0 collective-permute-done.4.from_b
  34.8 0.0 collective-permute-done.5.from_a
  34.8 2.1 %shard_map.101 = (f32[6,8,32,128]{3,2,1,0:T(8,128)}, f32[8,16,128]{2,1,0:T(8,128)S(1)}) custom-call(f32[56,128]{1,0:T(8,128)S(1)} %get-tuple-element.27.table, f32[8,32,128]{2,1,0:T(8,128)S(1)} %copy-done.2, f32[8,32,128]{2,1,0:T(8,128)S(1)} %get-tuple-element.26.after.strip, f32[536,128]{1,0:T(8,128)S(1)} %collective-permute-done.4.from_b, ...), custom_call_target="tpu_custom_call" | custom-call | flops 1000000 | bytes 1048576 | tf_op jit(solution)/shard_map/pallas_call | solution.py:669
  36.8 18.3 %all_to_all.5.parts = f32[8,16,128]{2,1,0:T(8,128)S(1)} all-to-all(f32[8,16,128]{2,1,0:T(8,128)S(1)} %get-tuple-element.43), channel_id=1, replica_groups=mesh['gx'=8,'gy'=12,'gz'=8] {'gz'}, dimensions={0} | all-to-all | bytes 131072 | tf_op jit(solution)/shard_map/all_to_all | solution.py:675
  55.1 0.6 %shard_map.102 = f32[16,32]{1,0:T(8,128)} custom-call(f32[8,16,128]{2,1,0:T(8,128)S(1)} %all_to_all.5.parts), custom_call_target="tpu_custom_call" | custom-call | flops 1000000 | bytes 1048576 | tf_op jit(solution)/shard_map/pallas_call | solution.py:676
  (14 shorter events, 0.0 us)
Async XLA Ops:
  0.6 1.4 %copy-start.2 = (f32[8,32,128]{2,1,0:T(8,128)S(1)}, f32[8,32,128]{2,1,0:T(8,128)}, u32[]{:S(2)}) copy-start(f32[8,32,128]{2,1,0:T(8,128)} %eddy.11) | copy-start | bytes 393220
  0.6 1.4 %copy-start.3 = (f32[8,32,128]{2,1,0:T(8,128)S(1)}, f32[8,32,128]{2,1,0:T(8,128)}, u32[]{:S(2)}) copy-start(f32[8,32,128]{2,1,0:T(8,128)} %diag.9) | copy-start | bytes 393220
  0.7 1.5 %copy-start.1 = (f32[6,8,32,128]{3,2,1,0:T(8,128)S(1)}, f32[6,8,32,128]{3,2,1,0:T(8,128)}, u32[]{:S(2)}) copy-start(f32[6,8,32,128]{3,2,1,0:T(8,128)} %adj.9) | copy-start | bytes 2359300
  0.7 13.8 %copy-start = (f32[3,6,8,32,128]{4,3,2,1,0:T(8,128)S(1)}, f32[3,6,8,32,128]{4,3,2,1,0:T(8,128)}, u32[]{:S(2)}) copy-start(f32[3,6,8,32,128]{4,3,2,1,0:T(8,128)} %metric.5) | copy-start | bytes 7077892
  2.8 9.8 %collective-permute-start = (f32[2,32,128]{2,1,0:T(8,128)S(1)}, f32[2,32,128]{2,1,0:T(8,128)S(1)}, u32[]{:S(2)}, u32[]{:S(2)}) collective-permute-start(f32[2,32,128]{2,1,0:T(8,128)S(1)} %get-tuple-element.24), channel_id=1, source_target_pairs={{8,16},{24,32},{40,48},{56,64},{72,80},{16,8},{32,24},{48,40},{64,... | collective-permute-start | bytes 98312 | tf_op jit(solution)/shard_map/ppermute | solution.py:623
  4.7 9.7 %collective-permute-start.1 = (f32[2,32,128]{2,1,0:T(8,128)S(1)}, f32[2,32,128]{2,1,0:T(8,128)S(1)}, u32[]{:S(2)}, u32[]{:S(2)}) collective-permute-start(f32[2,32,128]{2,1,0:T(8,128)S(1)} %get-tuple-element.25), channel_id=1, source_target_pairs={{0,8},{16,24},{32,40},{48,56},{64,72},{80,88},{8,0},{24,16},{40,32... | collective-permute-start | bytes 98312 | tf_op jit(solution)/shard_map/ppermute | solution.py:623
  14.5 7.0 %copy-start.4 = (s32[2048]{0:T(1024)S(1)}, s32[2048]{0:T(1024)}, u32[]{:S(2)}) copy-start(s32[2048]{0:T(1024)} %param.13) | copy-start | bytes 24580
  14.5 7.0 %copy-start.5 = (f32[2048]{0:T(1024)S(1)}, f32[2048]{0:T(1024)}, u32[]{:S(2)}) copy-start(f32[2048]{0:T(1024)} %param.14) | copy-start | bytes 24580
  14.5 7.0 %copy-start.6 = (f32[6,6]{1,0:T(8,128)S(1)}, f32[6,6]{1,0:T(8,128)}, u32[]{:S(2)}) copy-start(f32[6,6]{1,0:T(8,128)} %coup.1) | copy-start | bytes 436
  14.5 7.0 %copy-start.7 = (s32[6]{0:T(128)S(1)}, s32[6]{0:T(128)}, u32[]{:S(2)}) copy-start(s32[6]{0:T(128)} %codes.1) | copy-start | bytes 76
  14.7 8.0 %collective-permute-start.2 = (f32[8,32,128]{2,1,0:T(8,128)S(1)}, f32[8,32,128]{2,1,0:T(8,128)S(1)}, u32[]{:S(2)}, u32[]{:S(2)}) collective-permute-start(f32[8,32,128]{2,1,0:T(8,128)S(1)} %get-tuple-element.28), channel_id=1, source_target_pairs={{96,192},{288,384},{480,576},{192,96},{384,288},{576,480},{97,193}... | collective-permute-start | bytes 393224 | tf_op jit(solution)/shard_map/ppermute | solution.py:623
  15.4 9.1 %collective-permute-start.3 = (f32[8,32,128]{2,1,0:T(8,128)S(1)}, f32[8,32,128]{2,1,0:T(8,128)S(1)}, u32[]{:S(2)}, u32[]{:S(2)}) collective-permute-start(f32[8,32,128]{2,1,0:T(8,128)S(1)} %get-tuple-element.29), channel_id=1, source_target_pairs={{0,96},{192,288},{384,480},{576,672},{96,0},{288,192},{480,384},{6... | collective-permute-start | bytes 393224 | tf_op jit(solution)/shard_map/ppermute | solution.py:623
  24.6 10.1 %collective-permute-start.4 = (f32[536,128]{1,0:T(8,128)S(1)}, f32[536,128]{1,0:T(8,128)S(1)}, u32[]{:S(2)}, u32[]{:S(2)}) collective-permute-start(f32[536,128]{1,0:T(8,128)S(1)} %shard_map.98), channel_id=1, source_target_pairs={{1,2},{3,4},{5,6},{2,1},{4,3},{6,5},{9,10},{11,12},{13,14},{10,9},... | collective-permute-start | bytes 823304 | tf_op jit(solution)/shard_map/ppermute | solution.py:623
  25.5 9.3 %collective-permute-start.5 = (f32[536,128]{1,0:T(8,128)S(1)}, f32[536,128]{1,0:T(8,128)S(1)}, u32[]{:S(2)}, u32[]{:S(2)}) collective-permute-start(f32[536,128]{1,0:T(8,128)S(1)} %shard_map.99), channel_id=1, source_target_pairs={{0,1},{2,3},{4,5},{6,7},{1,0},{3,2},{5,4},{7,6},{8,9},{10,11},{12,... | collective-permute-start | bytes 823304 | tf_op jit(solution)/shard_map/ppermute | solution.py:623

commit v9 on v8

--- a/solution.py
+++ b/solution.py
@@ -172,7 +172,7 @@
 HIGH_METRIC, LOW_METRIC = 26, 0
 
 
-def pack_x(own, from_b, from_a, adj, eddy, diag, metric, strip, msg_a, msg_b, to_low, to_high):
+def pack_x(own, from_a, from_b, adj, eddy, diag, metric, strip, msg_a, msg_b, to_low, to_high):
     info = place()
     from_left, from_right = two_sides(info[1] % 2 == 0, from_a, from_b)
     even = info[0] % 2 == 0
@@ -632,7 +632,7 @@
         [VM] * 4,
         [buf(*level)],
     )(adjoint_start, eddy_visc, diag_coef, metric_terms[2:3])
-    beside = trade(msg_b, "gy", 1), trade(msg_a, "gy", 0)
+    beside = trade(msg_a, "gy", 0), trade(msg_b, "gy", 1)
     strip, msg_a, msg_b = call(pack_x, (f32(*level),) * 3, [VM] * 7, [buf(*level)] * 2)(
         own, *beside, adjoint_start, eddy_visc, diag_coef, metric_terms
     )

time: 56 us -> 56 us (level)
  the two profiles are of different devices: /device:TPU:128 before, /device:TPU:192 now
where the time goes in v9:
time: 56 us; the launch traced here: 55.7 us
  starting transfers between devices  23.1 us (41%)
  blocking collectives  18.3 us (33%)
  Pallas kernels  8.42 us (15%)
  waiting for transfers between devices  3.63 us (6%)
  local copies, waits for them, and re-layouts  1.48 us (3%)
  between operations  0.84 us (2%)
    ppermute x6, starting transfers between devices, trade(): return lax.ppermute(v, axis, pairs + [(b, a) for a, b in pairs])  23.1 us
    all_to_all x1, blocking collectives, local(): parts = lax.all_to_all(share, 'gz', 0, 0, tiled=True)  18.3 us
    ppermute x6, waiting for transfers between devices, trade(): return lax.ppermute(v, axis, pairs + [(b, a) for a, b in pairs])  3.63 us
    pallas_call x1, Pallas kernels, local(): call(inner_levels, (f32(LEV, 7, *ext), f32(2, 7, *ext), f32(2, 7, *ext),...  3.41 us
    pallas_call x1, Pallas kernels, local(): call(outer_levels, (f32(FIELDS, *level), f32(slices, COLS // slices, COLS...  2.07 us
    slice x1, local copies, waits for them, and re-layouts, local(): metric_terms[2:3]  1.36 us
    pallas_call x1, Pallas kernels, local(): call(make_source, (f32(2, EXT, COLS), f32(56, COLS)), [SM] * 2 + [VM] * 3)  1.13 us
  transfers between devices with their start and end apart: 6, of which 2 were waited for; matrix products, arithmetic and copies ran while one was open for 0% of the time, Pallas kernels for 8%

profile of v9, /device:TPU:192, one launch (start us, length us, event | category | flops | bytes accessed | tf_op | source)
XLA Modules:
  0.0 55.7 jit_solution(3961492450833349352)
XLA Ops:
  0.7 1.4 %slice.3.metric = f32[1,6,8,32,128]{4,3,2,1,0:T(8,128)S(1)} slice(f32[3,6,8,32,128]{4,3,2,1,0:T(8,128)} %metric.5), slice={[2:3], [0:6], [0:8], [0:32], [0:128]} | slice | bytes 1572864 | tf_op jit(solution)/shard_map/slice | solution.py:634
  2.1 0.1 copy-done.1
  2.1 0.7 %shard_map.95 = (f32[8,32,128]{2,1,0:T(8,128)S(1)}, f32[2,32,128]{2,1,0:T(8,128)S(1)}, f32[2,32,128]{2,1,0:T(8,128)S(1)}) custom-call(f32[6,8,32,128]{3,2,1,0:T(8,128)S(1)} %copy-done.1, f32[8,32,128]{2,1,0:T(8,128)S(1)} %copy-done.2, f32[8,32,128]{2,1,0:T(8,128)S(1)} %copy-done.3, f32[1,6,8,32,128]{4,3,2,1,0:T(8,128)S(1)} %slice.3.metric), custom_call_target="tpu_custom_call" | custom-call | flops 1000000 | bytes 1048576 | tf_op jit(solution)/shard_map/pallas_call | solution.py:629
  2.8 1.9 %collective-permute-start = (f32[2,32,128]{2,1,0:T(8,128)S(1)}, f32[2,32,128]{2,1,0:T(8,128)S(1)}, u32[]{:S(2)}, u32[]{:S(2)}) collective-permute-start(f32[2,32,128]{2,1,0:T(8,128)S(1)} %get-tuple-element.24), channel_id=1, source_target_pairs={{0,8},{16,24},{32,40},{48,56},{64,72},{80,88},{8,0},{24,16},{40,32... | collective-permute-start | bytes 98312 | tf_op jit(solution)/shard_map/ppermute | solution.py:623
  4.7 7.9 %collective-permute-start.1 = (f32[2,32,128]{2,1,0:T(8,128)S(1)}, f32[2,32,128]{2,1,0:T(8,128)S(1)}, u32[]{:S(2)}, u32[]{:S(2)}) collective-permute-start(f32[2,32,128]{2,1,0:T(8,128)S(1)} %get-tuple-element.25), channel_id=1, source_target_pairs={{8,16},{24,32},{40,48},{56,64},{72,80},{16,8},{32,24},{48,40},{64,... | collective-permute-start | bytes 98312 | tf_op jit(solution)/shard_map/ppermute | solution.py:623
  12.6 0.0 collective-permute-done.from_a
  12.6 1.9 %collective-permute-done.1.from_b = f32[2,32,128]{2,1,0:T(8,128)S(1)} collective-permute-done((f32[2,32,128]{2,1,0:T(8,128)S(1)}, f32[2,32,128]{2,1,0:T(8,128)S(1)}, u32[]{:S(2)}, u32[]{:S(2)}) %collective-permute-start.1) | collective-permute-done | bytes 32800 | tf_op jit(solution)/shard_map/ppermute | solution.py:623
  14.5 0.0 copy-start.7
  14.5 0.2 shard_map.96
  14.7 0.7 %collective-permute-start.2 = (f32[8,32,128]{2,1,0:T(8,128)S(1)}, f32[8,32,128]{2,1,0:T(8,128)S(1)}, u32[]{:S(2)}, u32[]{:S(2)}) collective-permute-start(f32[8,32,128]{2,1,0:T(8,128)S(1)} %get-tuple-element.28), channel_id=1, source_target_pairs={{96,192},{288,384},{480,576},{192,96},{384,288},{576,480},{97,193}... | collective-permute-start | bytes 393224 | tf_op jit(solution)/shard_map/ppermute | solution.py:623
  15.4 6.1 %collective-permute-start.3 = (f32[8,32,128]{2,1,0:T(8,128)S(1)}, f32[8,32,128]{2,1,0:T(8,128)S(1)}, u32[]{:S(2)}, u32[]{:S(2)}) collective-permute-start(f32[8,32,128]{2,1,0:T(8,128)S(1)} %get-tuple-element.29), channel_id=1, source_target_pairs={{0,96},{192,288},{384,480},{576,672},{96,0},{288,192},{480,384},{6... | collective-permute-start | bytes 393224 | tf_op jit(solution)/shard_map/ppermute | solution.py:623
  21.5 1.1 %shard_map.97 = (f32[2,40,128]{2,1,0:T(8,128)S(1)}, f32[56,128]{1,0:T(8,128)S(1)}) custom-call(s32[6]{0:T(128)S(1)} %copy-done.7, f32[6,6]{1,0:T(8,128)S(1)} %copy-done.6, s32[16,128]{1,0:T(8,128)S(1)} %bitcast.3, f32[16,128]{1,0:T(8,128)S(1)} %bitcast.4, f32[8,32,128]{2,1,0:T(8,128)S(1)} %get-tuple-element.26.after.strip), custom_call_target="tpu_custom_call" | custom-call | flops 1000000 | bytes 1048576 | tf_op jit(solution)/shard_map/pallas_call | solution.py:640
  22.7 0.0 collective-permute-done.2.from_b
  22.7 1.7 %collective-permute-done.3.from_a = f32[8,32,128]{2,1,0:T(8,128)S(1)} collective-permute-done((f32[8,32,128]{2,1,0:T(8,128)S(1)}, f32[8,32,128]{2,1,0:T(8,128)S(1)}, u32[]{:S(2)}, u32[]{:S(2)}) %collective-permute-start.3) | collective-permute-done | bytes 131104 | tf_op jit(solution)/shard_map/ppermute | solution.py:623
  24.4 0.2 shard_map.98
  24.6 0.7 %collective-permute-start.4 = (f32[536,128]{1,0:T(8,128)S(1)}, f32[536,128]{1,0:T(8,128)S(1)}, u32[]{:S(2)}, u32[]{:S(2)}) collective-permute-start(f32[536,128]{1,0:T(8,128)S(1)} %shard_map.98), channel_id=1, source_target_pairs={{1,2},{3,4},{5,6},{2,1},{4,3},{6,5},{9,10},{11,12},{13,14},{10,9},... | collective-permute-start | bytes 823304 | tf_op jit(solution)/shard_map/ppermute | solution.py:623
  25.3 0.2 shard_map.99
  25.5 5.8 %collective-permute-start.5 = (f32[536,128]{1,0:T(8,128)S(1)}, f32[536,128]{1,0:T(8,128)S(1)}, u32[]{:S(2)}, u32[]{:S(2)}) collective-permute-start(f32[536,128]{1,0:T(8,128)S(1)} %shard_map.99), channel_id=1, source_target_pairs={{0,1},{2,3},{4,5},{6,7},{1,0},{3,2},{5,4},{7,6},{8,9},{10,11},{12,... | collective-permute-start | bytes 823304 | tf_op jit(solution)/shard_map/ppermute | solution.py:623
  31.3 3.4 %shard_map.100 = (f32[8,7,40,128]{3,2,1,0:T(8,128)S(1)}, f32[2,7,40,128]{3,2,1,0:T(8,128)S(1)}, f32[2,7,40,128]{3,2,1,0:T(8,128)S(1)}, f32[8,7,40,128]{3,2,1,0:T...) custom-call(f32[56,128]{1,0:T(8,128)S(1)} %get-tuple-element.27.tabl, ...), custom_call_target="tpu_custom_call" | custom-call | flops 1000000 | bytes 1048576 | tf_op jit(solution)/shard_map/pallas_call | solution.py:651
  34.8 0.0 collective-permute-done.4.from_b
  34.8 0.0 collective-permute-done.5.from_a
  34.8 2.1 %shard_map.101 = (f32[6,8,32,128]{3,2,1,0:T(8,128)}, f32[8,16,128]{2,1,0:T(8,128)S(1)}) custom-call(f32[56,128]{1,0:T(8,128)S(1)} %get-tuple-element.27.table, f32[8,32,128]{2,1,0:T(8,128)S(1)} %copy-done.2, f32[8,32,128]{2,1,0:T(8,128)S(1)} %get-tuple-element.26.after.strip, f32[536,128]{1,0:T(8,128)S(1)} %collective-permute-done.4.from_b, ...), custom_call_target="tpu_custom_call" | custom-call | flops 1000000 | bytes 1048576 | tf_op jit(solution)/shard_map/pallas_call | solution.py:669
  36.8 18.3 %all_to_all.5.parts = f32[8,16,128]{2,1,0:T(8,128)S(1)} all-to-all(f32[8,16,128]{2,1,0:T(8,128)S(1)} %get-tuple-element.43), channel_id=1, replica_groups=mesh['gx'=8,'gy'=12,'gz'=8] {'gz'}, dimensions={0} | all-to-all | bytes 131072 | tf_op jit(solution)/shard_map/all_to_all | solution.py:675
  55.1 0.6 %shard_map.102 = f32[16,32]{1,0:T(8,128)} custom-call(f32[8,16,128]{2,1,0:T(8,128)S(1)} %all_to_all.5.parts), custom_call_target="tpu_custom_call" | custom-call | flops 1000000 | bytes 1048576 | tf_op jit(solution)/shard_map/pallas_call | solution.py:676
  (14 shorter events, 0.0 us)
Async XLA Ops:
  0.6 1.4 %copy-start.2 = (f32[8,32,128]{2,1,0:T(8,128)S(1)}, f32[8,32,128]{2,1,0:T(8,128)}, u32[]{:S(2)}) copy-start(f32[8,32,128]{2,1,0:T(8,128)} %eddy.11) | copy-start | bytes 393220
  0.6 1.4 %copy-start.3 = (f32[8,32,128]{2,1,0:T(8,128)S(1)}, f32[8,32,128]{2,1,0:T(8,128)}, u32[]{:S(2)}) copy-start(f32[8,32,128]{2,1,0:T(8,128)} %diag.9) | copy-start | bytes 393220
  0.7 1.5 %copy-start.1 = (f32[6,8,32,128]{3,2,1,0:T(8,128)S(1)}, f32[6,8,32,128]{3,2,1,0:T(8,128)}, u32[]{:S(2)}) copy-start(f32[6,8,32,128]{3,2,1,0:T(8,128)} %adj.9) | copy-start | bytes 2359300
  0.7 13.8 %copy-start = (f32[3,6,8,32,128]{4,3,2,1,0:T(8,128)S(1)}, f32[3,6,8,32,128]{4,3,2,1,0:T(8,128)}, u32[]{:S(2)}) copy-start(f32[3,6,8,32,128]{4,3,2,1,0:T(8,128)} %metric.5) | copy-start | bytes 7077892
  2.8 9.8 %collective-permute-start = (f32[2,32,128]{2,1,0:T(8,128)S(1)}, f32[2,32,128]{2,1,0:T(8,128)S(1)}, u32[]{:S(2)}, u32[]{:S(2)}) collective-permute-start(f32[2,32,128]{2,1,0:T(8,128)S(1)} %get-tuple-element.24), channel_id=1, source_target_pairs={{0,8},{16,24},{32,40},{48,56},{64,72},{80,88},{8,0},{24,16},{40,32... | collective-permute-start | bytes 98312 | tf_op jit(solution)/shard_map/ppermute | solution.py:623
  4.7 9.7 %collective-permute-start.1 = (f32[2,32,128]{2,1,0:T(8,128)S(1)}, f32[2,32,128]{2,1,0:T(8,128)S(1)}, u32[]{:S(2)}, u32[]{:S(2)}) collective-permute-start(f32[2,32,128]{2,1,0:T(8,128)S(1)} %get-tuple-element.25), channel_id=1, source_target_pairs={{8,16},{24,32},{40,48},{56,64},{72,80},{16,8},{32,24},{48,40},{64,... | collective-permute-start | bytes 98312 | tf_op jit(solution)/shard_map/ppermute | solution.py:623
  14.5 7.0 %copy-start.4 = (s32[2048]{0:T(1024)S(1)}, s32[2048]{0:T(1024)}, u32[]{:S(2)}) copy-start(s32[2048]{0:T(1024)} %param.13) | copy-start | bytes 24580
  14.5 7.0 %copy-start.5 = (f32[2048]{0:T(1024)S(1)}, f32[2048]{0:T(1024)}, u32[]{:S(2)}) copy-start(f32[2048]{0:T(1024)} %param.14) | copy-start | bytes 24580
  14.5 7.0 %copy-start.6 = (f32[6,6]{1,0:T(8,128)S(1)}, f32[6,6]{1,0:T(8,128)}, u32[]{:S(2)}) copy-start(f32[6,6]{1,0:T(8,128)} %coup.1) | copy-start | bytes 436
  14.5 7.0 %copy-start.7 = (s32[6]{0:T(128)S(1)}, s32[6]{0:T(128)}, u32[]{:S(2)}) copy-start(s32[6]{0:T(128)} %codes.1) | copy-start | bytes 76
  14.7 8.0 %collective-permute-start.2 = (f32[8,32,128]{2,1,0:T(8,128)S(1)}, f32[8,32,128]{2,1,0:T(8,128)S(1)}, u32[]{:S(2)}, u32[]{:S(2)}) collective-permute-start(f32[8,32,128]{2,1,0:T(8,128)S(1)} %get-tuple-element.28), channel_id=1, source_target_pairs={{96,192},{288,384},{480,576},{192,96},{384,288},{576,480},{97,193}... | collective-permute-start | bytes 393224 | tf_op jit(solution)/shard_map/ppermute | solution.py:623
  15.4 9.1 %collective-permute-start.3 = (f32[8,32,128]{2,1,0:T(8,128)S(1)}, f32[8,32,128]{2,1,0:T(8,128)S(1)}, u32[]{:S(2)}, u32[]{:S(2)}) collective-permute-start(f32[8,32,128]{2,1,0:T(8,128)S(1)} %get-tuple-element.29), channel_id=1, source_target_pairs={{0,96},{192,288},{384,480},{576,672},{96,0},{288,192},{480,384},{6... | collective-permute-start | bytes 393224 | tf_op jit(solution)/shard_map/ppermute | solution.py:623
  24.6 10.1 %collective-permute-start.4 = (f32[536,128]{1,0:T(8,128)S(1)}, f32[536,128]{1,0:T(8,128)S(1)}, u32[]{:S(2)}, u32[]{:S(2)}) collective-permute-start(f32[536,128]{1,0:T(8,128)S(1)} %shard_map.98), channel_id=1, source_target_pairs={{1,2},{3,4},{5,6},{2,1},{4,3},{6,5},{9,10},{11,12},{13,14},{10,9},... | collective-permute-start | bytes 823304 | tf_op jit(solution)/shard_map/ppermute | solution.py:623
  25.5 9.3 %collective-permute-start.5 = (f32[536,128]{1,0:T(8,128)S(1)}, f32[536,128]{1,0:T(8,128)S(1)}, u32[]{:S(2)}, u32[]{:S(2)}) collective-permute-start(f32[536,128]{1,0:T(8,128)S(1)} %shard_map.99), channel_id=1, source_target_pairs={{0,1},{2,3},{4,5},{6,7},{1,0},{3,2},{5,4},{7,6},{8,9},{10,11},{12,... | collective-permute-start | bytes 823304 | tf_op jit(solution)/shard_map/ppermute | solution.py:623

commit v10 on v8

--- a/solution.py
+++ b/solution.py
@@ -492,15 +492,20 @@
 def outer_levels(
     table, eddy, strip, from_b, from_a, metric, src,
     f0, near1, next2, f1, rates, edge_eddy, edge_rate, inner_out, inner_sums, halo_rows, metric_row,
-    out, share, sums, halo_a, halo_b, fh, gh, an, gn, a2, edge_over, ends, lateral,
+    out, share, levels, sems, sums, halo_a, halo_b, fh, gh, an, gn, a2, edge_over, ends, lateral,
 ):
     info = place()
     edges = Edges(info, table)
     hub = info[5] * LEV // 4 - info[2] * LEV
     sums[...] = inner_sums[...]
-    for f in range(FIELDS):
-        for z in range(2, LEV - 2):
-            out[f, z] = inner_out[f, z - 2]
+    copies = []
+
+    def leave(ref, at, z):
+        copies.append(pltpu.make_async_copy(ref, out.at[:, z], sems.at[at]))
+        copies[-1].start()
+
+    for z in range(2, LEV - 2):
+        leave(inner_out.at[:, z - 2], z - 2, z)
     even = info[2] % 2 == 0
 
     def flag_of(z):
@@ -573,10 +578,12 @@
         def after(p):
             return next2[i, p] + (edge_rate[next_] if p == FIELDS else rates[next_]) * gn[n, p]
 
-        level_sums(next_, info, after, after(FIELDS), strip, metric, metric_row, sums, out, next_)
+        level_sums(next_, info, after, after(FIELDS), strip, metric, metric_row, sums, levels, 2 * n)
+        leave(levels.at[:, 2 * n], 4 + 2 * n, next_)
     sweep([near_level(*s) for s in sides], table)
     for n, msg, i, near, *_ in sides:
-        level_sums(near, info, lambda f: a2[n, f], a2[n, FIELDS], strip, metric, metric_row, sums, out, near)
+        level_sums(near, info, lambda f: a2[n, f], a2[n, FIELDS], strip, metric, metric_row, sums, levels, 2 * n + 1)
+        leave(levels.at[:, 2 * n + 1], 5 + 2 * n, near)
 
     s1 = sums[1]
     stream = roll(s1, -1, 0)[:ROWS] - roll(s1, 1, 0)[:ROWS]
@@ -592,6 +599,8 @@
     turned = jnp.concatenate([total, jnp.zeros((COLS - ROWS, COLS), jnp.float32)], 0).T
     for k in range(share.shape[0]):
         share[k] = turned[share.shape[1] * k : share.shape[1] * (k + 1)]
+    for copy in copies:
+        copy.wait()
 
 
 def add_shares(parts, out):
@@ -601,12 +610,12 @@
     out[...] = total[:, :ROWS]
 
 
-def call(body, outs, ins, scratch=()):
+def call(body, outs, ins, scratch=(), places=None):
     return pl.pallas_call(
         body,
         out_shape=outs,
         in_specs=ins,
-        out_specs=jax.tree.map(lambda _: VM, outs),
+        out_specs=jax.tree.map(lambda _: VM, outs) if places is None else places,
         scratch_shapes=list(scratch),
         compiler_params=pltpu.CompilerParams(vmem_limit_bytes=16 << 20),
         cost_estimate=pl.CostEstimate(flops=1000000, bytes_accessed=1 << 20, transcendentals=0),
@@ -670,7 +679,8 @@
         outer_levels,
         (f32(FIELDS, *level), f32(slices, COLS // slices, COLS)),
         [VM] * 18,
-        [buf(4, *ext), buf(16, *ext), buf(16, *ext)] + [buf(2, 7, *ext)] * 5 + [buf(2, 2, *ext), buf(4, *ext), buf(4, *ext)],
+        [buf(FIELDS, 4, ROWS, COLS), pltpu.SemaphoreType.DMA((8,)), buf(4, *ext), buf(16, *ext), buf(16, *ext)] + [buf(2, 7, *ext)] * 5 + [buf(2, 2, *ext), buf(4, *ext), buf(4, *ext)],
+        (pl.BlockSpec(memory_space=pl.ANY), VM),
     )(table, eddy_visc, strip, from_b, from_a, metric_terms, src, *inner)
     parts = lax.all_to_all(share, "gz", 0, 0, tiled=True)
     height_grad = call(add_shares, f32(COLS // slices, ROWS), [VM])(parts).T

time: 56 us -> 55.9 us (level)
  transfers between devices with their start and end apart: 6 -> 6, of which waited for: 2 -> 2; matrix products, arithmetic and copies ran while one was open for 0% -> 0% of each run, Pallas kernels for 8% -> 9%
where the time goes in v10:
time: 55.9 us; the launch traced here: 55.6 us
  starting transfers between devices  23.1 us (41%)
  blocking collectives  18.3 us (33%)
  Pallas kernels  8.24 us (15%)
  waiting for transfers between devices  3.63 us (6%)
  local copies, waits for them, and re-layouts  1.48 us (3%)
  between operations  0.85 us (2%)
    ppermute x6, starting transfers between devices, trade(): return lax.ppermute(v, axis, pairs + [(b, a) for a, b in pairs])  23.1 us
    all_to_all x1, blocking collectives, local(): parts = lax.all_to_all(share, 'gz', 0, 0, tiled=True)  18.3 us
    ppermute x6, waiting for transfers between devices, trade(): return lax.ppermute(v, axis, pairs + [(b, a) for a, b in pairs])  3.63 us
    pallas_call x1, Pallas kernels, local(): call(inner_levels, (f32(LEV, 7, *ext), f32(2, 7, *ext), f32(2, 7, *ext),...  3.41 us
    pallas_call x1, Pallas kernels, local(): call(outer_levels, (f32(FIELDS, *level), f32(slices, COLS // slices, COLS...  1.88 us
    slice x1, local copies, waits for them, and re-layouts, local(): metric_terms[2:3]  1.36 us
    pallas_call x1, Pallas kernels, local(): call(make_source, (f32(2, EXT, COLS), f32(56, COLS)), [SM] * 2 + [VM] * 3)  1.12 us
  transfers between devices with their start and end apart: 6, of which 2 were waited for; matrix products, arithmetic and copies ran while one was open for 0% of the time, Pallas kernels for 9%

profile of v10, /device:TPU:128, one launch (start us, length us, event | category | flops | bytes accessed | tf_op | source)
XLA Modules:
  0.0 55.6 jit_solution(13851927088872064806)
XLA Ops:
  0.7 1.4 %slice.3.metric = f32[1,6,8,32,128]{4,3,2,1,0:T(8,128)S(1)} slice(f32[3,6,8,32,128]{4,3,2,1,0:T(8,128)} %metric.5), slice={[2:3], [0:6], [0:8], [0:32], [0:128]} | slice | bytes 1572864 | tf_op jit(solution)/shard_map/slice | solution.py:643
  2.1 0.1 copy-done.1
  2.1 0.7 %shard_map.95 = (f32[8,32,128]{2,1,0:T(8,128)S(1)}, f32[2,32,128]{2,1,0:T(8,128)S(1)}, f32[2,32,128]{2,1,0:T(8,128)S(1)}) custom-call(f32[6,8,32,128]{3,2,1,0:T(8,128)S(1)} %copy-done.1, f32[8,32,128]{2,1,0:T(8,128)S(1)} %copy-done.2, f32[8,32,128]{2,1,0:T(8,128)S(1)} %copy-done.3, f32[1,6,8,32,128]{4,3,2,1,0:T(8,128)S(1)} %slice.3.metric), custom_call_target="tpu_custom_call" | custom-call | flops 1000000 | bytes 1048576 | tf_op jit(solution)/shard_map/pallas_call | solution.py:638
  2.8 1.9 %collective-permute-start = (f32[2,32,128]{2,1,0:T(8,128)S(1)}, f32[2,32,128]{2,1,0:T(8,128)S(1)}, u32[]{:S(2)}, u32[]{:S(2)}) collective-permute-start(f32[2,32,128]{2,1,0:T(8,128)S(1)} %get-tuple-element.24), channel_id=1, source_target_pairs={{8,16},{24,32},{40,48},{56,64},{72,80},{16,8},{32,24},{48,40},{64,... | collective-permute-start | bytes 98312 | tf_op jit(solution)/shard_map/ppermute | solution.py:632
  4.7 7.9 %collective-permute-start.1 = (f32[2,32,128]{2,1,0:T(8,128)S(1)}, f32[2,32,128]{2,1,0:T(8,128)S(1)}, u32[]{:S(2)}, u32[]{:S(2)}) collective-permute-start(f32[2,32,128]{2,1,0:T(8,128)S(1)} %get-tuple-element.25), channel_id=1, source_target_pairs={{0,8},{16,24},{32,40},{48,56},{64,72},{80,88},{8,0},{24,16},{40,32... | collective-permute-start | bytes 98312 | tf_op jit(solution)/shard_map/ppermute | solution.py:632
  12.6 0.0 collective-permute-done.from_b
  12.6 1.9 %collective-permute-done.1.from_a = f32[2,32,128]{2,1,0:T(8,128)S(1)} collective-permute-done((f32[2,32,128]{2,1,0:T(8,128)S(1)}, f32[2,32,128]{2,1,0:T(8,128)S(1)}, u32[]{:S(2)}, u32[]{:S(2)}) %collective-permute-start.1) | collective-permute-done | bytes 32800 | tf_op jit(solution)/shard_map/ppermute | solution.py:632
  14.5 0.0 copy-start.7
  14.5 0.2 shard_map.96
  14.7 0.7 %collective-permute-start.2 = (f32[8,32,128]{2,1,0:T(8,128)S(1)}, f32[8,32,128]{2,1,0:T(8,128)S(1)}, u32[]{:S(2)}, u32[]{:S(2)}) collective-permute-start(f32[8,32,128]{2,1,0:T(8,128)S(1)} %get-tuple-element.28), channel_id=1, source_target_pairs={{96,192},{288,384},{480,576},{192,96},{384,288},{576,480},{97,193}... | collective-permute-start | bytes 393224 | tf_op jit(solution)/shard_map/ppermute | solution.py:632
  15.4 6.1 %collective-permute-start.3 = (f32[8,32,128]{2,1,0:T(8,128)S(1)}, f32[8,32,128]{2,1,0:T(8,128)S(1)}, u32[]{:S(2)}, u32[]{:S(2)}) collective-permute-start(f32[8,32,128]{2,1,0:T(8,128)S(1)} %get-tuple-element.29), channel_id=1, source_target_pairs={{0,96},{192,288},{384,480},{576,672},{96,0},{288,192},{480,384},{6... | collective-permute-start | bytes 393224 | tf_op jit(solution)/shard_map/ppermute | solution.py:632
  21.5 1.1 %shard_map.97 = (f32[2,40,128]{2,1,0:T(8,128)S(1)}, f32[56,128]{1,0:T(8,128)S(1)}) custom-call(s32[6]{0:T(128)S(1)} %copy-done.7, f32[6,6]{1,0:T(8,128)S(1)} %copy-done.6, s32[16,128]{1,0:T(8,128)S(1)} %bitcast.3, f32[16,128]{1,0:T(8,128)S(1)} %bitcast.4, f32[8,32,128]{2,1,0:T(8,128)S(1)} %get-tuple-element.26.after.strip), custom_call_target="tpu_custom_call" | custom-call | flops 1000000 | bytes 1048576 | tf_op jit(solution)/shard_map/pallas_call | solution.py:649
  22.7 0.0 collective-permute-done.2.from_b
  22.7 1.7 %collective-permute-done.3.from_a = f32[8,32,128]{2,1,0:T(8,128)S(1)} collective-permute-done((f32[8,32,128]{2,1,0:T(8,128)S(1)}, f32[8,32,128]{2,1,0:T(8,128)S(1)}, u32[]{:S(2)}, u32[]{:S(2)}) %collective-permute-start.3) | collective-permute-done | bytes 131104 | tf_op jit(solution)/shard_map/ppermute | solution.py:632
  24.4 0.2 shard_map.98
  24.6 0.7 %collective-permute-start.4 = (f32[536,128]{1,0:T(8,128)S(1)}, f32[536,128]{1,0:T(8,128)S(1)}, u32[]{:S(2)}, u32[]{:S(2)}) collective-permute-start(f32[536,128]{1,0:T(8,128)S(1)} %shard_map.98), channel_id=1, source_target_pairs={{1,2},{3,4},{5,6},{2,1},{4,3},{6,5},{9,10},{11,12},{13,14},{10,9},... | collective-permute-start | bytes 823304 | tf_op jit(solution)/shard_map/ppermute | solution.py:632
  25.3 0.2 shard_map.99
  25.5 5.8 %collective-permute-start.5 = (f32[536,128]{1,0:T(8,128)S(1)}, f32[536,128]{1,0:T(8,128)S(1)}, u32[]{:S(2)}, u32[]{:S(2)}) collective-permute-start(f32[536,128]{1,0:T(8,128)S(1)} %shard_map.99), channel_id=1, source_target_pairs={{0,1},{2,3},{4,5},{6,7},{1,0},{3,2},{5,4},{7,6},{8,9},{10,11},{12,... | collective-permute-start | bytes 823304 | tf_op jit(solution)/shard_map/ppermute | solution.py:632
  31.3 3.4 %shard_map.100 = (f32[8,7,40,128]{3,2,1,0:T(8,128)S(1)}, f32[2,7,40,128]{3,2,1,0:T(8,128)S(1)}, f32[2,7,40,128]{3,2,1,0:T(8,128)S(1)}, f32[8,7,40,128]{3,2,1,0:T...) custom-call(f32[56,128]{1,0:T(8,128)S(1)} %get-tuple-element.27.tabl, ...), custom_call_target="tpu_custom_call" | custom-call | flops 1000000 | bytes 1048576 | tf_op jit(solution)/shard_map/pallas_call | solution.py:660
  34.8 0.0 collective-permute-done.4.from_b
  34.8 0.0 collective-permute-done.5.from_a
  34.8 1.9 %shard_map.101 = (f32[6,8,32,128]{3,2,1,0:T(8,128)}, f32[8,16,128]{2,1,0:T(8,128)S(1)}) custom-call(f32[56,128]{1,0:T(8,128)S(1)} %get-tuple-element.27.table, f32[8,32,128]{2,1,0:T(8,128)S(1)} %copy-done.2, f32[8,32,128]{2,1,0:T(8,128)S(1)} %get-tuple-element.26.after.strip, f32[536,128]{1,0:T(8,128)S(1)} %collective-permute-done.4.from_b, ...), custom_call_target="tpu_custom_call" | custom-call | flops 1000000 | bytes 1048576 | tf_op jit(solution)/shard_map/pallas_call | solution.py:678
  36.7 18.3 %all_to_all.5.parts = f32[8,16,128]{2,1,0:T(8,128)S(1)} all-to-all(f32[8,16,128]{2,1,0:T(8,128)S(1)} %get-tuple-element.43), channel_id=1, replica_groups=mesh['gx'=8,'gy'=12,'gz'=8] {'gz'}, dimensions={0} | all-to-all | bytes 131072 | tf_op jit(solution)/shard_map/all_to_all | solution.py:685
  55.0 0.6 %shard_map.102 = f32[16,32]{1,0:T(8,128)} custom-call(f32[8,16,128]{2,1,0:T(8,128)S(1)} %all_to_all.5.parts), custom_call_target="tpu_custom_call" | custom-call | flops 1000000 | bytes 1048576 | tf_op jit(solution)/shard_map/pallas_call | solution.py:686
  (14 shorter events, 0.0 us)
Async XLA Ops:
  0.6 1.4 %copy-start.2 = (f32[8,32,128]{2,1,0:T(8,128)S(1)}, f32[8,32,128]{2,1,0:T(8,128)}, u32[]{:S(2)}) copy-start(f32[8,32,128]{2,1,0:T(8,128)} %eddy.11) | copy-start | bytes 393220
  0.6 1.4 %copy-start.3 = (f32[8,32,128]{2,1,0:T(8,128)S(1)}, f32[8,32,128]{2,1,0:T(8,128)}, u32[]{:S(2)}) copy-start(f32[8,32,128]{2,1,0:T(8,128)} %diag.9) | copy-start | bytes 393220
  0.7 1.5 %copy-start.1 = (f32[6,8,32,128]{3,2,1,0:T(8,128)S(1)}, f32[6,8,32,128]{3,2,1,0:T(8,128)}, u32[]{:S(2)}) copy-start(f32[6,8,32,128]{3,2,1,0:T(8,128)} %adj.9) | copy-start | bytes 2359300
  0.7 13.8 %copy-start = (f32[3,6,8,32,128]{4,3,2,1,0:T(8,128)S(1)}, f32[3,6,8,32,128]{4,3,2,1,0:T(8,128)}, u32[]{:S(2)}) copy-start(f32[3,6,8,32,128]{4,3,2,1,0:T(8,128)} %metric.5) | copy-start | bytes 7077892
  2.8 9.8 %collective-permute-start = (f32[2,32,128]{2,1,0:T(8,128)S(1)}, f32[2,32,128]{2,1,0:T(8,128)S(1)}, u32[]{:S(2)}, u32[]{:S(2)}) collective-permute-start(f32[2,32,128]{2,1,0:T(8,128)S(1)} %get-tuple-element.24), channel_id=1, source_target_pairs={{8,16},{24,32},{40,48},{56,64},{72,80},{16,8},{32,24},{48,40},{64,... | collective-permute-start | bytes 98312 | tf_op jit(solution)/shard_map/ppermute | solution.py:632
  4.7 9.7 %collective-permute-start.1 = (f32[2,32,128]{2,1,0:T(8,128)S(1)}, f32[2,32,128]{2,1,0:T(8,128)S(1)}, u32[]{:S(2)}, u32[]{:S(2)}) collective-permute-start(f32[2,32,128]{2,1,0:T(8,128)S(1)} %get-tuple-element.25), channel_id=1, source_target_pairs={{0,8},{16,24},{32,40},{48,56},{64,72},{80,88},{8,0},{24,16},{40,32... | collective-permute-start | bytes 98312 | tf_op jit(solution)/shard_map/ppermute | solution.py:632
  14.5 7.0 %copy-start.4 = (s32[2048]{0:T(1024)S(1)}, s32[2048]{0:T(1024)}, u32[]{:S(2)}) copy-start(s32[2048]{0:T(1024)} %param.13) | copy-start | bytes 24580
  14.5 7.0 %copy-start.5 = (f32[2048]{0:T(1024)S(1)}, f32[2048]{0:T(1024)}, u32[]{:S(2)}) copy-start(f32[2048]{0:T(1024)} %param.14) | copy-start | bytes 24580
  14.5 7.0 %copy-start.6 = (f32[6,6]{1,0:T(8,128)S(1)}, f32[6,6]{1,0:T(8,128)}, u32[]{:S(2)}) copy-start(f32[6,6]{1,0:T(8,128)} %coup.1) | copy-start | bytes 436
  14.5 7.0 %copy-start.7 = (s32[6]{0:T(128)S(1)}, s32[6]{0:T(128)}, u32[]{:S(2)}) copy-start(s32[6]{0:T(128)} %codes.1) | copy-start | bytes 76
  14.7 8.0 %collective-permute-start.2 = (f32[8,32,128]{2,1,0:T(8,128)S(1)}, f32[8,32,128]{2,1,0:T(8,128)S(1)}, u32[]{:S(2)}, u32[]{:S(2)}) collective-permute-start(f32[8,32,128]{2,1,0:T(8,128)S(1)} %get-tuple-element.28), channel_id=1, source_target_pairs={{96,192},{288,384},{480,576},{192,96},{384,288},{576,480},{97,193}... | collective-permute-start | bytes 393224 | tf_op jit(solution)/shard_map/ppermute | solution.py:632
  15.4 9.1 %collective-permute-start.3 = (f32[8,32,128]{2,1,0:T(8,128)S(1)}, f32[8,32,128]{2,1,0:T(8,128)S(1)}, u32[]{:S(2)}, u32[]{:S(2)}) collective-permute-start(f32[8,32,128]{2,1,0:T(8,128)S(1)} %get-tuple-element.29), channel_id=1, source_target_pairs={{0,96},{192,288},{384,480},{576,672},{96,0},{288,192},{480,384},{6... | collective-permute-start | bytes 393224 | tf_op jit(solution)/shard_map/ppermute | solution.py:632
  24.6 10.1 %collective-permute-start.4 = (f32[536,128]{1,0:T(8,128)S(1)}, f32[536,128]{1,0:T(8,128)S(1)}, u32[]{:S(2)}, u32[]{:S(2)}) collective-permute-start(f32[536,128]{1,0:T(8,128)S(1)} %shard_map.98), channel_id=1, source_target_pairs={{1,2},{3,4},{5,6},{2,1},{4,3},{6,5},{9,10},{11,12},{13,14},{10,9},... | collective-permute-start | bytes 823304 | tf_op jit(solution)/shard_map/ppermute | solution.py:632
  25.5 9.3 %collective-permute-start.5 = (f32[536,128]{1,0:T(8,128)S(1)}, f32[536,128]{1,0:T(8,128)S(1)}, u32[]{:S(2)}, u32[]{:S(2)}) collective-permute-start(f32[536,128]{1,0:T(8,128)S(1)} %shard_map.99), channel_id=1, source_target_pairs={{0,1},{2,3},{4,5},{6,7},{1,0},{3,2},{5,4},{7,6},{8,9},{10,11},{12,... | collective-permute-start | bytes 823304 | tf_op jit(solution)/shard_map/ppermute | solution.py:632
